TPU v7x, 32 devices: a whole 2x2x4 slice. The times are simulated.
32 devices in a mesh: ctx: 16 (over z, x, core), tp: 2 (over y).
Axes of the slice: x: 2, y: 2, z: 4, core: 2. Of those that a mesh axis runs over, the one named last changes fastest.
Arguments:
- stored: bfloat16 [2048, 4096], P('ctx', 'tp'), may hold values from -6 to 6
- source_owner: int32 [2048], P('ctx'), may hold values from 0 to 15, as said below
- doc_ids: int32 [2048], P('ctx'), may hold values from 0 to 12, as said below
- doc_starts: int32 [13], replicated, may hold values from 0 to 2040, as said below
- wq: bfloat16 [4096, 4096], P('ctx', 'tp'), may hold values from -1 to 1
- wk: bfloat16 [4096, 1024], P('ctx', 'tp'), may hold values from -1 to 1
- wv: bfloat16 [4096, 1024], P('ctx', 'tp'), may hold values from -0.09375 to 0.09375
Outputs:
- context: bfloat16 [2048, 4096], P('ctx', 'tp')
Inputs may be any that keep to these rules, and one draw needn't show every extreme that they name: `source_owner`: every owner stores exactly 128 rows, taken in packed order; each packed shard of 128 rows takes at most 16 rows from any one owner, and exactly 16 from some owner. `doc_ids`: Nondecreasing; document k occupies positions doc_starts[k] up to the next document's start; one document has exactly 1280 tokens. Increasing, doc_starts[0] = 0, consistent with doc_ids.
All inputs are finite; a program needn't handle non-finite values.
Results may differ from a plain program's by a relative error of at most 0.0035.
The roundings to bfloat16 on the way count: a program that leaves them out, or rounds other values in their place, can miss the bound.
Values may be sent and summed in bfloat16 or wider, within the bound.
No kernel may reach another device: no remote copies, remote signals or barrier semaphores. Data moves between devices by JAX's collectives and lax.ppermute only.
A program may use at most 64 MiB of HBM per device.

v0:
```python
import functools

import jax
import jax.numpy as jnp
import numpy as np
from jax import lax
from jax.experimental import pallas as pl
from jax.experimental.pallas import tpu as pltpu
from jax.sharding import PartitionSpec as P

HEAD_SIZE = 128
LANES = 128
ROPE_BASE = 500000.0
OTHER = -(2.0**100)

VMEM_SPEC = pl.BlockSpec(memory_space=pltpu.VMEM)
SMEM_SPEC = pl.BlockSpec(memory_space=pltpu.SMEM)
ANY_SPEC = pl.BlockSpec(memory_space=pl.ANY)


def dot(a, b):
    return jnp.dot(a, b, preferred_element_type=jnp.float32)


def dot_rows(a, b):
    return lax.dot_general(
        a, b, (((1,), (1,)), ((), ())), preferred_element_type=jnp.float32
    )


def call(kernel, out_shape, operands, scratch=(), flops=0, smem=(), anywhere=(), vmem=24):
    specs = [
        SMEM_SPEC if at in smem else ANY_SPEC if at in anywhere else VMEM_SPEC
        for at in range(len(operands))
    ]
    many = isinstance(out_shape, (list, tuple))
    outs = out_shape if many else [out_shape]
    moved = sum(x.size * x.dtype.itemsize for x in [*operands, *outs])
    return pl.pallas_call(
        kernel,
        out_shape=out_shape,
        in_specs=specs,
        out_specs=[VMEM_SPEC] * len(out_shape) if many else VMEM_SPEC,
        scratch_shapes=list(scratch),
        compiler_params=pltpu.CompilerParams(vmem_limit_bytes=vmem * 2**20),
        cost_estimate=pl.CostEstimate(flops=flops, bytes_accessed=moved, transcendentals=0),
    )(*operands)


def weights_kernel(far, owner, wq, wk, wv, *outs):
    depth = wq.shape[0]
    for step, out in enumerate(outs):
        start = pl.multiple_of(far[step] * HEAD_SIZE, HEAD_SIZE)
        width = out.shape[1] - 2 * HEAD_SIZE
        out[:depth, :HEAD_SIZE] = wk[:, pl.ds(start, HEAD_SIZE)]
        out[:depth, HEAD_SIZE : 2 * HEAD_SIZE] = wv[:, pl.ds(start, HEAD_SIZE)]
        start = pl.multiple_of(far[step] * width, width)
        out[:depth, 2 * HEAD_SIZE :] = wq[:, pl.ds(start, width)]
        below = out.shape[0] - depth
        if below:
            row = owner[...].astype(jnp.float32).astype(jnp.bfloat16)
            out[depth:, :] = jnp.zeros((below, out.shape[1]), jnp.bfloat16)
            out[depth:, : row.shape[1]] = jnp.broadcast_to(row, (below, row.shape[1]))


def join_kernel(depth, first, *refs):
    blocks, second, out = refs[:-2], refs[-2], refs[-1]
    tile = out.shape[0] - depth * len(blocks)
    count = LANES
    for step, block in enumerate(blocks):
        out[step * depth : (step + 1) * depth, :] = block[:depth, :]
    row = lax.broadcasted_iota(jnp.int32, (tile, count), 0)

    def spread_row(ref):
        if ref.shape[0] == 1:
            return jnp.broadcast_to(ref[...].astype(jnp.float32), (tile, count))
        return ref[depth:, :count].astype(jnp.float32)

    both = jnp.where(row == 0, spread_row(first), spread_row(second)).astype(out.dtype)
    out[depth * len(blocks) :, :] = jnp.zeros((tile, out.shape[1]), out.dtype)
    out[depth * len(blocks) :, :count] = both


def split_kernel(value, left, right):
    left[...] = value[:, : left.shape[1]]
    right[...] = value[:, left.shape[1] :]


def places_kernel(cap, mine, order, came, mate, twist, doc_starts, freqs, *refs):
    outs, scratch = refs[-11:-6], refs[-6:]
    angles, key_hot, query_bar, slots, columns = outs
    coded, starts, local, owners, landed, semaphore = scratch
    shards, rows = owners.shape
    sources = refs[:-11]
    tile = landed.shape[1]
    copies = []
    for at, source in enumerate(sources):
        bottom = source.at[source.shape[0] - tile :, :rows]
        copies.append(pltpu.make_async_copy(bottom, landed.at[at], semaphore.at[at]))
        copies[-1].start()
    for copy in copies:
        copy.wait()
    each = shards // len(sources)
    for source in range(shards):
        value = landed[source // each].astype(jnp.float32).astype(jnp.int32)
        owners[pl.ds(came[source], 1), :] = value[source % each : source % each + 1, :]
    groups = mine.shape[0]
    team = shards // groups
    span = groups * cap
    owner_at = lax.broadcasted_iota(jnp.int32, (shards, rows), 0)
    upper = jnp.where(
        lax.broadcasted_iota(jnp.int32, (rows, rows), 0)
        < lax.broadcasted_iota(jnp.int32, (rows, rows), 1),
        1.0,
        0.0,
    ).astype(jnp.bfloat16)
    rank_at = lax.broadcasted_iota(jnp.int32, (rows, rows), 0).astype(jnp.float32)
    lane = lax.broadcasted_iota(jnp.int32, (1, rows), 1).astype(jnp.float32)
    before = jnp.zeros((shards, 1), jnp.float32)
    found = jnp.zeros((3 * shards, rows), jnp.float32)
    for shard in range(shards):
        hot = jnp.where(owners[shard : shard + 1, :] == owner_at, 1.0, 0.0)
        within = dot(hot.astype(jnp.bfloat16), upper)
        local[shard : shard + 1, :] = jnp.sum(hot * within, axis=0, keepdims=True)
        rank = jnp.sum(hot * (within + before), axis=0, keepdims=True)
        before = before + jnp.sum(hot, axis=1, keepdims=True)
        rank_hot = jnp.where(rank_at == rank, 1.0, 0.0).astype(jnp.bfloat16)
        codes = jnp.concatenate([hot * float(shard), hot * lane, hot * within], axis=0)
        found = found + dot_rows(codes.astype(jnp.bfloat16), rank_hot)
    shard_of = found[:shards]
    place = shard_of * rows + found[shards : 2 * shards]
    docs = doc_starts.shape[0]
    doc_lane = lax.broadcasted_iota(jnp.int32, (1, LANES), 1)
    doc_row = jnp.full((1, LANES), -1.0, jnp.float32)
    start = jnp.zeros_like(place)
    for doc in range(docs):
        value = doc_starts[doc].astype(jnp.float32)
        start = jnp.maximum(start, jnp.where(value <= place, value, 0.0))
        doc_row = jnp.where(doc_lane == doc, value, doc_row)
    to_shard = shard_of.astype(jnp.int32)
    to_group = jnp.zeros_like(to_shard)
    for group in range(1, groups):
        to_group = jnp.where(to_shard >= group * team, group, to_group)
    to_mate = (to_shard - to_group * team) ^ twist[0]
    inside = found[2 * shards :].astype(jnp.int32)
    coded[...] = (to_mate * groups + to_group) * span + inside
    starts[:shards, :] = start
    starts[shards : 2 * shards, :] = place - start
    flat = jnp.transpose(starts[...])
    which = lax.broadcasted_iota(jnp.int32, flat.shape, 1)
    column = lax.broadcasted_iota(jnp.int32, (rows, 1), 0)
    for group in range(groups):
        own = slice(group * rows, (group + 1) * rows)
        at = mine[group]
        offset = jnp.sum(jnp.where(which == at + shards, flat, 0.0), axis=1, keepdims=True)
        angles[own, :] = offset * freqs[...]
        slots[:, own] = coded[pl.ds(at, 1), :] + group * cap
        shard = group * team + mate[0]
        place = column + shard * rows
        begin = jnp.zeros_like(column)
        for doc in range(docs):
            begin = jnp.where(doc_starts[doc] <= place, doc_starts[doc], begin)
        query_bar[own, :] = jnp.where(begin.astype(jnp.float32) == doc_row, 0.0, OTHER).astype(
            jnp.bfloat16
        )
        owner = owners[pl.ds(shard, 1), :]
        owner_group = jnp.zeros_like(owner)
        for step in range(1, groups):
            owner_group = jnp.where(owner >= step * team, step, owner_group)
        owner_mate = (owner - owner_group * team) ^ twist[0]
        rank = local[pl.ds(shard, 1), :].astype(jnp.int32)
        columns[group : group + 1, :] = owner_mate * span + owner_group * cap + rank
    for block in range(shards):
        own = slice(block * rows, (block + 1) * rows)
        begin = jnp.sum(jnp.where(which == order[block], flat, 0.0), axis=1, keepdims=True)
        key_hot[own, :] = jnp.where(begin == doc_row, 1.0, 0.0).astype(jnp.bfloat16)


def rotate(raw, cosine, sine):
    return raw * cosine + pltpu.roll(raw, HEAD_SIZE // 2, 1) * sine


def project(tokens, weights, cols=slice(None)):
    total = None
    start = 0
    for weight in weights:
        depth = weight.shape[0] // LANES * LANES
        part = dot(tokens[:, start : start + depth], weight[:depth, cols])
        total = part if total is None else total + part
        start += depth
    return total


def tokens_kernel(layout, places, table, *refs):
    row_blocks, col_chunks, blocks = layout
    count = row_blocks * col_chunks
    pieces, weights = refs[:count], refs[count:-4]
    total, later, tokens, loose = refs[-4:]
    rows, width = pieces[0].shape
    for row in range(row_blocks):
        there = pl.ds(pl.multiple_of(places[row] * rows, rows), rows)
        for col in range(col_chunks):
            loose[there, col * width : (col + 1) * width] = pieces[row * col_chunks + col][...]
    width = loose.shape[1] // blocks
    for block in range(blocks):
        source = pl.ds(pl.multiple_of(table[block] * width, width), width)
        tokens[:, block * width : (block + 1) * width] = loose[:, source]
    if later.shape[1] < tokens.shape[1]:
        later[...] = tokens[:, tokens.shape[1] - later.shape[1] :]
    for start in range(0, total.shape[1], 2 * HEAD_SIZE):
        cols = slice(start, start + 2 * HEAD_SIZE)
        total[:, cols] = project(tokens, weights, cols)


def finish_projection(total, later, weights, cols, skip=0):
    if not weights:
        return total[:, cols]
    return total[:, cols] + project(later, weights, slice(cols.start - skip, cols.stop - skip))


def kv_kernel(total, later, *refs):
    weights = refs[:-3]
    cosine, sine, kv = refs[-3:]
    raw = finish_projection(total, later, weights, slice(0, 2 * HEAD_SIZE))
    kv[:, :HEAD_SIZE] = rotate(raw[:, :HEAD_SIZE], cosine[...], sine[...]).astype(kv.dtype)
    kv[:, HEAD_SIZE:] = raw[:, HEAD_SIZE:].astype(kv.dtype)


def query_kernel(layout, total, later, *refs):
    parts, start = layout
    weights = refs[:parts]
    cosine, sine, slots = refs[parts : parts + 3]
    outs, queries = refs[parts + 3 : -1], refs[-1]
    cols = slice(start, start + queries.shape[1])
    raw = finish_projection(total, later, weights, cols, 2 * HEAD_SIZE)
    for head in range(queries.shape[1] // HEAD_SIZE):
        cols = slice(head * HEAD_SIZE, (head + 1) * HEAD_SIZE)
        queries[:, cols] = rotate(raw[:, cols], cosine[...], sine[...]).astype(queries.dtype)
    count = outs[0].shape[0]
    at = lax.broadcasted_iota(jnp.int32, (count, queries.shape[0]), 0)
    for step, out in enumerate(outs):
        hot = jnp.where(at + step * count == slots[...], 1.0, 0.0).astype(jnp.bfloat16)
        out[...] = dot(hot, queries[...]).astype(out.dtype)


def attention_kernel(layout, far, columns, query_bar, key_hot, *refs):
    query_parts, kv_parts, block_rows = layout
    arrived = refs[:query_parts]
    kvs = refs[query_parts : query_parts + kv_parts]
    outs = refs[query_parts + kv_parts : -5]
    keys, values, long, scores, context = refs[-5:]
    groups, rows = columns.shape
    heads = arrived[0].shape[1] // HEAD_SIZE
    start = 0
    for kv in kvs:
        own = slice(start, start + kv.shape[0])
        keys[own, :HEAD_SIZE] = kv[:, :HEAD_SIZE]
        values[own, :] = kv[:, HEAD_SIZE:]
        start += kv.shape[0]
    keys[:, HEAD_SIZE:] = key_hot[...]
    span = arrived[0].shape[0] // groups
    at = lax.broadcasted_iota(jnp.int32, (span * query_parts, rows), 0)
    for group in range(groups):
        hot = jnp.where(at == columns[group : group + 1, :], 1.0, 0.0).astype(jnp.bfloat16)
        there = slice(group * span, (group + 1) * span)
        slab = jnp.concatenate([part[there, :] for part in arrived], axis=0)
        picked = lax.dot_general(
            hot, slab, (((0,), (0,)), ((), ())), preferred_element_type=jnp.float32
        ).astype(jnp.bfloat16)
        own = slice(group * rows, (group + 1) * rows)
        for head in range(heads):
            long[head, own, :HEAD_SIZE] = picked[:, head * HEAD_SIZE : (head + 1) * HEAD_SIZE]
            long[head, own, HEAD_SIZE:] = query_bar[own, :]
    factor = 1.4426950408889634 / HEAD_SIZE**0.5
    blocks = groups * rows // block_rows
    steps = [(block, head) for block in range(blocks) for head in range(heads)]

    def score(step):
        block, head = steps[step]
        own = slice(block * block_rows, (block + 1) * block_rows)
        scores[step % 2] = dot_rows(long[head, own, :], keys[...])

    score(0)
    for step, (block, head) in enumerate(steps):
        if step + 1 < len(steps):
            score(step + 1)
        own = slice(block * block_rows, (block + 1) * block_rows)
        held = scores[step % 2]
        top = jnp.max(held, axis=1, keepdims=True)
        kept = jnp.exp2((held - top) * factor)
        total = jnp.sum(kept, axis=1, keepdims=True)
        mixed = dot(kept.astype(jnp.bfloat16), values[...])
        context[own, head * HEAD_SIZE : (head + 1) * HEAD_SIZE] = (mixed / total).astype(
            context.dtype
        )
    for step, out in enumerate(outs):
        out[...] = context[pl.ds(pl.multiple_of(far[step] * rows, rows), rows), :]


def finish_kernel(far, *refs):
    out = refs[-1]
    groups = far.shape[0]
    parts = (len(refs) - 1) // groups
    width = refs[0].shape[1]
    for part in range(parts):
        for step in range(groups):
            start = pl.multiple_of((far[step] * parts + part) * width, width)
            out[:, pl.ds(start, width)] = refs[part * groups + step][...]


def turn(value, axis, bits):
    count = lax.axis_size(axis)
    return lax.ppermute(value, axis, [(i, i ^ bits) for i in range(count)])


def after(value, *others):
    return lax.optimization_barrier((value, *others))[0]


def spread(value, *others):
    across = turn(value, "team", 2)
    last = turn(after(across, *others), "team", 1)
    return [value, across, turn(value, "team", 1), last]


def body(stored, source_owner, doc_ids, doc_starts, wq, wk, wv):
    groups, team = lax.axis_size("line"), lax.axis_size("team")
    nctx, ntp = groups * team, lax.axis_size("tp")
    group, mate = lax.axis_index("line"), lax.axis_index("team")
    rows = stored.shape[0]
    cap = 2 * rows // nctx
    size = HEAD_SIZE
    depth = wq.shape[0]
    split = groups > 1
    pair = 2 * size
    parts = wq.shape[1] // groups // pair
    total_rows = groups * rows
    width = stored.shape[1] * ntp
    keys = nctx * rows
    far = group ^ jnp.arange(groups, dtype=jnp.int32)

    def flip(value):
        return lax.ppermute(value, "tp", [(0, 1), (1, 0)])

    columns_each = (1 + parts) * pair
    tile = 16
    slabs = call(
        weights_kernel,
        [
            jax.ShapeDtypeStruct((depth + tile * (step % 2), columns_each), jnp.bfloat16)
            for step in range(groups)
        ],
        [far, source_owner[None, :], wq, wk, wv],
        smem=(0,),
    )

    if split:
        def join(first, blocks, second):
            shape = (depth * len(blocks) + tile, columns_each)
            return call(
                functools.partial(join_kernel, depth),
                jax.ShapeDtypeStruct(shape, jnp.bfloat16),
                [first, *blocks, second],
            )

        inner, outer = [(1, 2), (2, 1)], [(1, 0), (2, 3)]
        near = turn(stored, "line", 1)
        over = lax.ppermute(stored, "line", inner)
        flips = [flip(stored)]
        weights_near = turn(slabs[1], "line", 1)
        weights_third = turn(slabs[3], "line", 3)
        over_near = lax.ppermute(after(near, over, flips[0], *slabs), "line", inner)
        end = lax.ppermute(after(over, near, weights_near), "line", outer)
        flips.append(flip(after(near, flips[0], weights_third)))
        held = join(source_owner[None, :], [slabs[0], weights_near], weights_near)
        second_owner = turn(after(source_owner, weights_near), "line", 2)[None, :]
        first = spread(held)
        edge = (group == 0) | (group == groups - 1)
        third = jnp.where(edge, end, over)
        end_near = lax.ppermute(after(over_near, flips[1]), "line", outer)
        flips.append(flip(after(third, flips[1], second_owner)))
        weights_second = turn(after(slabs[2], over_near, end, first[1]), "line", 2)
        fourth = jnp.where(edge, end_near, over_near)
        flips.append(flip(after(fourth, flips[2])))
        third_held = join(weights_third, [weights_third], second_owner)
        second = spread(after(third_held, flips[2], first[1]))
        kv_second, query_second = call(
            split_kernel,
            [
                jax.ShapeDtypeStruct((depth, pair), jnp.bfloat16),
                jax.ShapeDtypeStruct((depth, parts * pair), jnp.bfloat16),
            ],
            [after(weights_second, flips[3], second[1])],
        )
        early = [part for both in zip(first, second) for part in both]
        places = jnp.stack(
            [group, group ^ 1, group ^ jnp.where(edge, 2, 3), group ^ jnp.where(edge, 3, 2)]
        )
        pieces = [
            chunk for both in zip((stored, near, third, fourth), flips) for chunk in both
        ]
        chunks = ntp
        owners = early
    else:
        pieces = [lax.all_gather(stored, "tp", axis=1, tiled=True)]
        places = jnp.zeros((1,), jnp.int32)
        chunks = 1
        early = [lax.all_gather(slabs[0], "team", axis=0, tiled=True)]
        owners = [lax.all_gather(source_owner, "team", axis=0)]

    if split:
        rel = jnp.arange(groups, dtype=jnp.int32)
        turns = mate ^ jnp.array([0, 2, 1, 3], dtype=jnp.int32)
        order = (rel[None, :] * team + turns[:, None]).reshape(-1)
        came = (far[jnp.array([0, 1, 3, 2])][None, :] * team + turns[:, None]).reshape(-1)
        rows_of = jnp.concatenate(
            [came.reshape(team, groups)[:, :3].reshape(-1), came.reshape(team, groups)[:, 3]]
        )
        mine = rel * team + mate
        twist = mate[None]
        share = nctx // ntp
        table = rows_of % share + jnp.where(rows_of // share == lax.axis_index("tp"), 0, share)
    else:
        order = came = jnp.arange(nctx, dtype=jnp.int32)
        mine = mate[None]
        twist = table = jnp.zeros((1,), jnp.int32)

    freqs = ROPE_BASE ** (-np.arange(size // 2) * 2.0 / size)
    freqs = jnp.asarray(np.concatenate([freqs, freqs])[None, :], jnp.float32)
    sign = jnp.asarray(np.repeat([-1.0, 1.0], size // 2)[None, :], jnp.float32)
    angles, key_hot, query_bar, slots, columns = call(
        functools.partial(places_kernel, cap),
        [
            jax.ShapeDtypeStruct((total_rows, size), jnp.float32),
            jax.ShapeDtypeStruct((keys, LANES), jnp.bfloat16),
            jax.ShapeDtypeStruct((total_rows, LANES), jnp.bfloat16),
            jax.ShapeDtypeStruct((1, total_rows), jnp.int32),
            jax.ShapeDtypeStruct((groups, rows), jnp.int32),
        ],
        [mine, order, came, mate[None], twist, doc_starts, freqs, *owners],
        scratch=[
            pltpu.VMEM((nctx, rows), jnp.int32),
            pltpu.VMEM((max(2 * nctx, LANES), rows), jnp.float32),
            pltpu.VMEM((nctx, rows), jnp.float32),
            pltpu.VMEM((nctx, rows), jnp.int32),
            pltpu.VMEM((len(owners), tile if split else nctx, rows), owners[0].dtype),
            pltpu.SemaphoreType.DMA((len(owners),)),
        ],
        flops=10**9,
        smem=(0, 1, 2, 3, 4, 5),
        anywhere=range(7, 7 + len(owners)),
    )
    cosine = jnp.cos(angles)
    sine = jnp.sin(angles) * sign

    rest = width // groups if split else width
    total, later = call(
        functools.partial(tokens_kernel, (groups, chunks, nctx if split else 1)),
        [
            jax.ShapeDtypeStruct((total_rows, columns_each), jnp.float32),
            jax.ShapeDtypeStruct((total_rows, rest if split else LANES), jnp.bfloat16),
        ],
        [places, table, *pieces, *early],
        scratch=[
            pltpu.VMEM((total_rows, width), jnp.bfloat16),
            pltpu.VMEM((total_rows, width), jnp.bfloat16),
        ],
        flops=2 * total_rows * width * columns_each,
        smem=(0, 1),
        vmem=32,
    )
    kv_late = spread(kv_second, total, cosine) if split else []
    kv = call(
        kv_kernel,
        jax.ShapeDtypeStruct((total_rows, pair), jnp.bfloat16),
        [total, later, *kv_late, cosine, sine],
        flops=2 * total_rows * rest * pair,
    )
    late = spread(query_second, kv) if split else []

    block_rows = min(2 * rows, total_rows)
    lanes_out = team if split else 1
    slot_count = nctx * groups * cap

    def project_part(part):
        return call(
            functools.partial(query_kernel, (len(late), (1 + part) * pair)),
            [jax.ShapeDtypeStruct((slot_count // lanes_out, pair), jnp.bfloat16)] * lanes_out,
            [total, later, *late, cosine, sine, slots],
            scratch=[pltpu.VMEM((total_rows, pair), jnp.bfloat16)],
            flops=2 * total_rows * (rest + slot_count) * pair,
        )

    def attend(arrived):
        context = call(
            functools.partial(attention_kernel, (len(arrived), len(kvs), block_rows)),
            [jax.ShapeDtypeStruct((rows, pair), jnp.bfloat16)] * groups,
            [far, columns, query_bar, key_hot, *arrived, *kvs],
            scratch=[
                pltpu.VMEM((keys, size + LANES), jnp.bfloat16),
                pltpu.VMEM((keys, size), jnp.bfloat16),
                pltpu.VMEM((pair // size, total_rows, size + LANES), jnp.bfloat16),
                pltpu.VMEM((2, block_rows, keys), jnp.float32),
                pltpu.VMEM((total_rows, pair), jnp.bfloat16),
            ],
            flops=8 * total_rows * pair * keys,
            smem=(0,),
            vmem=40,
        )
        return [context[0]] + [turn(context[step], "line", step) for step in range(1, groups)]

    def exchange(leaving):
        if split:
            return [leaving[0]] + [turn(leaving[e], "team", e) for e in range(1, team)]
        return [lax.all_to_all(leaving[0], "team", 0, 0, tiled=True)]

    leaving = [project_part(part) for part in range(parts)]
    arrived = [exchange(part) for part in leaving]
    if split:
        across = turn(kv, "team", 2)
        kvs = [kv, across] + [
            turn(after(part, arrived[0][1], leaving[-1][0]), "team", 1) for part in (kv, across)
        ]
    else:
        kvs = [lax.all_gather(kv, "team", axis=0, tiled=True)]
    ready = [piece for queries in arrived for piece in attend(queries)]

    return call(
        finish_kernel,
        jax.ShapeDtypeStruct((rows, wq.shape[1]), jnp.bfloat16),
        [far, *ready],
        smem=(0,),
    )


def solution(mesh):
    def program(stored, source_owner, doc_ids, doc_starts, wq, wk, wv):
        ctx, tp = mesh.shape["ctx"], mesh.shape["tp"]
        groups = wk.shape[1] // HEAD_SIZE // tp
        parts = jax.sharding.Mesh(
            mesh.devices.reshape(groups, ctx // groups, tp), ("line", "team", "tp")
        )
        both = ("line", "team")
        return jax.shard_map(
            body,
            mesh=parts,
            in_specs=(
                P(both, "tp"),
                P(both),
                P(both),
                P(),
                P(both, "tp"),
                P(both, "tp"),
                P(both, "tp"),
            ),
            out_specs=P(both, "tp"),
            check_vma=False,
        )(stored, source_owner, doc_ids, doc_starts, wq, wk, wv)

    return program
```

profile of v0, /device:TPU:0, one launch (start us, length us, event | category | flops | bytes accessed | tf_op | source)
XLA Modules:
  0.0 130.9 jit_solution(13238070713657229624)
XLA Ops:
  0.0 3.0 %collective-permute-start.4 = (bf16[128,2048]{1,0:T(8,128)(2,1)}, bf16[128,2048]{1,0:T(8,128)(2,1)S(1)}, u32[]{:S(2)}, u32[]{:S(2)}) collective-permute-start(bf16[128,2048]{1,0:T(8,128)(2,1)} %refs_0_.1), channel_id=1, source_target_pairs={{0,8},{8,0},{16,24},{24,16},{1,9},{9,1},{17,25},{25,17},{2,10},{10... | collective-permute-start | bytes 1572872 | tf_op jit(solution)/shard_map/ppermute | solution.py:313
  3.0 1.5 %collective-permute-start.3 = (bf16[128,2048]{1,0:T(8,128)(2,1)}, bf16[128,2048]{1,0:T(8,128)(2,1)}, u32[]{:S(2)}, u32[]{:S(2)}) collective-permute-start(bf16[128,2048]{1,0:T(8,128)(2,1)} %refs_0_.1), channel_id=1, source_target_pairs={{8,16},{16,8},{9,17},{17,9},{10,18},{18,10},{11,19},{19,11},{12,20... | collective-permute-start | bytes 1572872 | tf_op jit(solution)/shard_map/ppermute | solution.py:368
  4.5 1.5 %collective-permute-start.6 = (bf16[128,2048]{1,0:T(8,128)(2,1)}, bf16[128,2048]{1,0:T(8,128)(2,1)S(1)}, u32[]{:S(2)}, u32[]{:S(2)}) collective-permute-start(bf16[128,2048]{1,0:T(8,128)(2,1)} %refs_0_.1), channel_id=1, source_target_pairs={{0,1},{1,0},{2,3},{3,2},{4,5},{5,4},{6,7},{7,6},{8,9},{9,8},{10,11... | collective-permute-start | bytes 1572872 | tf_op jit(solution)/shard_map/ppermute | solution.py:343
  6.0 1.2 copy-done
  7.2 0.9 copy-done.1
  8.2 0.9 copy-done.2
  9.2 0.7 copy-done.3
  9.8 0.7 shard_map.100
  10.5 2.5 %collective-permute-start.1 = (bf16[272,768]{1,0:T(8,128)(2,1)S(1)}, bf16[272,768]{1,0:T(8,128)(2,1)S(1)}, u32[]{:S(2)}, u32[]{:S(2)}) collective-permute-start(bf16[272,768]{1,0:T(8,128)(2,1)S(1)} %get-tuple-element.50), channel_id=1, source_target_pairs={{0,24},{8,16},{16,8},{24,0},{1,25},{9,17},{17,9},{25,1},{2,26},{10... | collective-permute-start | bytes 1253384 | tf_op jit(solution)/shard_map/ppermute | solution.py:313
  13.1 1.3 collective-permute-start
  14.3 1.3 %collective-permute-done.4.refs_2_ = bf16[128,2048]{1,0:T(8,128)(2,1)S(1)} collective-permute-done((bf16[128,2048]{1,0:T(8,128)(2,1)}, bf16[128,2048]{1,0:T(8,128)(2,1)S(1)}, u32[]{:S(2)}, u32[]{:S(2)}) %collective-permute-start.4) | collective-permute-done | bytes 524320 | tf_op jit(solution)/shard_map/ppermute | solution.py:313
  15.7 2.4 %collective-permute-done.6.refs_1_ = bf16[128,2048]{1,0:T(8,128)(2,1)S(1)} collective-permute-done((bf16[128,2048]{1,0:T(8,128)(2,1)}, bf16[128,2048]{1,0:T(8,128)(2,1)S(1)}, u32[]{:S(2)}, u32[]{:S(2)}) %collective-permute-start.6) | collective-permute-done | bytes 524320 | tf_op jit(solution)/shard_map/ppermute | solution.py:343
  18.1 1.5 %collective-permute-start.15 = (bf16[128,2048]{1,0:T(8,128)(2,1)S(1)}, bf16[128,2048]{1,0:T(8,128)(2,1)}, u32[]{:S(2)}, u32[]{:S(2)}) collective-permute-start(bf16[128,2048]{1,0:T(8,128)(2,1)S(1)} %collective-permute-done.4.refs_2_), channel_id=1, source_target_pairs={{8,16},{16,8},{9,17},{17,9},{10,18},{18,10},{11,19},{19,11},{12,20... | collective-permute-start | bytes 1572872 | tf_op jit(solution)/shard_map/ppermute | solution.py:372
  19.6 8.0 %collective-permute-done.1.first.refs_0_ = bf16[272,768]{1,0:T(8,128)(2,1)S(1)} collective-permute-done((bf16[272,768]{1,0:T(8,128)(2,1)S(1)}, bf16[272,768]{1,0:T(8,128)(2,1)S(1)}, u32[]{:S(2)}, u32[]{:S(2)}) %collective-permute-start.1) | collective-permute-done | bytes 417824 | tf_op jit(solution)/shard_map/ppermute | solution.py:313
  27.5 1.5 %collective-permute-start.7 = (bf16[128,2048]{1,0:T(8,128)(2,1)S(1)}, bf16[128,2048]{1,0:T(8,128)(2,1)}, u32[]{:S(2)}, u32[]{:S(2)}) collective-permute-start(bf16[128,2048]{1,0:T(8,128)(2,1)S(1)} %collective-permute-done.4.refs_2_), channel_id=1, source_target_pairs={{0,1},{1,0},{2,3},{3,2},{4,5},{5,4},{6,7},{7,6},{8,9},{9,8},{10,11... | collective-permute-start | bytes 1572872 | tf_op jit(solution)/shard_map/ppermute | solution.py:343
  29.0 4.0 %collective-permute-done.refs_1_.refs_2_ = bf16[272,768]{1,0:T(8,128)(2,1)S(1)} collective-permute-done((bf16[272,768]{1,0:T(8,128)(2,1)S(1)}, bf16[272,768]{1,0:T(8,128)(2,1)S(1)}, u32[]{:S(2)}, u32[]{:S(2)}) %collective-permute-start) | collective-permute-done | bytes 417824 | tf_op jit(solution)/shard_map/ppermute | solution.py:313
  33.1 1.3 collective-permute-start.5
  34.4 0.6 gather_fusion
  35.0 9.7 %collective-permute-start.2 = (s32[128]{0:T(128)S(1)}, s32[128]{0:T(128)S(1)}, u32[]{:S(2)}, u32[]{:S(2)}) collective-permute-start(s32[128]{0:T(128)S(1)} %copy-done.4), channel_id=1, source_target_pairs={{0,16},{8,24},{16,0},{24,8},{1,17},{9,25},{17,1},{25,9},{2,18},{10... | collective-permute-start | bytes 1544 | tf_op jit(solution)/shard_map/ppermute | solution.py:313
  44.8 1.6 %collective-permute-start.9 = (bf16[528,768]{1,0:T(8,128)(2,1)S(1)}, bf16[528,768]{1,0:T(8,128)(2,1)S(1)}, u32[]{:S(2)}, u32[]{:S(2)}) collective-permute-start(bf16[528,768]{1,0:T(8,128)(2,1)S(1)} %shard_map.101.refs_0_.refs_8_), channel_id=1, source_target_pairs={{0,4},{2,6},{4,0},{6,2},{1,5},{3,7},{5,1},{7,3},{8,12},{10,14},{12... | collective-permute-start | bytes 2433032 | tf_op jit(solution)/shard_map/ppermute | solution.py:313
  46.4 1.3 collective-permute-start.16
  47.7 5.1 %collective-permute-done.5 = bf16[128,2048]{1,0:T(8,128)(2,1)} collective-permute-done((bf16[128,2048]{1,0:T(8,128)(2,1)}, bf16[128,2048]{1,0:T(8,128)(2,1)}, u32[]{:S(2)}, u32[]{:S(2)}) %collective-permute-start.5) | collective-permute-done | bytes 524320 | tf_op jit(solution)/shard_map/ppermute | solution.py:373
  52.8 1.1 broadcast_select_fusion.1.refs_4_
  54.7 6.8 %collective-permute-done.9.refs_2_.refs_10_ = bf16[528,768]{1,0:T(8,128)(2,1)S(1)} collective-permute-done((bf16[528,768]{1,0:T(8,128)(2,1)S(1)}, bf16[528,768]{1,0:T(8,128)(2,1)S(1)}, u32[]{:S(2)}, u32[]{:S(2)}) %collective-permute-start.9) | collective-permute-done | bytes 811040 | tf_op jit(solution)/shard_map/ppermute | solution.py:313
  61.5 0.3 collective-permute-start.18
  61.8 1.9 %collective-permute-done.8.refs_5_ = bf16[128,2048]{1,0:T(8,128)(2,1)} collective-permute-done((bf16[128,2048]{1,0:T(8,128)(2,1)S(1)}, bf16[128,2048]{1,0:T(8,128)(2,1)}, u32[]{:S(2)}, u32[]{:S(2)}) %collective-permute-start.8) | collective-permute-done | bytes 524320 | tf_op jit(solution)/shard_map/ppermute | solution.py:343
  63.7 1.5 %collective-permute-start.10 = (bf16[272,768]{1,0:T(8,128)(2,1)S(1)}, bf16[272,768]{1,0:T(8,128)(2,1)S(1)}, u32[]{:S(2)}, u32[]{:S(2)}) collective-permute-start(bf16[272,768]{1,0:T(8,128)(2,1)S(1)} %shard_map.102.refs_1_.refs_9_), channel_id=1, source_target_pairs={{0,4},{2,6},{4,0},{6,2},{1,5},{3,7},{5,1},{7,3},{8,12},{10,14},{12... | collective-permute-start | bytes 1253384 | tf_op jit(solution)/shard_map/ppermute | solution.py:313
  65.2 1.1 broadcast_select_fusion.refs_6_
  66.3 0.6 collective-permute-start.17
  66.9 7.0 %collective-permute-done.10.refs_3_.refs_11_ = bf16[272,768]{1,0:T(8,128)(2,1)S(1)} collective-permute-done((bf16[272,768]{1,0:T(8,128)(2,1)S(1)}, bf16[272,768]{1,0:T(8,128)(2,1)S(1)}, u32[]{:S(2)}, u32[]{:S(2)}) %collective-permute-start.10) | collective-permute-done | bytes 417824 | tf_op jit(solution)/shard_map/ppermute | solution.py:313
  73.9 3.5 %collective-permute-done.18.value = bf16[256,768]{1,0:T(8,128)(2,1)S(1)} collective-permute-done((bf16[256,768]{1,0:T(8,128)(2,1)S(1)}, bf16[256,768]{1,0:T(8,128)(2,1)S(1)}, u32[]{:S(2)}, u32[]{:S(2)}) %collective-permute-start.18) | collective-permute-done | bytes 393248 | tf_op jit(solution)/shard_map/ppermute | solution.py:313
  77.5 1.0 collective-permute-done.17.refs_7_
  78.6 0.6 collective-permute-start.21
  79.3 1.4 %collective-permute-start.19 = (bf16[256,512]{1,0:T(8,128)(2,1)S(1)}, bf16[256,512]{1,0:T(8,128)(2,1)S(1)}, u32[]{:S(2)}, u32[]{:S(2)}) collective-permute-start(bf16[256,512]{1,0:T(8,128)(2,1)S(1)} %get-tuple-element.67.refs_0_), channel_id=1, source_target_pairs={{0,4},{2,6},{4,0},{6,2},{1,5},{3,7},{5,1},{7,3},{8,12},{10,14},{12... | collective-permute-start | bytes 786440 | tf_op jit(solution)/shard_map/ppermute | solution.py:313
  80.8 4.3 %shard_map.104 = (f32[512,768]{1,0:T(8,128)S(1)}, bf16[512,1024]{1,0:T(8,128)(2,1)S(1)}) custom-call(s32[4]{0:T(128)S(1)} %pad_add_fusion.places, s32[16]{0:T(128)S(1)} %fusion.table, bf16[128,2048]{1,0:T(8,128)(2,1)S(1)} %copy-done.7, bf16[128,2048]{1,0:T(8,128)(2,1)S(1)} %copy-done.9, bf16[128,2048]{1,0:T(8,128)(2,1)S(1)} %collective-permute-done.4.refs_2_, ...), custom_call_target="tpu_custom_call" | custom-call | flops 3221225472 | bytes 11731024 | tf_op jit(solution)/shard_map/pallas_call | solution.py:39
  85.1 2.7 %shard_map.103 = (f32[512,128]{1,0:T(8,128)S(1)}, bf16[2048,128]{1,0:T(8,128)(2,1)S(1)}, bf16[512,128]{1,0:T(8,128)(2,1)S(1)}, s32[1,512]{1,0:T(1,128)S(1)}, s32[4,128]{1,0:T(4,128)S(1)}) custom-call(s32[4]{0:T(128)S(1)} %broadcast_add_fusion.2.mine, s32[16]{0:T(128)S(1)} %add.56.order, s32[16]{0:T(128)S(1)} %add.60.came, s32[1]{0:T(128)} %bitcast.mate.twist, ...), custom_call_target="tpu_custom_call" | custom-call | flops 1000000000 | bytes 5837516 | tf_op jit(solution)/shard_map/pallas_call | solution.py:39
  87.8 0.9 sine_multiply_fusion
  89.0 0.3 collective-permute-start.20
  89.3 0.8 collective-permute-done.23.refs_3_
  90.2 0.5 shard_map.106.refs_4_
  90.7 0.2 collective-permute-start.24
  90.9 0.7 collective-permute-start.28
  91.6 0.7 collective-permute-done.24.refs_3_
  92.3 1.4 %shard_map.107 = (bf16[256,256]{1,0:T(8,128)(2,1)S(1)}, bf16[256,256]{1,0:T(8,128)(2,1)S(1)}, bf16[256,256]{1,0:T(8,128)(2,1)S(1)}, bf16[256,256]{1,0:T(8,128)(2,1)S(1)}) custom-call(f32[512,768]{1,0:T(8,128)S(1)} %get-tuple-element.63.total, bf16[512,1024]{1,0:T(8,128)(2,1)S(1)} %get-tuple-element.64.later, bf16[256,512]{1,0:T(8,128)(2,1)S(1)} %get-tuple-element.67.refs_0_, ...), custom_call_target="tpu_custom_call" | custom-call | flops 536870912 | bytes 4720640 | tf_op jit(solution)/shard_map/pallas_call | solution.py:39
  93.7 0.2 collective-permute-start.25
  94.0 1.4 %shard_map.108 = (bf16[256,256]{1,0:T(8,128)(2,1)S(1)}, bf16[256,256]{1,0:T(8,128)(2,1)S(1)}, bf16[256,256]{1,0:T(8,128)(2,1)S(1)}, bf16[256,256]{1,0:T(8,128)(2,1)S(1)}) custom-call(f32[512,768]{1,0:T(8,128)S(1)} %get-tuple-element.63.total, bf16[512,1024]{1,0:T(8,128)(2,1)S(1)} %get-tuple-element.64.later, bf16[256,512]{1,0:T(8,128)(2,1)S(1)} %get-tuple-element.67.refs_0_, ...), custom_call_target="tpu_custom_call" | custom-call | flops 536870912 | bytes 4720640 | tf_op jit(solution)/shard_map/pallas_call | solution.py:39
  95.4 4.1 %collective-permute-done.28.refs_5_ = bf16[512,256]{1,0:T(8,128)(2,1)S(1)} collective-permute-done((bf16[512,256]{1,0:T(8,128)(2,1)S(1)}, bf16[512,256]{1,0:T(8,128)(2,1)S(1)}, u32[]{:S(2)}, u32[]{:S(2)}) %collective-permute-start.28) | collective-permute-done | bytes 262176 | tf_op jit(solution)/shard_map/ppermute | solution.py:313
  99.5 0.5 collective-permute-start.29
  100.0 0.7 collective-permute-start.35
  100.7 1.2 collective-permute-start.36
  101.9 0.7 collective-permute-start.26
  102.5 3.8 %collective-permute-done.35.refs_2_ = bf16[256,256]{1,0:T(8,128)(2,1)S(1)} collective-permute-done((bf16[256,256]{1,0:T(8,128)(2,1)S(1)}, bf16[256,256]{1,0:T(8,128)(2,1)S(1)}, u32[]{:S(2)}, u32[]{:S(2)}) %collective-permute-start.35) | collective-permute-done | bytes 131104 | tf_op jit(solution)/shard_map/ppermute | solution.py:313
  106.3 2.0 %collective-permute-done.36.refs_3_ = bf16[256,256]{1,0:T(8,128)(2,1)S(1)} collective-permute-done((bf16[256,256]{1,0:T(8,128)(2,1)S(1)}, bf16[256,256]{1,0:T(8,128)(2,1)S(1)}, u32[]{:S(2)}, u32[]{:S(2)}) %collective-permute-start.36) | collective-permute-done | bytes 131104 | tf_op jit(solution)/shard_map/ppermute | solution.py:313
  108.3 4.0 %shard_map.110 = (bf16[128,256]{1,0:T(8,128)(2,1)S(1)}, bf16[128,256]{1,0:T(8,128)(2,1)S(1)}, bf16[128,256]{1,0:T(8,128)(2,1)S(1)}, bf16[128,256]{1,0:T(8,128)(2,1)S(1)}) custom-call(s32[4]{0:T(128)S(1)} %iota_xor_fusion.far, s32[4,128]{1,0:T(4,128)S(1)} %get-tuple-element.56.columns, bf16[512,128]{1,0:T(8,128)(2,1)S(1)} %get-tuple-element.57.query_bar, ...), custom_call_target="tpu_custom_call" | custom-call | flops 2147483648 | bytes 2492432 | tf_op jit(solution)/shard_map/pallas_call | solution.py:39
  112.3 1.8 %collective-permute-start.37 = (bf16[128,256]{1,0:T(8,128)(2,1)S(1)}, bf16[128,256]{1,0:T(8,128)(2,1)S(1)}, u32[]{:S(2)}, u32[]{:S(2)}) collective-permute-start(bf16[128,256]{1,0:T(8,128)(2,1)S(1)} %get-tuple-element.88), channel_id=1, source_target_pairs={{0,8},{8,0},{16,24},{24,16},{1,9},{9,1},{17,25},{25,17},{2,10},{10... | collective-permute-start | bytes 196616 | tf_op jit(solution)/shard_map/ppermute | solution.py:313
  114.2 0.9 collective-permute-start.38
  115.1 1.7 %collective-permute-start.39 = (bf16[128,256]{1,0:T(8,128)(2,1)S(1)}, bf16[128,256]{1,0:T(8,128)(2,1)S(1)}, u32[]{:S(2)}, u32[]{:S(2)}) collective-permute-start(bf16[128,256]{1,0:T(8,128)(2,1)S(1)} %get-tuple-element.90), channel_id=1, source_target_pairs={{0,24},{8,16},{16,8},{24,0},{1,25},{9,17},{17,9},{25,1},{2,26},{10... | collective-permute-start | bytes 196616 | tf_op jit(solution)/shard_map/ppermute | solution.py:313
  116.8 3.8 %shard_map.109 = (bf16[128,256]{1,0:T(8,128)(2,1)S(1)}, bf16[128,256]{1,0:T(8,128)(2,1)S(1)}, bf16[128,256]{1,0:T(8,128)(2,1)S(1)}, bf16[128,256]{1,0:T(8,128)(2,1)S(1)}) custom-call(s32[4]{0:T(128)S(1)} %iota_xor_fusion.far, s32[4,128]{1,0:T(4,128)S(1)} %get-tuple-element.56.columns, bf16[512,128]{1,0:T(8,128)(2,1)S(1)} %get-tuple-element.57.query_bar, ...), custom_call_target="tpu_custom_call" | custom-call | flops 2147483648 | bytes 2492432 | tf_op jit(solution)/shard_map/pallas_call | solution.py:39
  120.6 0.9 collective-permute-start.31
  121.5 1.8 %collective-permute-start.32 = (bf16[128,256]{1,0:T(8,128)(2,1)S(1)}, bf16[128,256]{1,0:T(8,128)(2,1)S(1)}, u32[]{:S(2)}, u32[]{:S(2)}) collective-permute-start(bf16[128,256]{1,0:T(8,128)(2,1)S(1)} %get-tuple-element.82), channel_id=1, source_target_pairs={{0,16},{8,24},{16,0},{24,8},{1,17},{9,25},{17,1},{25,9},{2,18},{10... | collective-permute-start | bytes 196616 | tf_op jit(solution)/shard_map/ppermute | solution.py:313
  123.4 1.7 %collective-permute-start.33 = (bf16[128,256]{1,0:T(8,128)(2,1)S(1)}, bf16[128,256]{1,0:T(8,128)(2,1)S(1)}, u32[]{:S(2)}, u32[]{:S(2)}) collective-permute-start(bf16[128,256]{1,0:T(8,128)(2,1)S(1)} %get-tuple-element.83), channel_id=1, source_target_pairs={{0,24},{8,16},{16,8},{24,0},{1,25},{9,17},{17,9},{25,1},{2,26},{10... | collective-permute-start | bytes 196616 | tf_op jit(solution)/shard_map/ppermute | solution.py:313
  125.0 0.6 collective-permute-done.31.refs_1_
  125.6 3.9 %collective-permute-done.32.refs_2_ = bf16[128,256]{1,0:T(8,128)(2,1)S(1)} collective-permute-done((bf16[128,256]{1,0:T(8,128)(2,1)S(1)}, bf16[128,256]{1,0:T(8,128)(2,1)S(1)}, u32[]{:S(2)}, u32[]{:S(2)}) %collective-permute-start.32) | collective-permute-done | bytes 65568 | tf_op jit(solution)/shard_map/ppermute | solution.py:313
  129.5 1.4 %shard_map.111 = bf16[128,2048]{1,0:T(8,128)(2,1)} custom-call(s32[4]{0:T(128)S(1)} %iota_xor_fusion.far, bf16[128,256]{1,0:T(8,128)(2,1)S(1)} %get-tuple-element.80.refs_0_, bf16[128,256]{1,0:T(8,128)(2,1)S(1)} %collective-permute-done.31.refs_1_, bf16[128,256]{1,0:T(8,128)(2,1)S(1)} %collective-permute-done.32.refs_2_, ...), custom_call_target="tpu_custom_call" | custom-call | bytes 1048592 | tf_op jit(solution)/shard_map/pallas_call | solution.py:39
  (73 shorter events, 1.5 us)
Async XLA Ops:
  0.0 34.4 %copy-start.10 = (s32[4]{0:T(128)S(1)}, s32[4]{0:T(128)}, u32[]{:S(2)}) copy-start(s32[4]{0:T(128)} %constant.65) | copy-start | bytes 52
  0.0 35.0 %copy-start.4 = (s32[128]{0:T(128)S(1)}, s32[128]{0:T(128)}, u32[]{:S(2)}) copy-start(s32[128]{0:T(128)} %param.12) | copy-start | bytes 1540
  0.0 15.7 %collective-permute-start.4 = (bf16[128,2048]{1,0:T(8,128)(2,1)}, bf16[128,2048]{1,0:T(8,128)(2,1)S(1)}, u32[]{:S(2)}, u32[]{:S(2)}) collective-permute-start(bf16[128,2048]{1,0:T(8,128)(2,1)} %refs_0_.1), channel_id=1, source_target_pairs={{0,8},{8,0},{16,24},{24,16},{1,9},{9,1},{17,25},{25,17},{2,10},{10... | collective-permute-start | bytes 1572872 | tf_op jit(solution)/shard_map/ppermute | solution.py:313
  3.0 12.6 %collective-permute-start.3 = (bf16[128,2048]{1,0:T(8,128)(2,1)}, bf16[128,2048]{1,0:T(8,128)(2,1)}, u32[]{:S(2)}, u32[]{:S(2)}) collective-permute-start(bf16[128,2048]{1,0:T(8,128)(2,1)} %refs_0_.1), channel_id=1, source_target_pairs={{8,16},{16,8},{9,17},{17,9},{10,18},{18,10},{11,19},{19,11},{12,20... | collective-permute-start | bytes 1572872 | tf_op jit(solution)/shard_map/ppermute | solution.py:368
  4.5 13.6 %collective-permute-start.6 = (bf16[128,2048]{1,0:T(8,128)(2,1)}, bf16[128,2048]{1,0:T(8,128)(2,1)S(1)}, u32[]{:S(2)}, u32[]{:S(2)}) collective-permute-start(bf16[128,2048]{1,0:T(8,128)(2,1)} %refs_0_.1), channel_id=1, source_target_pairs={{0,1},{1,0},{2,3},{3,2},{4,5},{5,4},{6,7},{7,6},{8,9},{9,8},{10,11... | collective-permute-start | bytes 1572872 | tf_op jit(solution)/shard_map/ppermute | solution.py:343
  6.0 1.2 copy-start
  7.2 0.9 copy-start.1
  8.2 0.9 copy-start.2
  9.1 0.7 copy-start.3
  10.5 17.0 %collective-permute-start.1 = (bf16[272,768]{1,0:T(8,128)(2,1)S(1)}, bf16[272,768]{1,0:T(8,128)(2,1)S(1)}, u32[]{:S(2)}, u32[]{:S(2)}) collective-permute-start(bf16[272,768]{1,0:T(8,128)(2,1)S(1)} %get-tuple-element.50), channel_id=1, source_target_pairs={{0,24},{8,16},{16,8},{24,0},{1,25},{9,17},{17,9},{25,1},{2,26},{10... | collective-permute-start | bytes 1253384 | tf_op jit(solution)/shard_map/ppermute | solution.py:313
  13.1 20.0 %collective-permute-start = (bf16[272,768]{1,0:T(8,128)(2,1)S(1)}, bf16[272,768]{1,0:T(8,128)(2,1)S(1)}, u32[]{:S(2)}, u32[]{:S(2)}) collective-permute-start(bf16[272,768]{1,0:T(8,128)(2,1)S(1)} %get-tuple-element.49), channel_id=1, source_target_pairs={{0,8},{8,0},{16,24},{24,16},{1,9},{9,1},{17,25},{25,17},{2,10},{10... | collective-permute-start | bytes 1253384 | tf_op jit(solution)/shard_map/ppermute | solution.py:313
  18.1 29.6 %copy-start.8 = (bf16[128,2048]{1,0:T(8,128)(2,1)}, bf16[128,2048]{1,0:T(8,128)(2,1)S(1)}, u32[]{:S(2)}) copy-start(bf16[128,2048]{1,0:T(8,128)(2,1)S(1)} %collective-permute-done.6.refs_1_) | copy-start | bytes 1572868
  18.1 28.3 %collective-permute-start.15 = (bf16[128,2048]{1,0:T(8,128)(2,1)S(1)}, bf16[128,2048]{1,0:T(8,128)(2,1)}, u32[]{:S(2)}, u32[]{:S(2)}) collective-permute-start(bf16[128,2048]{1,0:T(8,128)(2,1)S(1)} %collective-permute-done.4.refs_2_), channel_id=1, source_target_pairs={{8,16},{16,8},{9,17},{17,9},{10,18},{18,10},{11,19},{19,11},{12,20... | collective-permute-start | bytes 1572872 | tf_op jit(solution)/shard_map/ppermute | solution.py:372
  27.5 18.9 %collective-permute-start.7 = (bf16[128,2048]{1,0:T(8,128)(2,1)S(1)}, bf16[128,2048]{1,0:T(8,128)(2,1)}, u32[]{:S(2)}, u32[]{:S(2)}) collective-permute-start(bf16[128,2048]{1,0:T(8,128)(2,1)S(1)} %collective-permute-done.4.refs_2_), channel_id=1, source_target_pairs={{0,1},{1,0},{2,3},{3,2},{4,5},{5,4},{6,7},{7,6},{8,9},{9,8},{10,11... | collective-permute-start | bytes 1572872 | tf_op jit(solution)/shard_map/ppermute | solution.py:343
  33.1 19.7 %collective-permute-start.5 = (bf16[128,2048]{1,0:T(8,128)(2,1)}, bf16[128,2048]{1,0:T(8,128)(2,1)}, u32[]{:S(2)}, u32[]{:S(2)}) collective-permute-start(bf16[128,2048]{1,0:T(8,128)(2,1)} %collective-permute-done.3), channel_id=1, source_target_pairs={{8,0},{16,24},{9,1},{17,25},{10,2},{18,26},{11,3},{19,27},{12,4},{... | collective-permute-start | bytes 1572872 | tf_op jit(solution)/shard_map/ppermute | solution.py:373
  35.0 19.0 %copy-start.11 = (s32[4]{0:T(128)S(1)}, s32[4]{0:T(128)}, u32[]{:S(2)}) copy-start(s32[4]{0:T(128)} %constant.56.clone) | copy-start | bytes 52
  35.0 18.9 %collective-permute-start.2 = (s32[128]{0:T(128)S(1)}, s32[128]{0:T(128)S(1)}, u32[]{:S(2)}, u32[]{:S(2)}) collective-permute-start(s32[128]{0:T(128)S(1)} %copy-done.4), channel_id=1, source_target_pairs={{0,16},{8,24},{16,0},{24,8},{1,17},{9,25},{17,1},{25,9},{2,18},{10... | collective-permute-start | bytes 1544 | tf_op jit(solution)/shard_map/ppermute | solution.py:313
  44.8 16.7 %collective-permute-start.9 = (bf16[528,768]{1,0:T(8,128)(2,1)S(1)}, bf16[528,768]{1,0:T(8,128)(2,1)S(1)}, u32[]{:S(2)}, u32[]{:S(2)}) collective-permute-start(bf16[528,768]{1,0:T(8,128)(2,1)S(1)} %shard_map.101.refs_0_.refs_8_), channel_id=1, source_target_pairs={{0,4},{2,6},{4,0},{6,2},{1,5},{3,7},{5,1},{7,3},{8,12},{10,14},{12... | collective-permute-start | bytes 2433032 | tf_op jit(solution)/shard_map/ppermute | solution.py:313
  46.4 18.8 %collective-permute-start.16 = (bf16[128,2048]{1,0:T(8,128)(2,1)}, bf16[128,2048]{1,0:T(8,128)(2,1)}, u32[]{:S(2)}, u32[]{:S(2)}) collective-permute-start(bf16[128,2048]{1,0:T(8,128)(2,1)} %collective-permute-done.15), channel_id=1, source_target_pairs={{8,0},{16,24},{9,1},{17,25},{10,2},{18,26},{11,3},{19,27},{12,4},{... | collective-permute-start | bytes 1572872 | tf_op jit(solution)/shard_map/ppermute | solution.py:380
  53.9 9.8 %collective-permute-start.8 = (bf16[128,2048]{1,0:T(8,128)(2,1)S(1)}, bf16[128,2048]{1,0:T(8,128)(2,1)}, u32[]{:S(2)}, u32[]{:S(2)}) collective-permute-start(bf16[128,2048]{1,0:T(8,128)(2,1)S(1)} %broadcast_select_fusion.1.refs_4_), channel_id=1, source_target_pairs={{0,1},{1,0},{2,3},{3,2},{4,5},{5,4},{6,7},{7,6},{8,9},{9,8},{10,11... | collective-permute-start | bytes 1572872 | tf_op jit(solution)/shard_map/ppermute | solution.py:343
  54.6 26.1 %copy-start.7 = (bf16[128,2048]{1,0:T(8,128)(2,1)S(1)}, bf16[128,2048]{1,0:T(8,128)(2,1)}, u32[]{:S(2)}) copy-start(bf16[128,2048]{1,0:T(8,128)(2,1)} %refs_0_.1) | copy-start | bytes 1572868
  54.6 26.1 %copy-start.9 = (bf16[128,2048]{1,0:T(8,128)(2,1)S(1)}, bf16[128,2048]{1,0:T(8,128)(2,1)}, u32[]{:S(2)}) copy-start(bf16[128,2048]{1,0:T(8,128)(2,1)} %copy-done.8) | copy-start | bytes 1572868
  54.6 24.5 %collective-permute-start.11 = (bf16[528,768]{1,0:T(8,128)(2,1)S(1)}, bf16[528,768]{1,0:T(8,128)(2,1)S(1)}, u32[]{:S(2)}, u32[]{:S(2)}) collective-permute-start(bf16[528,768]{1,0:T(8,128)(2,1)S(1)} %shard_map.101.refs_0_.refs_8_), channel_id=1, source_target_pairs={{0,2},{2,0},{4,6},{6,4},{1,3},{3,1},{5,7},{7,5},{8,10},{10,8},{12,... | collective-permute-start | bytes 2433032 | tf_op jit(solution)/shard_map/ppermute | solution.py:313
  61.5 15.8 %collective-permute-start.18 = (bf16[256,768]{1,0:T(8,128)(2,1)S(1)}, bf16[256,768]{1,0:T(8,128)(2,1)S(1)}, u32[]{:S(2)}, u32[]{:S(2)}) collective-permute-start(bf16[256,768]{1,0:T(8,128)(2,1)S(1)} %get-tuple-element.65), channel_id=1, source_target_pairs={{0,16},{8,24},{16,0},{24,8},{1,17},{9,25},{17,1},{25,9},{2,18},{10... | collective-permute-start | bytes 1179656 | tf_op jit(solution)/shard_map/ppermute | solution.py:313
  61.8 19.0 %collective-permute-start.13 = (bf16[528,768]{1,0:T(8,128)(2,1)S(1)}, bf16[528,768]{1,0:T(8,128)(2,1)S(1)}, u32[]{:S(2)}, u32[]{:S(2)}) collective-permute-start(bf16[528,768]{1,0:T(8,128)(2,1)S(1)} %collective-permute-done.9.refs_2_.refs_10_), channel_id=1, source_target_pairs={{0,2},{2,0},{4,6},{6,4},{1,3},{3,1},{5,7},{7,5},{8,10},{10,8},{12,... | collective-permute-start | bytes 2433032 | tf_op jit(solution)/shard_map/ppermute | solution.py:313
  63.7 10.1 %collective-permute-start.10 = (bf16[272,768]{1,0:T(8,128)(2,1)S(1)}, bf16[272,768]{1,0:T(8,128)(2,1)S(1)}, u32[]{:S(2)}, u32[]{:S(2)}) collective-permute-start(bf16[272,768]{1,0:T(8,128)(2,1)S(1)} %shard_map.102.refs_1_.refs_9_), channel_id=1, source_target_pairs={{0,4},{2,6},{4,0},{6,2},{1,5},{3,7},{5,1},{7,3},{8,12},{10,14},{12... | collective-permute-start | bytes 1253384 | tf_op jit(solution)/shard_map/ppermute | solution.py:313
  66.3 12.2 %collective-permute-start.17 = (bf16[128,2048]{1,0:T(8,128)(2,1)S(1)}, bf16[128,2048]{1,0:T(8,128)(2,1)S(1)}, u32[]{:S(2)}, u32[]{:S(2)}) collective-permute-start(bf16[128,2048]{1,0:T(8,128)(2,1)S(1)} %broadcast_select_fusion.refs_6_), channel_id=1, source_target_pairs={{0,1},{1,0},{2,3},{3,2},{4,5},{5,4},{6,7},{7,6},{8,9},{9,8},{10,11... | collective-permute-start | bytes 1572872 | tf_op jit(solution)/shard_map/ppermute | solution.py:343
  73.9 5.5 %collective-permute-start.12 = (bf16[272,768]{1,0:T(8,128)(2,1)S(1)}, bf16[272,768]{1,0:T(8,128)(2,1)S(1)}, u32[]{:S(2)}, u32[]{:S(2)}) collective-permute-start(bf16[272,768]{1,0:T(8,128)(2,1)S(1)} %shard_map.102.refs_1_.refs_9_), channel_id=1, source_target_pairs={{0,2},{2,0},{4,6},{6,4},{1,3},{3,1},{5,7},{7,5},{8,10},{10,8},{12,... | collective-permute-start | bytes 1253384 | tf_op jit(solution)/shard_map/ppermute | solution.py:313
  77.3 3.4 %collective-permute-start.14 = (bf16[272,768]{1,0:T(8,128)(2,1)S(1)}, bf16[272,768]{1,0:T(8,128)(2,1)S(1)}, u32[]{:S(2)}, u32[]{:S(2)}) collective-permute-start(bf16[272,768]{1,0:T(8,128)(2,1)S(1)} %collective-permute-done.10.refs_3_.refs_11_), channel_id=1, source_target_pairs={{0,2},{2,0},{4,6},{6,4},{1,3},{3,1},{5,7},{7,5},{8,10},{10,8},{12,... | collective-permute-start | bytes 1253384 | tf_op jit(solution)/shard_map/ppermute | solution.py:313
  78.6 10.2 %collective-permute-start.21 = (bf16[256,256]{1,0:T(8,128)(2,1)S(1)}, bf16[256,256]{1,0:T(8,128)(2,1)S(1)}, u32[]{:S(2)}, u32[]{:S(2)}) collective-permute-start(bf16[256,256]{1,0:T(8,128)(2,1)S(1)} %get-tuple-element.68.refs_0_), channel_id=1, source_target_pairs={{0,4},{2,6},{4,0},{6,2},{1,5},{3,7},{5,1},{7,3},{8,12},{10,14},{12... | collective-permute-start | bytes 393224 | tf_op jit(solution)/shard_map/ppermute | solution.py:313
  79.2 10.2 %collective-permute-start.22 = (bf16[256,256]{1,0:T(8,128)(2,1)S(1)}, bf16[256,256]{1,0:T(8,128)(2,1)S(1)}, u32[]{:S(2)}, u32[]{:S(2)}) collective-permute-start(bf16[256,256]{1,0:T(8,128)(2,1)S(1)} %get-tuple-element.68.refs_0_), channel_id=1, source_target_pairs={{0,2},{2,0},{4,6},{6,4},{1,3},{3,1},{5,7},{7,5},{8,10},{10,8},{12,... | collective-permute-start | bytes 393224 | tf_op jit(solution)/shard_map/ppermute | solution.py:313
  79.3 5.7 %copy-start.5 = (s32[13]{0:T(128)S(1)}, s32[13]{0:T(128)}, u32[]{:S(2)}) copy-start(s32[13]{0:T(128)} %doc_starts.1) | copy-start | bytes 160
  79.3 5.7 %copy-start.6 = (f32[1,128]{1,0:T(1,128)S(1)}, f32[1,128]{1,0:T(1,128)}, u32[]{:S(2)}) copy-start(f32[1,128]{1,0:T(1,128)} %constant.58.clone.freqs) | copy-start | bytes 1540
  79.3 11.4 %collective-permute-start.19 = (bf16[256,512]{1,0:T(8,128)(2,1)S(1)}, bf16[256,512]{1,0:T(8,128)(2,1)S(1)}, u32[]{:S(2)}, u32[]{:S(2)}) collective-permute-start(bf16[256,512]{1,0:T(8,128)(2,1)S(1)} %get-tuple-element.67.refs_0_), channel_id=1, source_target_pairs={{0,4},{2,6},{4,0},{6,2},{1,5},{3,7},{5,1},{7,3},{8,12},{10,14},{12... | collective-permute-start | bytes 786440 | tf_op jit(solution)/shard_map/ppermute | solution.py:313
  85.1 2.7 %copy-start.12 = (f32[128]{0:T(128)S(1)}, f32[128]{0:T(128)}, u32[]{:S(2)}) copy-start(f32[128]{0:T(128)} %constant.64) | copy-start | bytes 1540
  88.8 1.4 %collective-permute-start.23 = (bf16[256,256]{1,0:T(8,128)(2,1)S(1)}, bf16[256,256]{1,0:T(8,128)(2,1)S(1)}, u32[]{:S(2)}, u32[]{:S(2)}) collective-permute-start(bf16[256,256]{1,0:T(8,128)(2,1)S(1)} %collective-permute-done.21.refs_1_), channel_id=1, source_target_pairs={{0,2},{2,0},{4,6},{6,4},{1,3},{3,1},{5,7},{7,5},{8,10},{10,8},{12,... | collective-permute-start | bytes 393224 | tf_op jit(solution)/shard_map/ppermute | solution.py:313
  89.0 2.6 %collective-permute-start.20 = (bf16[256,512]{1,0:T(8,128)(2,1)S(1)}, bf16[256,512]{1,0:T(8,128)(2,1)S(1)}, u32[]{:S(2)}, u32[]{:S(2)}) collective-permute-start(bf16[256,512]{1,0:T(8,128)(2,1)S(1)} %get-tuple-element.67.refs_0_), channel_id=1, source_target_pairs={{0,2},{2,0},{4,6},{6,4},{1,3},{3,1},{5,7},{7,5},{8,10},{10,8},{12,... | collective-permute-start | bytes 786440 | tf_op jit(solution)/shard_map/ppermute | solution.py:313
  90.7 1.6 %collective-permute-start.24 = (bf16[256,512]{1,0:T(8,128)(2,1)S(1)}, bf16[256,512]{1,0:T(8,128)(2,1)S(1)}, u32[]{:S(2)}, u32[]{:S(2)}) collective-permute-start(bf16[256,512]{1,0:T(8,128)(2,1)S(1)} %collective-permute-done.19.refs_1_), channel_id=1, source_target_pairs={{0,2},{2,0},{4,6},{6,4},{1,3},{3,1},{5,7},{7,5},{8,10},{10,8},{12,... | collective-permute-start | bytes 786440 | tf_op jit(solution)/shard_map/ppermute | solution.py:313
  90.9 8.5 %collective-permute-start.28 = (bf16[512,256]{1,0:T(8,128)(2,1)S(1)}, bf16[512,256]{1,0:T(8,128)(2,1)S(1)}, u32[]{:S(2)}, u32[]{:S(2)}) collective-permute-start(bf16[512,256]{1,0:T(8,128)(2,1)S(1)} %shard_map.106.refs_4_), channel_id=1, source_target_pairs={{0,4},{2,6},{4,0},{6,2},{1,5},{3,7},{5,1},{7,3},{8,12},{10,14},{12... | collective-permute-start | bytes 786440 | tf_op jit(solution)/shard_map/ppermute | solution.py:313
  93.7 5.8 %collective-permute-start.25 = (bf16[256,256]{1,0:T(8,128)(2,1)S(1)}, bf16[256,256]{1,0:T(8,128)(2,1)S(1)}, u32[]{:S(2)}, u32[]{:S(2)}) collective-permute-start(bf16[256,256]{1,0:T(8,128)(2,1)S(1)} %get-tuple-element.74), channel_id=1, source_target_pairs={{0,2},{2,0},{4,6},{6,4},{1,3},{3,1},{5,7},{7,5},{8,10},{10,8},{12,... | collective-permute-start | bytes 393224 | tf_op jit(solution)/shard_map/ppermute | solution.py:313
  99.5 8.8 %collective-permute-start.30 = (bf16[512,256]{1,0:T(8,128)(2,1)S(1)}, bf16[512,256]{1,0:T(8,128)(2,1)S(1)}, u32[]{:S(2)}, u32[]{:S(2)}) collective-permute-start(bf16[512,256]{1,0:T(8,128)(2,1)S(1)} %collective-permute-done.28.refs_5_), channel_id=1, source_target_pairs={{0,2},{2,0},{4,6},{6,4},{1,3},{3,1},{5,7},{7,5},{8,10},{10,8},{12,... | collective-permute-start | bytes 786440 | tf_op jit(solution)/shard_map/ppermute | solution.py:313
  99.5 8.8 %collective-permute-start.29 = (bf16[512,256]{1,0:T(8,128)(2,1)S(1)}, bf16[512,256]{1,0:T(8,128)(2,1)S(1)}, u32[]{:S(2)}, u32[]{:S(2)}) collective-permute-start(bf16[512,256]{1,0:T(8,128)(2,1)S(1)} %shard_map.106.refs_4_), channel_id=1, source_target_pairs={{0,2},{2,0},{4,6},{6,4},{1,3},{3,1},{5,7},{7,5},{8,10},{10,8},{12,... | collective-permute-start | bytes 786440 | tf_op jit(solution)/shard_map/ppermute | solution.py:313
  100.0 1.9 %collective-permute-start.34 = (bf16[256,256]{1,0:T(8,128)(2,1)S(1)}, bf16[256,256]{1,0:T(8,128)(2,1)S(1)}, u32[]{:S(2)}, u32[]{:S(2)}) collective-permute-start(bf16[256,256]{1,0:T(8,128)(2,1)S(1)} %get-tuple-element.84), channel_id=1, source_target_pairs={{0,2},{2,0},{4,6},{6,4},{1,3},{3,1},{5,7},{7,5},{8,10},{10,8},{12,... | collective-permute-start | bytes 393224 | tf_op jit(solution)/shard_map/ppermute | solution.py:313
  100.0 6.3 %collective-permute-start.35 = (bf16[256,256]{1,0:T(8,128)(2,1)S(1)}, bf16[256,256]{1,0:T(8,128)(2,1)S(1)}, u32[]{:S(2)}, u32[]{:S(2)}) collective-permute-start(bf16[256,256]{1,0:T(8,128)(2,1)S(1)} %get-tuple-element.85), channel_id=1, source_target_pairs={{0,4},{2,6},{4,0},{6,2},{1,5},{3,7},{5,1},{7,3},{8,12},{10,14},{12... | collective-permute-start | bytes 393224 | tf_op jit(solution)/shard_map/ppermute | solution.py:313
  100.7 7.7 %collective-permute-start.36 = (bf16[256,256]{1,0:T(8,128)(2,1)S(1)}, bf16[256,256]{1,0:T(8,128)(2,1)S(1)}, u32[]{:S(2)}, u32[]{:S(2)}) collective-permute-start(bf16[256,256]{1,0:T(8,128)(2,1)S(1)} %get-tuple-element.86), channel_id=1, source_target_pairs={{0,6},{2,4},{4,2},{6,0},{1,7},{3,5},{5,3},{7,1},{8,14},{10,12},{12... | collective-permute-start | bytes 393224 | tf_op jit(solution)/shard_map/ppermute | solution.py:313
  101.9 14.9 %collective-permute-start.26 = (bf16[256,256]{1,0:T(8,128)(2,1)S(1)}, bf16[256,256]{1,0:T(8,128)(2,1)S(1)}, u32[]{:S(2)}, u32[]{:S(2)}) collective-permute-start(bf16[256,256]{1,0:T(8,128)(2,1)S(1)} %get-tuple-element.75), channel_id=1, source_target_pairs={{0,4},{2,6},{4,0},{6,2},{1,5},{3,7},{5,1},{7,3},{8,12},{10,14},{12... | collective-permute-start | bytes 393224 | tf_op jit(solution)/shard_map/ppermute | solution.py:313
  106.3 10.5 %collective-permute-start.27 = (bf16[256,256]{1,0:T(8,128)(2,1)S(1)}, bf16[256,256]{1,0:T(8,128)(2,1)S(1)}, u32[]{:S(2)}, u32[]{:S(2)}) collective-permute-start(bf16[256,256]{1,0:T(8,128)(2,1)S(1)} %get-tuple-element.76), channel_id=1, source_target_pairs={{0,6},{2,4},{4,2},{6,0},{1,7},{3,5},{5,3},{7,1},{8,14},{10,12},{12... | collective-permute-start | bytes 393224 | tf_op jit(solution)/shard_map/ppermute | solution.py:313
  112.3 11.0 %collective-permute-start.37 = (bf16[128,256]{1,0:T(8,128)(2,1)S(1)}, bf16[128,256]{1,0:T(8,128)(2,1)S(1)}, u32[]{:S(2)}, u32[]{:S(2)}) collective-permute-start(bf16[128,256]{1,0:T(8,128)(2,1)S(1)} %get-tuple-element.88), channel_id=1, source_target_pairs={{0,8},{8,0},{16,24},{24,16},{1,9},{9,1},{17,25},{25,17},{2,10},{10... | collective-permute-start | bytes 196616 | tf_op jit(solution)/shard_map/ppermute | solution.py:313
  114.2 10.9 %collective-permute-start.38 = (bf16[128,256]{1,0:T(8,128)(2,1)S(1)}, bf16[128,256]{1,0:T(8,128)(2,1)S(1)}, u32[]{:S(2)}, u32[]{:S(2)}) collective-permute-start(bf16[128,256]{1,0:T(8,128)(2,1)S(1)} %get-tuple-element.89), channel_id=1, source_target_pairs={{0,16},{8,24},{16,0},{24,8},{1,17},{9,25},{17,1},{25,9},{2,18},{10... | collective-permute-start | bytes 196616 | tf_op jit(solution)/shard_map/ppermute | solution.py:313
  115.1 9.9 %collective-permute-start.39 = (bf16[128,256]{1,0:T(8,128)(2,1)S(1)}, bf16[128,256]{1,0:T(8,128)(2,1)S(1)}, u32[]{:S(2)}, u32[]{:S(2)}) collective-permute-start(bf16[128,256]{1,0:T(8,128)(2,1)S(1)} %get-tuple-element.90), channel_id=1, source_target_pairs={{0,24},{8,16},{16,8},{24,0},{1,25},{9,17},{17,9},{25,1},{2,26},{10... | collective-permute-start | bytes 196616 | tf_op jit(solution)/shard_map/ppermute | solution.py:313
  120.6 5.0 %collective-permute-start.31 = (bf16[128,256]{1,0:T(8,128)(2,1)S(1)}, bf16[128,256]{1,0:T(8,128)(2,1)S(1)}, u32[]{:S(2)}, u32[]{:S(2)}) collective-permute-start(bf16[128,256]{1,0:T(8,128)(2,1)S(1)} %get-tuple-element.81), channel_id=1, source_target_pairs={{0,8},{8,0},{16,24},{24,16},{1,9},{9,1},{17,25},{25,17},{2,10},{10... | collective-permute-start | bytes 196616 | tf_op jit(solution)/shard_map/ppermute | solution.py:313
  121.5 8.0 %collective-permute-start.32 = (bf16[128,256]{1,0:T(8,128)(2,1)S(1)}, bf16[128,256]{1,0:T(8,128)(2,1)S(1)}, u32[]{:S(2)}, u32[]{:S(2)}) collective-permute-start(bf16[128,256]{1,0:T(8,128)(2,1)S(1)} %get-tuple-element.82), channel_id=1, source_target_pairs={{0,16},{8,24},{16,0},{24,8},{1,17},{9,25},{17,1},{25,9},{2,18},{10... | collective-permute-start | bytes 196616 | tf_op jit(solution)/shard_map/ppermute | solution.py:313
  123.4 6.2 %collective-permute-start.33 = (bf16[128,256]{1,0:T(8,128)(2,1)S(1)}, bf16[128,256]{1,0:T(8,128)(2,1)S(1)}, u32[]{:S(2)}, u32[]{:S(2)}) collective-permute-start(bf16[128,256]{1,0:T(8,128)(2,1)S(1)} %get-tuple-element.83), channel_id=1, source_target_pairs={{0,24},{8,16},{16,8},{24,0},{1,25},{9,17},{17,9},{25,1},{2,26},{10... | collective-permute-start | bytes 196616 | tf_op jit(solution)/shard_map/ppermute | solution.py:313
where the time goes:
time: 131 us
  waiting for transfers between devices  57 us (44%)
  starting transfers between devices  45 us (34%)
  Pallas kernels  20.3 us (15%)
  local copies, waits for them, and re-layouts  4.99 us (4%)
  other arithmetic  3.38 us (3%)
    ppermute x32, waiting for transfers between devices, turn(): return lax.ppermute(value, axis, [(i, i ^ bits) for i in range(count)])  46.6 us
    ppermute x32, starting transfers between devices, turn(): return lax.ppermute(value, axis, [(i, i ^ bits) for i in range(count)])  35.8 us
    pallas_call x12, Pallas kernels, call(): pl.pallas_call(kernel, out_shape=out_shape, in_specs=specs, out_specs=[VM...  20.3 us
    ppermute x4, waiting for transfers between devices, flip(): return lax.ppermute(value, 'tp', [(0, 1), (1, 0)])  5.35 us
    ppermute x1, waiting for transfers between devices, body(): end = lax.ppermute(after(over, near, weights_near), 'line', outer)  5.08 us
    unnamed x26, local copies, waits for them, and re-layouts  3.81 us
    ppermute x4, starting transfers between devices, flip(): return lax.ppermute(value, 'tp', [(0, 1), (1, 0)])  3.67 us
  transfers between devices with their start and end apart: 40, of which 17 were waited for; matrix products, arithmetic and copies ran while one was open for 3% of the time, Pallas kernels for 14%

commit v1 on v0

--- a/solution.py
+++ b/solution.py
@@ -519,7 +519,7 @@
     if split:
         across = turn(kv, "team", 2)
         kvs = [kv, across] + [
-            turn(after(part, arrived[0][1], leaving[-1][0]), "team", 1) for part in (kv, across)
+            turn(after(part, *arrived[-1], leaving[0][0]), "team", 1) for part in (kv, across)
         ]
     else:
         kvs = [lax.all_gather(kv, "team", axis=0, tiled=True)]

time: 131 us -> 130 us (level)
  waiting for transfers between devices: 57 us -> 54.7 us
    ppermute x32, waiting for transfers between devices: 46.6 us -> 44.2 us  [turn(): return lax.ppermute(value, axis, [(i, i ^ bits) for i in range(count)])]
  transfers between devices with their start and end apart: 40 -> 40, of which waited for: 17 -> 17; matrix products, arithmetic and copies ran while one was open for 3% -> 4% of each run, Pallas kernels for 14% -> 15%
where the time goes in v1:
time: 130 us
  waiting for transfers between devices  54.7 us (42%)
  starting transfers between devices  46 us (35%)
  Pallas kernels  20.3 us (16%)
  local copies, waits for them, and re-layouts  4.99 us (4%)
  other arithmetic  3.38 us (3%)
    ppermute x32, waiting for transfers between devices, turn(): return lax.ppermute(value, axis, [(i, i ^ bits) for i in range(count)])  44.2 us
    ppermute x32, starting transfers between devices, turn(): return lax.ppermute(value, axis, [(i, i ^ bits) for i in range(count)])  36.8 us
    pallas_call x12, Pallas kernels, call(): pl.pallas_call(kernel, out_shape=out_shape, in_specs=specs, out_specs=[VM...  20.3 us
    ppermute x4, waiting for transfers between devices, flip(): return lax.ppermute(value, 'tp', [(0, 1), (1, 0)])  5.35 us
    ppermute x1, waiting for transfers between devices, body(): end = lax.ppermute(after(over, near, weights_near), 'line', outer)  5.08 us
    unnamed x26, local copies, waits for them, and re-layouts  3.81 us
    ppermute x4, starting transfers between devices, flip(): return lax.ppermute(value, 'tp', [(0, 1), (1, 0)])  3.67 us
  transfers between devices with their start and end apart: 40, of which 17 were waited for; matrix products, arithmetic and copies ran while one was open for 4% of the time, Pallas kernels for 15%

profile of v1, /device:TPU:0, one launch (start us, length us, event | category | flops | bytes accessed | tf_op | source)
XLA Modules:
  0.0 129.6 jit_solution(10370329191734639385)
XLA Ops:
  0.0 3.0 %collective-permute-start.4 = (bf16[128,2048]{1,0:T(8,128)(2,1)}, bf16[128,2048]{1,0:T(8,128)(2,1)S(1)}, u32[]{:S(2)}, u32[]{:S(2)}) collective-permute-start(bf16[128,2048]{1,0:T(8,128)(2,1)} %refs_0_.1), channel_id=1, source_target_pairs={{0,8},{8,0},{16,24},{24,16},{1,9},{9,1},{17,25},{25,17},{2,10},{10... | collective-permute-start | bytes 1572872 | tf_op jit(solution)/shard_map/ppermute | solution.py:313
  3.0 1.5 %collective-permute-start.3 = (bf16[128,2048]{1,0:T(8,128)(2,1)}, bf16[128,2048]{1,0:T(8,128)(2,1)}, u32[]{:S(2)}, u32[]{:S(2)}) collective-permute-start(bf16[128,2048]{1,0:T(8,128)(2,1)} %refs_0_.1), channel_id=1, source_target_pairs={{8,16},{16,8},{9,17},{17,9},{10,18},{18,10},{11,19},{19,11},{12,20... | collective-permute-start | bytes 1572872 | tf_op jit(solution)/shard_map/ppermute | solution.py:368
  4.5 1.5 %collective-permute-start.6 = (bf16[128,2048]{1,0:T(8,128)(2,1)}, bf16[128,2048]{1,0:T(8,128)(2,1)S(1)}, u32[]{:S(2)}, u32[]{:S(2)}) collective-permute-start(bf16[128,2048]{1,0:T(8,128)(2,1)} %refs_0_.1), channel_id=1, source_target_pairs={{0,1},{1,0},{2,3},{3,2},{4,5},{5,4},{6,7},{7,6},{8,9},{9,8},{10,11... | collective-permute-start | bytes 1572872 | tf_op jit(solution)/shard_map/ppermute | solution.py:343
  6.0 1.2 copy-done
  7.2 0.9 copy-done.1
  8.2 0.9 copy-done.2
  9.2 0.7 copy-done.3
  9.8 0.7 shard_map.100
  10.5 2.5 %collective-permute-start.1 = (bf16[272,768]{1,0:T(8,128)(2,1)S(1)}, bf16[272,768]{1,0:T(8,128)(2,1)S(1)}, u32[]{:S(2)}, u32[]{:S(2)}) collective-permute-start(bf16[272,768]{1,0:T(8,128)(2,1)S(1)} %get-tuple-element.50), channel_id=1, source_target_pairs={{0,24},{8,16},{16,8},{24,0},{1,25},{9,17},{17,9},{25,1},{2,26},{10... | collective-permute-start | bytes 1253384 | tf_op jit(solution)/shard_map/ppermute | solution.py:313
  13.1 1.3 collective-permute-start
  14.3 1.3 %collective-permute-done.4.refs_2_ = bf16[128,2048]{1,0:T(8,128)(2,1)S(1)} collective-permute-done((bf16[128,2048]{1,0:T(8,128)(2,1)}, bf16[128,2048]{1,0:T(8,128)(2,1)S(1)}, u32[]{:S(2)}, u32[]{:S(2)}) %collective-permute-start.4) | collective-permute-done | bytes 524320 | tf_op jit(solution)/shard_map/ppermute | solution.py:313
  15.7 2.4 %collective-permute-done.6.refs_1_ = bf16[128,2048]{1,0:T(8,128)(2,1)S(1)} collective-permute-done((bf16[128,2048]{1,0:T(8,128)(2,1)}, bf16[128,2048]{1,0:T(8,128)(2,1)S(1)}, u32[]{:S(2)}, u32[]{:S(2)}) %collective-permute-start.6) | collective-permute-done | bytes 524320 | tf_op jit(solution)/shard_map/ppermute | solution.py:343
  18.1 1.5 %collective-permute-start.15 = (bf16[128,2048]{1,0:T(8,128)(2,1)S(1)}, bf16[128,2048]{1,0:T(8,128)(2,1)}, u32[]{:S(2)}, u32[]{:S(2)}) collective-permute-start(bf16[128,2048]{1,0:T(8,128)(2,1)S(1)} %collective-permute-done.4.refs_2_), channel_id=1, source_target_pairs={{8,16},{16,8},{9,17},{17,9},{10,18},{18,10},{11,19},{19,11},{12,20... | collective-permute-start | bytes 1572872 | tf_op jit(solution)/shard_map/ppermute | solution.py:372
  19.6 8.0 %collective-permute-done.1.first.refs_0_ = bf16[272,768]{1,0:T(8,128)(2,1)S(1)} collective-permute-done((bf16[272,768]{1,0:T(8,128)(2,1)S(1)}, bf16[272,768]{1,0:T(8,128)(2,1)S(1)}, u32[]{:S(2)}, u32[]{:S(2)}) %collective-permute-start.1) | collective-permute-done | bytes 417824 | tf_op jit(solution)/shard_map/ppermute | solution.py:313
  27.5 1.5 %collective-permute-start.7 = (bf16[128,2048]{1,0:T(8,128)(2,1)S(1)}, bf16[128,2048]{1,0:T(8,128)(2,1)}, u32[]{:S(2)}, u32[]{:S(2)}) collective-permute-start(bf16[128,2048]{1,0:T(8,128)(2,1)S(1)} %collective-permute-done.4.refs_2_), channel_id=1, source_target_pairs={{0,1},{1,0},{2,3},{3,2},{4,5},{5,4},{6,7},{7,6},{8,9},{9,8},{10,11... | collective-permute-start | bytes 1572872 | tf_op jit(solution)/shard_map/ppermute | solution.py:343
  29.0 4.0 %collective-permute-done.refs_1_.refs_2_ = bf16[272,768]{1,0:T(8,128)(2,1)S(1)} collective-permute-done((bf16[272,768]{1,0:T(8,128)(2,1)S(1)}, bf16[272,768]{1,0:T(8,128)(2,1)S(1)}, u32[]{:S(2)}, u32[]{:S(2)}) %collective-permute-start) | collective-permute-done | bytes 417824 | tf_op jit(solution)/shard_map/ppermute | solution.py:313
  33.1 1.3 collective-permute-start.5
  34.4 0.6 gather_fusion
  35.0 9.7 %collective-permute-start.2 = (s32[128]{0:T(128)S(1)}, s32[128]{0:T(128)S(1)}, u32[]{:S(2)}, u32[]{:S(2)}) collective-permute-start(s32[128]{0:T(128)S(1)} %copy-done.4), channel_id=1, source_target_pairs={{0,16},{8,24},{16,0},{24,8},{1,17},{9,25},{17,1},{25,9},{2,18},{10... | collective-permute-start | bytes 1544 | tf_op jit(solution)/shard_map/ppermute | solution.py:313
  44.8 1.6 %collective-permute-start.9 = (bf16[528,768]{1,0:T(8,128)(2,1)S(1)}, bf16[528,768]{1,0:T(8,128)(2,1)S(1)}, u32[]{:S(2)}, u32[]{:S(2)}) collective-permute-start(bf16[528,768]{1,0:T(8,128)(2,1)S(1)} %shard_map.101.refs_0_.refs_8_), channel_id=1, source_target_pairs={{0,4},{2,6},{4,0},{6,2},{1,5},{3,7},{5,1},{7,3},{8,12},{10,14},{12... | collective-permute-start | bytes 2433032 | tf_op jit(solution)/shard_map/ppermute | solution.py:313
  46.4 1.3 collective-permute-start.16
  47.7 5.1 %collective-permute-done.5 = bf16[128,2048]{1,0:T(8,128)(2,1)} collective-permute-done((bf16[128,2048]{1,0:T(8,128)(2,1)}, bf16[128,2048]{1,0:T(8,128)(2,1)}, u32[]{:S(2)}, u32[]{:S(2)}) %collective-permute-start.5) | collective-permute-done | bytes 524320 | tf_op jit(solution)/shard_map/ppermute | solution.py:373
  52.8 1.1 broadcast_select_fusion.1.refs_4_
  54.7 6.8 %collective-permute-done.9.refs_2_.refs_10_ = bf16[528,768]{1,0:T(8,128)(2,1)S(1)} collective-permute-done((bf16[528,768]{1,0:T(8,128)(2,1)S(1)}, bf16[528,768]{1,0:T(8,128)(2,1)S(1)}, u32[]{:S(2)}, u32[]{:S(2)}) %collective-permute-start.9) | collective-permute-done | bytes 811040 | tf_op jit(solution)/shard_map/ppermute | solution.py:313
  61.5 0.3 collective-permute-start.18
  61.8 1.9 %collective-permute-done.8.refs_5_ = bf16[128,2048]{1,0:T(8,128)(2,1)} collective-permute-done((bf16[128,2048]{1,0:T(8,128)(2,1)S(1)}, bf16[128,2048]{1,0:T(8,128)(2,1)}, u32[]{:S(2)}, u32[]{:S(2)}) %collective-permute-start.8) | collective-permute-done | bytes 524320 | tf_op jit(solution)/shard_map/ppermute | solution.py:343
  63.7 1.5 %collective-permute-start.10 = (bf16[272,768]{1,0:T(8,128)(2,1)S(1)}, bf16[272,768]{1,0:T(8,128)(2,1)S(1)}, u32[]{:S(2)}, u32[]{:S(2)}) collective-permute-start(bf16[272,768]{1,0:T(8,128)(2,1)S(1)} %shard_map.102.refs_1_.refs_9_), channel_id=1, source_target_pairs={{0,4},{2,6},{4,0},{6,2},{1,5},{3,7},{5,1},{7,3},{8,12},{10,14},{12... | collective-permute-start | bytes 1253384 | tf_op jit(solution)/shard_map/ppermute | solution.py:313
  65.2 1.1 broadcast_select_fusion.refs_6_
  66.3 0.6 collective-permute-start.17
  66.9 7.0 %collective-permute-done.10.refs_3_.refs_11_ = bf16[272,768]{1,0:T(8,128)(2,1)S(1)} collective-permute-done((bf16[272,768]{1,0:T(8,128)(2,1)S(1)}, bf16[272,768]{1,0:T(8,128)(2,1)S(1)}, u32[]{:S(2)}, u32[]{:S(2)}) %collective-permute-start.10) | collective-permute-done | bytes 417824 | tf_op jit(solution)/shard_map/ppermute | solution.py:313
  73.9 3.5 %collective-permute-done.18.value = bf16[256,768]{1,0:T(8,128)(2,1)S(1)} collective-permute-done((bf16[256,768]{1,0:T(8,128)(2,1)S(1)}, bf16[256,768]{1,0:T(8,128)(2,1)S(1)}, u32[]{:S(2)}, u32[]{:S(2)}) %collective-permute-start.18) | collective-permute-done | bytes 393248 | tf_op jit(solution)/shard_map/ppermute | solution.py:313
  77.5 1.0 collective-permute-done.17.refs_7_
  78.6 0.6 collective-permute-start.21
  79.3 1.4 %collective-permute-start.19 = (bf16[256,512]{1,0:T(8,128)(2,1)S(1)}, bf16[256,512]{1,0:T(8,128)(2,1)S(1)}, u32[]{:S(2)}, u32[]{:S(2)}) collective-permute-start(bf16[256,512]{1,0:T(8,128)(2,1)S(1)} %get-tuple-element.67.refs_0_), channel_id=1, source_target_pairs={{0,4},{2,6},{4,0},{6,2},{1,5},{3,7},{5,1},{7,3},{8,12},{10,14},{12... | collective-permute-start | bytes 786440 | tf_op jit(solution)/shard_map/ppermute | solution.py:313
  80.8 4.3 %shard_map.104 = (f32[512,768]{1,0:T(8,128)S(1)}, bf16[512,1024]{1,0:T(8,128)(2,1)S(1)}) custom-call(s32[4]{0:T(128)S(1)} %pad_add_fusion.places, s32[16]{0:T(128)S(1)} %fusion.table, bf16[128,2048]{1,0:T(8,128)(2,1)S(1)} %copy-done.7, bf16[128,2048]{1,0:T(8,128)(2,1)S(1)} %copy-done.9, bf16[128,2048]{1,0:T(8,128)(2,1)S(1)} %collective-permute-done.4.refs_2_, ...), custom_call_target="tpu_custom_call" | custom-call | flops 3221225472 | bytes 11731024 | tf_op jit(solution)/shard_map/pallas_call | solution.py:39
  85.1 2.7 %shard_map.103 = (f32[512,128]{1,0:T(8,128)S(1)}, bf16[2048,128]{1,0:T(8,128)(2,1)S(1)}, bf16[512,128]{1,0:T(8,128)(2,1)S(1)}, s32[1,512]{1,0:T(1,128)S(1)}, s32[4,128]{1,0:T(4,128)S(1)}) custom-call(s32[4]{0:T(128)S(1)} %broadcast_add_fusion.2.mine, s32[16]{0:T(128)S(1)} %add.56.order, s32[16]{0:T(128)S(1)} %add.60.came, s32[1]{0:T(128)} %bitcast.mate.twist, ...), custom_call_target="tpu_custom_call" | custom-call | flops 1000000000 | bytes 5837516 | tf_op jit(solution)/shard_map/pallas_call | solution.py:39
  87.8 0.9 sine_multiply_fusion
  89.0 0.3 collective-permute-start.20
  89.3 0.8 collective-permute-done.23.refs_3_
  90.2 0.5 shard_map.106.refs_4_
  90.9 0.7 collective-permute-start.28
  91.6 0.7 collective-permute-done.24.refs_3_
  92.3 1.4 %shard_map.108 = (bf16[256,256]{1,0:T(8,128)(2,1)S(1)}, bf16[256,256]{1,0:T(8,128)(2,1)S(1)}, bf16[256,256]{1,0:T(8,128)(2,1)S(1)}, bf16[256,256]{1,0:T(8,128)(2,1)S(1)}) custom-call(f32[512,768]{1,0:T(8,128)S(1)} %get-tuple-element.63.total, bf16[512,1024]{1,0:T(8,128)(2,1)S(1)} %get-tuple-element.64.later, bf16[256,512]{1,0:T(8,128)(2,1)S(1)} %get-tuple-element.67.refs_0_, ...), custom_call_target="tpu_custom_call" | custom-call | flops 536870912 | bytes 4720640 | tf_op jit(solution)/shard_map/pallas_call | solution.py:39
  94.0 0.7 collective-permute-start.30
  94.6 1.0 collective-permute-start.31
  95.6 1.4 %shard_map.107 = (bf16[256,256]{1,0:T(8,128)(2,1)S(1)}, bf16[256,256]{1,0:T(8,128)(2,1)S(1)}, bf16[256,256]{1,0:T(8,128)(2,1)S(1)}, bf16[256,256]{1,0:T(8,128)(2,1)S(1)}) custom-call(f32[512,768]{1,0:T(8,128)S(1)} %get-tuple-element.63.total, bf16[512,1024]{1,0:T(8,128)(2,1)S(1)} %get-tuple-element.64.later, bf16[256,512]{1,0:T(8,128)(2,1)S(1)} %get-tuple-element.67.refs_0_, ...), custom_call_target="tpu_custom_call" | custom-call | flops 536870912 | bytes 4720640 | tf_op jit(solution)/shard_map/pallas_call | solution.py:39
  97.1 3.0 %collective-permute-done.28.refs_5_ = bf16[512,256]{1,0:T(8,128)(2,1)S(1)} collective-permute-done((bf16[512,256]{1,0:T(8,128)(2,1)S(1)}, bf16[512,256]{1,0:T(8,128)(2,1)S(1)}, u32[]{:S(2)}, u32[]{:S(2)}) %collective-permute-start.28) | collective-permute-done | bytes 262176 | tf_op jit(solution)/shard_map/ppermute | solution.py:313
  100.1 2.8 %collective-permute-done.30.refs_2_ = bf16[256,256]{1,0:T(8,128)(2,1)S(1)} collective-permute-done((bf16[256,256]{1,0:T(8,128)(2,1)S(1)}, bf16[256,256]{1,0:T(8,128)(2,1)S(1)}, u32[]{:S(2)}, u32[]{:S(2)}) %collective-permute-start.30) | collective-permute-done | bytes 131104 | tf_op jit(solution)/shard_map/ppermute | solution.py:313
  102.9 1.6 %collective-permute-done.31.refs_3_ = bf16[256,256]{1,0:T(8,128)(2,1)S(1)} collective-permute-done((bf16[256,256]{1,0:T(8,128)(2,1)S(1)}, bf16[256,256]{1,0:T(8,128)(2,1)S(1)}, u32[]{:S(2)}, u32[]{:S(2)}) %collective-permute-start.31) | collective-permute-done | bytes 131104 | tf_op jit(solution)/shard_map/ppermute | solution.py:313
  104.5 0.4 collective-permute-start.33
  105.0 0.4 collective-permute-start.25
  105.4 0.7 collective-permute-start.26
  106.1 0.8 collective-permute-start.27
  106.9 4.0 %shard_map.110 = (bf16[128,256]{1,0:T(8,128)(2,1)S(1)}, bf16[128,256]{1,0:T(8,128)(2,1)S(1)}, bf16[128,256]{1,0:T(8,128)(2,1)S(1)}, bf16[128,256]{1,0:T(8,128)(2,1)S(1)}) custom-call(s32[4]{0:T(128)S(1)} %iota_xor_fusion.far, s32[4,128]{1,0:T(4,128)S(1)} %get-tuple-element.56.columns, bf16[512,128]{1,0:T(8,128)(2,1)S(1)} %get-tuple-element.57.query_bar, ...), custom_call_target="tpu_custom_call" | custom-call | flops 2147483648 | bytes 2492432 | tf_op jit(solution)/shard_map/pallas_call | solution.py:39
  110.9 1.8 %collective-permute-start.37 = (bf16[128,256]{1,0:T(8,128)(2,1)S(1)}, bf16[128,256]{1,0:T(8,128)(2,1)S(1)}, u32[]{:S(2)}, u32[]{:S(2)}) collective-permute-start(bf16[128,256]{1,0:T(8,128)(2,1)S(1)} %get-tuple-element.88), channel_id=1, source_target_pairs={{0,8},{8,0},{16,24},{24,16},{1,9},{9,1},{17,25},{25,17},{2,10},{10... | collective-permute-start | bytes 196616 | tf_op jit(solution)/shard_map/ppermute | solution.py:313
  112.7 0.9 collective-permute-start.38
  113.7 1.7 %collective-permute-start.39 = (bf16[128,256]{1,0:T(8,128)(2,1)S(1)}, bf16[128,256]{1,0:T(8,128)(2,1)S(1)}, u32[]{:S(2)}, u32[]{:S(2)}) collective-permute-start(bf16[128,256]{1,0:T(8,128)(2,1)S(1)} %get-tuple-element.90), channel_id=1, source_target_pairs={{0,24},{8,16},{16,8},{24,0},{1,25},{9,17},{17,9},{25,1},{2,26},{10... | collective-permute-start | bytes 196616 | tf_op jit(solution)/shard_map/ppermute | solution.py:313
  115.4 3.8 %shard_map.109 = (bf16[128,256]{1,0:T(8,128)(2,1)S(1)}, bf16[128,256]{1,0:T(8,128)(2,1)S(1)}, bf16[128,256]{1,0:T(8,128)(2,1)S(1)}, bf16[128,256]{1,0:T(8,128)(2,1)S(1)}) custom-call(s32[4]{0:T(128)S(1)} %iota_xor_fusion.far, s32[4,128]{1,0:T(4,128)S(1)} %get-tuple-element.56.columns, bf16[512,128]{1,0:T(8,128)(2,1)S(1)} %get-tuple-element.57.query_bar, ...), custom_call_target="tpu_custom_call" | custom-call | flops 2147483648 | bytes 2492432 | tf_op jit(solution)/shard_map/pallas_call | solution.py:39
  119.1 0.9 collective-permute-start.34
  120.1 1.8 %collective-permute-start.35 = (bf16[128,256]{1,0:T(8,128)(2,1)S(1)}, bf16[128,256]{1,0:T(8,128)(2,1)S(1)}, u32[]{:S(2)}, u32[]{:S(2)}) collective-permute-start(bf16[128,256]{1,0:T(8,128)(2,1)S(1)} %get-tuple-element.85), channel_id=1, source_target_pairs={{0,16},{8,24},{16,0},{24,8},{1,17},{9,25},{17,1},{25,9},{2,18},{10... | collective-permute-start | bytes 196616 | tf_op jit(solution)/shard_map/ppermute | solution.py:313
  121.9 1.7 %collective-permute-start.36 = (bf16[128,256]{1,0:T(8,128)(2,1)S(1)}, bf16[128,256]{1,0:T(8,128)(2,1)S(1)}, u32[]{:S(2)}, u32[]{:S(2)}) collective-permute-start(bf16[128,256]{1,0:T(8,128)(2,1)S(1)} %get-tuple-element.86), channel_id=1, source_target_pairs={{0,24},{8,16},{16,8},{24,0},{1,25},{9,17},{17,9},{25,1},{2,26},{10... | collective-permute-start | bytes 196616 | tf_op jit(solution)/shard_map/ppermute | solution.py:313
  123.6 0.6 collective-permute-done.34.refs_1_
  124.2 4.1 %collective-permute-done.35.refs_2_ = bf16[128,256]{1,0:T(8,128)(2,1)S(1)} collective-permute-done((bf16[128,256]{1,0:T(8,128)(2,1)S(1)}, bf16[128,256]{1,0:T(8,128)(2,1)S(1)}, u32[]{:S(2)}, u32[]{:S(2)}) %collective-permute-start.35) | collective-permute-done | bytes 65568 | tf_op jit(solution)/shard_map/ppermute | solution.py:313
  128.2 1.4 %shard_map.111 = bf16[128,2048]{1,0:T(8,128)(2,1)} custom-call(s32[4]{0:T(128)S(1)} %iota_xor_fusion.far, bf16[128,256]{1,0:T(8,128)(2,1)S(1)} %get-tuple-element.83.refs_0_, bf16[128,256]{1,0:T(8,128)(2,1)S(1)} %collective-permute-done.34.refs_1_, bf16[128,256]{1,0:T(8,128)(2,1)S(1)} %collective-permute-done.35.refs_2_, ...), custom_call_target="tpu_custom_call" | custom-call | bytes 1048592 | tf_op jit(solution)/shard_map/pallas_call | solution.py:39
  (73 shorter events, 2.1 us)
Async XLA Ops:
  0.0 34.4 %copy-start.10 = (s32[4]{0:T(128)S(1)}, s32[4]{0:T(128)}, u32[]{:S(2)}) copy-start(s32[4]{0:T(128)} %constant.65) | copy-start | bytes 52
  0.0 35.0 %copy-start.4 = (s32[128]{0:T(128)S(1)}, s32[128]{0:T(128)}, u32[]{:S(2)}) copy-start(s32[128]{0:T(128)} %param.12) | copy-start | bytes 1540
  0.0 15.7 %collective-permute-start.4 = (bf16[128,2048]{1,0:T(8,128)(2,1)}, bf16[128,2048]{1,0:T(8,128)(2,1)S(1)}, u32[]{:S(2)}, u32[]{:S(2)}) collective-permute-start(bf16[128,2048]{1,0:T(8,128)(2,1)} %refs_0_.1), channel_id=1, source_target_pairs={{0,8},{8,0},{16,24},{24,16},{1,9},{9,1},{17,25},{25,17},{2,10},{10... | collective-permute-start | bytes 1572872 | tf_op jit(solution)/shard_map/ppermute | solution.py:313
  3.0 12.6 %collective-permute-start.3 = (bf16[128,2048]{1,0:T(8,128)(2,1)}, bf16[128,2048]{1,0:T(8,128)(2,1)}, u32[]{:S(2)}, u32[]{:S(2)}) collective-permute-start(bf16[128,2048]{1,0:T(8,128)(2,1)} %refs_0_.1), channel_id=1, source_target_pairs={{8,16},{16,8},{9,17},{17,9},{10,18},{18,10},{11,19},{19,11},{12,20... | collective-permute-start | bytes 1572872 | tf_op jit(solution)/shard_map/ppermute | solution.py:368
  4.5 13.6 %collective-permute-start.6 = (bf16[128,2048]{1,0:T(8,128)(2,1)}, bf16[128,2048]{1,0:T(8,128)(2,1)S(1)}, u32[]{:S(2)}, u32[]{:S(2)}) collective-permute-start(bf16[128,2048]{1,0:T(8,128)(2,1)} %refs_0_.1), channel_id=1, source_target_pairs={{0,1},{1,0},{2,3},{3,2},{4,5},{5,4},{6,7},{7,6},{8,9},{9,8},{10,11... | collective-permute-start | bytes 1572872 | tf_op jit(solution)/shard_map/ppermute | solution.py:343
  6.0 1.2 copy-start
  7.2 0.9 copy-start.1
  8.2 0.9 copy-start.2
  9.1 0.7 copy-start.3
  10.5 17.0 %collective-permute-start.1 = (bf16[272,768]{1,0:T(8,128)(2,1)S(1)}, bf16[272,768]{1,0:T(8,128)(2,1)S(1)}, u32[]{:S(2)}, u32[]{:S(2)}) collective-permute-start(bf16[272,768]{1,0:T(8,128)(2,1)S(1)} %get-tuple-element.50), channel_id=1, source_target_pairs={{0,24},{8,16},{16,8},{24,0},{1,25},{9,17},{17,9},{25,1},{2,26},{10... | collective-permute-start | bytes 1253384 | tf_op jit(solution)/shard_map/ppermute | solution.py:313
  13.1 20.0 %collective-permute-start = (bf16[272,768]{1,0:T(8,128)(2,1)S(1)}, bf16[272,768]{1,0:T(8,128)(2,1)S(1)}, u32[]{:S(2)}, u32[]{:S(2)}) collective-permute-start(bf16[272,768]{1,0:T(8,128)(2,1)S(1)} %get-tuple-element.49), channel_id=1, source_target_pairs={{0,8},{8,0},{16,24},{24,16},{1,9},{9,1},{17,25},{25,17},{2,10},{10... | collective-permute-start | bytes 1253384 | tf_op jit(solution)/shard_map/ppermute | solution.py:313
  18.1 29.6 %copy-start.8 = (bf16[128,2048]{1,0:T(8,128)(2,1)}, bf16[128,2048]{1,0:T(8,128)(2,1)S(1)}, u32[]{:S(2)}) copy-start(bf16[128,2048]{1,0:T(8,128)(2,1)S(1)} %collective-permute-done.6.refs_1_) | copy-start | bytes 1572868
  18.1 28.3 %collective-permute-start.15 = (bf16[128,2048]{1,0:T(8,128)(2,1)S(1)}, bf16[128,2048]{1,0:T(8,128)(2,1)}, u32[]{:S(2)}, u32[]{:S(2)}) collective-permute-start(bf16[128,2048]{1,0:T(8,128)(2,1)S(1)} %collective-permute-done.4.refs_2_), channel_id=1, source_target_pairs={{8,16},{16,8},{9,17},{17,9},{10,18},{18,10},{11,19},{19,11},{12,20... | collective-permute-start | bytes 1572872 | tf_op jit(solution)/shard_map/ppermute | solution.py:372
  27.5 18.9 %collective-permute-start.7 = (bf16[128,2048]{1,0:T(8,128)(2,1)S(1)}, bf16[128,2048]{1,0:T(8,128)(2,1)}, u32[]{:S(2)}, u32[]{:S(2)}) collective-permute-start(bf16[128,2048]{1,0:T(8,128)(2,1)S(1)} %collective-permute-done.4.refs_2_), channel_id=1, source_target_pairs={{0,1},{1,0},{2,3},{3,2},{4,5},{5,4},{6,7},{7,6},{8,9},{9,8},{10,11... | collective-permute-start | bytes 1572872 | tf_op jit(solution)/shard_map/ppermute | solution.py:343
  33.1 19.7 %collective-permute-start.5 = (bf16[128,2048]{1,0:T(8,128)(2,1)}, bf16[128,2048]{1,0:T(8,128)(2,1)}, u32[]{:S(2)}, u32[]{:S(2)}) collective-permute-start(bf16[128,2048]{1,0:T(8,128)(2,1)} %collective-permute-done.3), channel_id=1, source_target_pairs={{8,0},{16,24},{9,1},{17,25},{10,2},{18,26},{11,3},{19,27},{12,4},{... | collective-permute-start | bytes 1572872 | tf_op jit(solution)/shard_map/ppermute | solution.py:373
  35.0 19.0 %copy-start.11 = (s32[4]{0:T(128)S(1)}, s32[4]{0:T(128)}, u32[]{:S(2)}) copy-start(s32[4]{0:T(128)} %constant.56.clone) | copy-start | bytes 52
  35.0 18.9 %collective-permute-start.2 = (s32[128]{0:T(128)S(1)}, s32[128]{0:T(128)S(1)}, u32[]{:S(2)}, u32[]{:S(2)}) collective-permute-start(s32[128]{0:T(128)S(1)} %copy-done.4), channel_id=1, source_target_pairs={{0,16},{8,24},{16,0},{24,8},{1,17},{9,25},{17,1},{25,9},{2,18},{10... | collective-permute-start | bytes 1544 | tf_op jit(solution)/shard_map/ppermute | solution.py:313
  44.8 16.7 %collective-permute-start.9 = (bf16[528,768]{1,0:T(8,128)(2,1)S(1)}, bf16[528,768]{1,0:T(8,128)(2,1)S(1)}, u32[]{:S(2)}, u32[]{:S(2)}) collective-permute-start(bf16[528,768]{1,0:T(8,128)(2,1)S(1)} %shard_map.101.refs_0_.refs_8_), channel_id=1, source_target_pairs={{0,4},{2,6},{4,0},{6,2},{1,5},{3,7},{5,1},{7,3},{8,12},{10,14},{12... | collective-permute-start | bytes 2433032 | tf_op jit(solution)/shard_map/ppermute | solution.py:313
  46.4 18.8 %collective-permute-start.16 = (bf16[128,2048]{1,0:T(8,128)(2,1)}, bf16[128,2048]{1,0:T(8,128)(2,1)}, u32[]{:S(2)}, u32[]{:S(2)}) collective-permute-start(bf16[128,2048]{1,0:T(8,128)(2,1)} %collective-permute-done.15), channel_id=1, source_target_pairs={{8,0},{16,24},{9,1},{17,25},{10,2},{18,26},{11,3},{19,27},{12,4},{... | collective-permute-start | bytes 1572872 | tf_op jit(solution)/shard_map/ppermute | solution.py:380
  53.9 9.8 %collective-permute-start.8 = (bf16[128,2048]{1,0:T(8,128)(2,1)S(1)}, bf16[128,2048]{1,0:T(8,128)(2,1)}, u32[]{:S(2)}, u32[]{:S(2)}) collective-permute-start(bf16[128,2048]{1,0:T(8,128)(2,1)S(1)} %broadcast_select_fusion.1.refs_4_), channel_id=1, source_target_pairs={{0,1},{1,0},{2,3},{3,2},{4,5},{5,4},{6,7},{7,6},{8,9},{9,8},{10,11... | collective-permute-start | bytes 1572872 | tf_op jit(solution)/shard_map/ppermute | solution.py:343
  54.6 26.1 %copy-start.7 = (bf16[128,2048]{1,0:T(8,128)(2,1)S(1)}, bf16[128,2048]{1,0:T(8,128)(2,1)}, u32[]{:S(2)}) copy-start(bf16[128,2048]{1,0:T(8,128)(2,1)} %refs_0_.1) | copy-start | bytes 1572868
  54.6 26.1 %copy-start.9 = (bf16[128,2048]{1,0:T(8,128)(2,1)S(1)}, bf16[128,2048]{1,0:T(8,128)(2,1)}, u32[]{:S(2)}) copy-start(bf16[128,2048]{1,0:T(8,128)(2,1)} %copy-done.8) | copy-start | bytes 1572868
  54.6 24.5 %collective-permute-start.11 = (bf16[528,768]{1,0:T(8,128)(2,1)S(1)}, bf16[528,768]{1,0:T(8,128)(2,1)S(1)}, u32[]{:S(2)}, u32[]{:S(2)}) collective-permute-start(bf16[528,768]{1,0:T(8,128)(2,1)S(1)} %shard_map.101.refs_0_.refs_8_), channel_id=1, source_target_pairs={{0,2},{2,0},{4,6},{6,4},{1,3},{3,1},{5,7},{7,5},{8,10},{10,8},{12,... | collective-permute-start | bytes 2433032 | tf_op jit(solution)/shard_map/ppermute | solution.py:313
  61.5 15.8 %collective-permute-start.18 = (bf16[256,768]{1,0:T(8,128)(2,1)S(1)}, bf16[256,768]{1,0:T(8,128)(2,1)S(1)}, u32[]{:S(2)}, u32[]{:S(2)}) collective-permute-start(bf16[256,768]{1,0:T(8,128)(2,1)S(1)} %get-tuple-element.65), channel_id=1, source_target_pairs={{0,16},{8,24},{16,0},{24,8},{1,17},{9,25},{17,1},{25,9},{2,18},{10... | collective-permute-start | bytes 1179656 | tf_op jit(solution)/shard_map/ppermute | solution.py:313
  61.8 19.0 %collective-permute-start.13 = (bf16[528,768]{1,0:T(8,128)(2,1)S(1)}, bf16[528,768]{1,0:T(8,128)(2,1)S(1)}, u32[]{:S(2)}, u32[]{:S(2)}) collective-permute-start(bf16[528,768]{1,0:T(8,128)(2,1)S(1)} %collective-permute-done.9.refs_2_.refs_10_), channel_id=1, source_target_pairs={{0,2},{2,0},{4,6},{6,4},{1,3},{3,1},{5,7},{7,5},{8,10},{10,8},{12,... | collective-permute-start | bytes 2433032 | tf_op jit(solution)/shard_map/ppermute | solution.py:313
  63.7 10.1 %collective-permute-start.10 = (bf16[272,768]{1,0:T(8,128)(2,1)S(1)}, bf16[272,768]{1,0:T(8,128)(2,1)S(1)}, u32[]{:S(2)}, u32[]{:S(2)}) collective-permute-start(bf16[272,768]{1,0:T(8,128)(2,1)S(1)} %shard_map.102.refs_1_.refs_9_), channel_id=1, source_target_pairs={{0,4},{2,6},{4,0},{6,2},{1,5},{3,7},{5,1},{7,3},{8,12},{10,14},{12... | collective-permute-start | bytes 1253384 | tf_op jit(solution)/shard_map/ppermute | solution.py:313
  66.3 12.2 %collective-permute-start.17 = (bf16[128,2048]{1,0:T(8,128)(2,1)S(1)}, bf16[128,2048]{1,0:T(8,128)(2,1)S(1)}, u32[]{:S(2)}, u32[]{:S(2)}) collective-permute-start(bf16[128,2048]{1,0:T(8,128)(2,1)S(1)} %broadcast_select_fusion.refs_6_), channel_id=1, source_target_pairs={{0,1},{1,0},{2,3},{3,2},{4,5},{5,4},{6,7},{7,6},{8,9},{9,8},{10,11... | collective-permute-start | bytes 1572872 | tf_op jit(solution)/shard_map/ppermute | solution.py:343
  73.9 5.5 %collective-permute-start.12 = (bf16[272,768]{1,0:T(8,128)(2,1)S(1)}, bf16[272,768]{1,0:T(8,128)(2,1)S(1)}, u32[]{:S(2)}, u32[]{:S(2)}) collective-permute-start(bf16[272,768]{1,0:T(8,128)(2,1)S(1)} %shard_map.102.refs_1_.refs_9_), channel_id=1, source_target_pairs={{0,2},{2,0},{4,6},{6,4},{1,3},{3,1},{5,7},{7,5},{8,10},{10,8},{12,... | collective-permute-start | bytes 1253384 | tf_op jit(solution)/shard_map/ppermute | solution.py:313
  77.3 3.4 %collective-permute-start.14 = (bf16[272,768]{1,0:T(8,128)(2,1)S(1)}, bf16[272,768]{1,0:T(8,128)(2,1)S(1)}, u32[]{:S(2)}, u32[]{:S(2)}) collective-permute-start(bf16[272,768]{1,0:T(8,128)(2,1)S(1)} %collective-permute-done.10.refs_3_.refs_11_), channel_id=1, source_target_pairs={{0,2},{2,0},{4,6},{6,4},{1,3},{3,1},{5,7},{7,5},{8,10},{10,8},{12,... | collective-permute-start | bytes 1253384 | tf_op jit(solution)/shard_map/ppermute | solution.py:313
  78.6 10.2 %collective-permute-start.21 = (bf16[256,256]{1,0:T(8,128)(2,1)S(1)}, bf16[256,256]{1,0:T(8,128)(2,1)S(1)}, u32[]{:S(2)}, u32[]{:S(2)}) collective-permute-start(bf16[256,256]{1,0:T(8,128)(2,1)S(1)} %get-tuple-element.68.refs_0_), channel_id=1, source_target_pairs={{0,4},{2,6},{4,0},{6,2},{1,5},{3,7},{5,1},{7,3},{8,12},{10,14},{12... | collective-permute-start | bytes 393224 | tf_op jit(solution)/shard_map/ppermute | solution.py:313
  79.2 10.2 %collective-permute-start.22 = (bf16[256,256]{1,0:T(8,128)(2,1)S(1)}, bf16[256,256]{1,0:T(8,128)(2,1)S(1)}, u32[]{:S(2)}, u32[]{:S(2)}) collective-permute-start(bf16[256,256]{1,0:T(8,128)(2,1)S(1)} %get-tuple-element.68.refs_0_), channel_id=1, source_target_pairs={{0,2},{2,0},{4,6},{6,4},{1,3},{3,1},{5,7},{7,5},{8,10},{10,8},{12,... | collective-permute-start | bytes 393224 | tf_op jit(solution)/shard_map/ppermute | solution.py:313
  79.3 5.7 %copy-start.5 = (s32[13]{0:T(128)S(1)}, s32[13]{0:T(128)}, u32[]{:S(2)}) copy-start(s32[13]{0:T(128)} %doc_starts.1) | copy-start | bytes 160
  79.3 5.7 %copy-start.6 = (f32[1,128]{1,0:T(1,128)S(1)}, f32[1,128]{1,0:T(1,128)}, u32[]{:S(2)}) copy-start(f32[1,128]{1,0:T(1,128)} %constant.58.clone.freqs) | copy-start | bytes 1540
  79.3 11.4 %collective-permute-start.19 = (bf16[256,512]{1,0:T(8,128)(2,1)S(1)}, bf16[256,512]{1,0:T(8,128)(2,1)S(1)}, u32[]{:S(2)}, u32[]{:S(2)}) collective-permute-start(bf16[256,512]{1,0:T(8,128)(2,1)S(1)} %get-tuple-element.67.refs_0_), channel_id=1, source_target_pairs={{0,4},{2,6},{4,0},{6,2},{1,5},{3,7},{5,1},{7,3},{8,12},{10,14},{12... | collective-permute-start | bytes 786440 | tf_op jit(solution)/shard_map/ppermute | solution.py:313
  85.1 2.7 %copy-start.12 = (f32[128]{0:T(128)S(1)}, f32[128]{0:T(128)}, u32[]{:S(2)}) copy-start(f32[128]{0:T(128)} %constant.64) | copy-start | bytes 1540
  88.8 1.4 %collective-permute-start.23 = (bf16[256,256]{1,0:T(8,128)(2,1)S(1)}, bf16[256,256]{1,0:T(8,128)(2,1)S(1)}, u32[]{:S(2)}, u32[]{:S(2)}) collective-permute-start(bf16[256,256]{1,0:T(8,128)(2,1)S(1)} %collective-permute-done.21.refs_1_), channel_id=1, source_target_pairs={{0,2},{2,0},{4,6},{6,4},{1,3},{3,1},{5,7},{7,5},{8,10},{10,8},{12,... | collective-permute-start | bytes 393224 | tf_op jit(solution)/shard_map/ppermute | solution.py:313
  89.0 2.6 %collective-permute-start.20 = (bf16[256,512]{1,0:T(8,128)(2,1)S(1)}, bf16[256,512]{1,0:T(8,128)(2,1)S(1)}, u32[]{:S(2)}, u32[]{:S(2)}) collective-permute-start(bf16[256,512]{1,0:T(8,128)(2,1)S(1)} %get-tuple-element.67.refs_0_), channel_id=1, source_target_pairs={{0,2},{2,0},{4,6},{6,4},{1,3},{3,1},{5,7},{7,5},{8,10},{10,8},{12,... | collective-permute-start | bytes 786440 | tf_op jit(solution)/shard_map/ppermute | solution.py:313
  90.7 1.6 %collective-permute-start.24 = (bf16[256,512]{1,0:T(8,128)(2,1)S(1)}, bf16[256,512]{1,0:T(8,128)(2,1)S(1)}, u32[]{:S(2)}, u32[]{:S(2)}) collective-permute-start(bf16[256,512]{1,0:T(8,128)(2,1)S(1)} %collective-permute-done.19.refs_1_), channel_id=1, source_target_pairs={{0,2},{2,0},{4,6},{6,4},{1,3},{3,1},{5,7},{7,5},{8,10},{10,8},{12,... | collective-permute-start | bytes 786440 | tf_op jit(solution)/shard_map/ppermute | solution.py:313
  90.9 9.1 %collective-permute-start.28 = (bf16[512,256]{1,0:T(8,128)(2,1)S(1)}, bf16[512,256]{1,0:T(8,128)(2,1)S(1)}, u32[]{:S(2)}, u32[]{:S(2)}) collective-permute-start(bf16[512,256]{1,0:T(8,128)(2,1)S(1)} %shard_map.106.refs_4_), channel_id=1, source_target_pairs={{0,4},{2,6},{4,0},{6,2},{1,5},{3,7},{5,1},{7,3},{8,12},{10,14},{12... | collective-permute-start | bytes 786440 | tf_op jit(solution)/shard_map/ppermute | solution.py:313
  93.7 6.4 %collective-permute-start.29 = (bf16[256,256]{1,0:T(8,128)(2,1)S(1)}, bf16[256,256]{1,0:T(8,128)(2,1)S(1)}, u32[]{:S(2)}, u32[]{:S(2)}) collective-permute-start(bf16[256,256]{1,0:T(8,128)(2,1)S(1)} %get-tuple-element.78), channel_id=1, source_target_pairs={{0,2},{2,0},{4,6},{6,4},{1,3},{3,1},{5,7},{7,5},{8,10},{10,8},{12,... | collective-permute-start | bytes 393224 | tf_op jit(solution)/shard_map/ppermute | solution.py:313
  94.0 8.9 %collective-permute-start.30 = (bf16[256,256]{1,0:T(8,128)(2,1)S(1)}, bf16[256,256]{1,0:T(8,128)(2,1)S(1)}, u32[]{:S(2)}, u32[]{:S(2)}) collective-permute-start(bf16[256,256]{1,0:T(8,128)(2,1)S(1)} %get-tuple-element.79), channel_id=1, source_target_pairs={{0,4},{2,6},{4,0},{6,2},{1,5},{3,7},{5,1},{7,3},{8,12},{10,14},{12... | collective-permute-start | bytes 393224 | tf_op jit(solution)/shard_map/ppermute | solution.py:313
  94.6 9.9 %collective-permute-start.31 = (bf16[256,256]{1,0:T(8,128)(2,1)S(1)}, bf16[256,256]{1,0:T(8,128)(2,1)S(1)}, u32[]{:S(2)}, u32[]{:S(2)}) collective-permute-start(bf16[256,256]{1,0:T(8,128)(2,1)S(1)} %get-tuple-element.80), channel_id=1, source_target_pairs={{0,6},{2,4},{4,2},{6,0},{1,7},{3,5},{5,3},{7,1},{8,14},{10,12},{12... | collective-permute-start | bytes 393224 | tf_op jit(solution)/shard_map/ppermute | solution.py:313
  104.5 2.4 %collective-permute-start.33 = (bf16[512,256]{1,0:T(8,128)(2,1)S(1)}, bf16[512,256]{1,0:T(8,128)(2,1)S(1)}, u32[]{:S(2)}, u32[]{:S(2)}) collective-permute-start(bf16[512,256]{1,0:T(8,128)(2,1)S(1)} %collective-permute-done.28.refs_5_), channel_id=1, source_target_pairs={{0,2},{2,0},{4,6},{6,4},{1,3},{3,1},{5,7},{7,5},{8,10},{10,8},{12,... | collective-permute-start | bytes 786440 | tf_op jit(solution)/shard_map/ppermute | solution.py:313
  104.9 2.0 %collective-permute-start.32 = (bf16[512,256]{1,0:T(8,128)(2,1)S(1)}, bf16[512,256]{1,0:T(8,128)(2,1)S(1)}, u32[]{:S(2)}, u32[]{:S(2)}) collective-permute-start(bf16[512,256]{1,0:T(8,128)(2,1)S(1)} %shard_map.106.refs_4_), channel_id=1, source_target_pairs={{0,2},{2,0},{4,6},{6,4},{1,3},{3,1},{5,7},{7,5},{8,10},{10,8},{12,... | collective-permute-start | bytes 786440 | tf_op jit(solution)/shard_map/ppermute | solution.py:313
  105.0 8.6 %collective-permute-start.25 = (bf16[256,256]{1,0:T(8,128)(2,1)S(1)}, bf16[256,256]{1,0:T(8,128)(2,1)S(1)}, u32[]{:S(2)}, u32[]{:S(2)}) collective-permute-start(bf16[256,256]{1,0:T(8,128)(2,1)S(1)} %get-tuple-element.74), channel_id=1, source_target_pairs={{0,2},{2,0},{4,6},{6,4},{1,3},{3,1},{5,7},{7,5},{8,10},{10,8},{12,... | collective-permute-start | bytes 393224 | tf_op jit(solution)/shard_map/ppermute | solution.py:313
  105.4 9.9 %collective-permute-start.26 = (bf16[256,256]{1,0:T(8,128)(2,1)S(1)}, bf16[256,256]{1,0:T(8,128)(2,1)S(1)}, u32[]{:S(2)}, u32[]{:S(2)}) collective-permute-start(bf16[256,256]{1,0:T(8,128)(2,1)S(1)} %get-tuple-element.75), channel_id=1, source_target_pairs={{0,4},{2,6},{4,0},{6,2},{1,5},{3,7},{5,1},{7,3},{8,12},{10,14},{12... | collective-permute-start | bytes 393224 | tf_op jit(solution)/shard_map/ppermute | solution.py:313
  106.1 9.2 %collective-permute-start.27 = (bf16[256,256]{1,0:T(8,128)(2,1)S(1)}, bf16[256,256]{1,0:T(8,128)(2,1)S(1)}, u32[]{:S(2)}, u32[]{:S(2)}) collective-permute-start(bf16[256,256]{1,0:T(8,128)(2,1)S(1)} %get-tuple-element.76), channel_id=1, source_target_pairs={{0,6},{2,4},{4,2},{6,0},{1,7},{3,5},{5,3},{7,1},{8,14},{10,12},{12... | collective-permute-start | bytes 393224 | tf_op jit(solution)/shard_map/ppermute | solution.py:313
  110.9 11.0 %collective-permute-start.37 = (bf16[128,256]{1,0:T(8,128)(2,1)S(1)}, bf16[128,256]{1,0:T(8,128)(2,1)S(1)}, u32[]{:S(2)}, u32[]{:S(2)}) collective-permute-start(bf16[128,256]{1,0:T(8,128)(2,1)S(1)} %get-tuple-element.88), channel_id=1, source_target_pairs={{0,8},{8,0},{16,24},{24,16},{1,9},{9,1},{17,25},{25,17},{2,10},{10... | collective-permute-start | bytes 196616 | tf_op jit(solution)/shard_map/ppermute | solution.py:313
  112.7 10.9 %collective-permute-start.38 = (bf16[128,256]{1,0:T(8,128)(2,1)S(1)}, bf16[128,256]{1,0:T(8,128)(2,1)S(1)}, u32[]{:S(2)}, u32[]{:S(2)}) collective-permute-start(bf16[128,256]{1,0:T(8,128)(2,1)S(1)} %get-tuple-element.89), channel_id=1, source_target_pairs={{0,16},{8,24},{16,0},{24,8},{1,17},{9,25},{17,1},{25,9},{2,18},{10... | collective-permute-start | bytes 196616 | tf_op jit(solution)/shard_map/ppermute | solution.py:313
  113.7 9.9 %collective-permute-start.39 = (bf16[128,256]{1,0:T(8,128)(2,1)S(1)}, bf16[128,256]{1,0:T(8,128)(2,1)S(1)}, u32[]{:S(2)}, u32[]{:S(2)}) collective-permute-start(bf16[128,256]{1,0:T(8,128)(2,1)S(1)} %get-tuple-element.90), channel_id=1, source_target_pairs={{0,24},{8,16},{16,8},{24,0},{1,25},{9,17},{17,9},{25,1},{2,26},{10... | collective-permute-start | bytes 196616 | tf_op jit(solution)/shard_map/ppermute | solution.py:313
  119.1 5.0 %collective-permute-start.34 = (bf16[128,256]{1,0:T(8,128)(2,1)S(1)}, bf16[128,256]{1,0:T(8,128)(2,1)S(1)}, u32[]{:S(2)}, u32[]{:S(2)}) collective-permute-start(bf16[128,256]{1,0:T(8,128)(2,1)S(1)} %get-tuple-element.84), channel_id=1, source_target_pairs={{0,8},{8,0},{16,24},{24,16},{1,9},{9,1},{17,25},{25,17},{2,10},{10... | collective-permute-start | bytes 196616 | tf_op jit(solution)/shard_map/ppermute | solution.py:313
  120.1 8.1 %collective-permute-start.35 = (bf16[128,256]{1,0:T(8,128)(2,1)S(1)}, bf16[128,256]{1,0:T(8,128)(2,1)S(1)}, u32[]{:S(2)}, u32[]{:S(2)}) collective-permute-start(bf16[128,256]{1,0:T(8,128)(2,1)S(1)} %get-tuple-element.85), channel_id=1, source_target_pairs={{0,16},{8,24},{16,0},{24,8},{1,17},{9,25},{17,1},{25,9},{2,18},{10... | collective-permute-start | bytes 196616 | tf_op jit(solution)/shard_map/ppermute | solution.py:313
  121.9 6.3 %collective-permute-start.36 = (bf16[128,256]{1,0:T(8,128)(2,1)S(1)}, bf16[128,256]{1,0:T(8,128)(2,1)S(1)}, u32[]{:S(2)}, u32[]{:S(2)}) collective-permute-start(bf16[128,256]{1,0:T(8,128)(2,1)S(1)} %get-tuple-element.86), channel_id=1, source_target_pairs={{0,24},{8,16},{16,8},{24,0},{1,25},{9,17},{17,9},{25,1},{2,26},{10... | collective-permute-start | bytes 196616 | tf_op jit(solution)/shard_map/ppermute | solution.py:313

commit v2 on v1

--- a/solution.py
+++ b/solution.py
@@ -207,15 +207,21 @@
         tokens[:, block * width : (block + 1) * width] = loose[:, source]
     if later.shape[1] < tokens.shape[1]:
         later[...] = tokens[:, tokens.shape[1] - later.shape[1] :]
+    total[...] = project(tokens, weights, slice(0, total.shape[1]))
+
+
+def rest_kernel(tokens, *refs):
+    weights, total = refs[:-1], refs[-1]
+    skip = weights[0].shape[1] - total.shape[1]
     for start in range(0, total.shape[1], 2 * HEAD_SIZE):
-        cols = slice(start, start + 2 * HEAD_SIZE)
-        total[:, cols] = project(tokens, weights, cols)
-
-
-def finish_projection(total, later, weights, cols, skip=0):
+        cols = slice(skip + start, skip + start + 2 * HEAD_SIZE)
+        total[:, start : start + 2 * HEAD_SIZE] = project(tokens, weights, cols)
+
+
+def finish_projection(total, later, weights, cols):
     if not weights:
         return total[:, cols]
-    return total[:, cols] + project(later, weights, slice(cols.start - skip, cols.stop - skip))
+    return total[:, cols] + project(later, weights, cols)
 
 
 def kv_kernel(total, later, *refs):
@@ -231,8 +237,7 @@
     weights = refs[:parts]
     cosine, sine, slots = refs[parts : parts + 3]
     outs, queries = refs[parts + 3 : -1], refs[-1]
-    cols = slice(start, start + queries.shape[1])
-    raw = finish_projection(total, later, weights, cols, 2 * HEAD_SIZE)
+    raw = finish_projection(total, later, weights, slice(start, start + queries.shape[1]))
     for head in range(queries.shape[1] // HEAD_SIZE):
         cols = slice(head * HEAD_SIZE, (head + 1) * HEAD_SIZE)
         queries[:, cols] = rotate(raw[:, cols], cosine[...], sine[...]).astype(queries.dtype)
@@ -454,27 +459,31 @@
     sine = jnp.sin(angles) * sign
 
     rest = width // groups if split else width
-    total, later = call(
+    kv_total, later, tokens = call(
         functools.partial(tokens_kernel, (groups, chunks, nctx if split else 1)),
         [
-            jax.ShapeDtypeStruct((total_rows, columns_each), jnp.float32),
+            jax.ShapeDtypeStruct((total_rows, pair), jnp.float32),
             jax.ShapeDtypeStruct((total_rows, rest if split else LANES), jnp.bfloat16),
+            jax.ShapeDtypeStruct((total_rows, width), jnp.bfloat16),
         ],
         [places, table, *pieces, *early],
-        scratch=[
-            pltpu.VMEM((total_rows, width), jnp.bfloat16),
-            pltpu.VMEM((total_rows, width), jnp.bfloat16),
-        ],
+        scratch=[pltpu.VMEM((total_rows, width), jnp.bfloat16)],
         flops=2 * total_rows * width * columns_each,
         smem=(0, 1),
         vmem=32,
     )
-    kv_late = spread(kv_second, total, cosine) if split else []
+    kv_late = spread(kv_second, kv_total, cosine) if split else []
     kv = call(
         kv_kernel,
         jax.ShapeDtypeStruct((total_rows, pair), jnp.bfloat16),
-        [total, later, *kv_late, cosine, sine],
+        [kv_total, later, *kv_late, cosine, sine],
         flops=2 * total_rows * rest * pair,
+    )
+    total = call(
+        rest_kernel,
+        jax.ShapeDtypeStruct((total_rows, parts * pair), jnp.float32),
+        [after(tokens, kv), *early],
+        flops=2 * total_rows * width * parts * pair,
     )
     late = spread(query_second, kv) if split else []
 
@@ -484,7 +493,7 @@
 
     def project_part(part):
         return call(
-            functools.partial(query_kernel, (len(late), (1 + part) * pair)),
+            functools.partial(query_kernel, (len(late), part * pair)),
             [jax.ShapeDtypeStruct((slot_count // lanes_out, pair), jnp.bfloat16)] * lanes_out,
             [total, later, *late, cosine, sine, slots],
             scratch=[pltpu.VMEM((total_rows, pair), jnp.bfloat16)],

time: 130 us -> 131 us (level)
  waiting for transfers between devices: 54.7 us -> 52.9 us
  local copies, waits for them, and re-layouts: 4.99 us -> 6.7 us
    unnamed x26 -> x24, local copies, waits for them, and re-layouts: 3.81 us -> 5.53 us
    ppermute x4, waiting for transfers between devices: 5.35 us -> 3.85 us  [flip(): return lax.ppermute(value, 'tp', [(0, 1), (1, 0)])]
    ppermute x1, waiting for transfers between devices: 5.08 us -> 3.76 us  [body(): end = lax.ppermute(after(over, near, weights_near), 'line', outer)]
    pallas_call x12 -> x13, Pallas kernels: 20.3 us -> 20.8 us  [call(): pl.pallas_call(kernel, out_shape=out_shape, in_specs=specs, out_specs=[VM...]
  transfers between devices with their start and end apart: 40 -> 40, of which waited for: 17 -> 16; matrix products, arithmetic and copies ran while one was open for 4% -> 4% of each run, Pallas kernels for 15% -> 15%
where the time goes in v2:
time: 131 us
  waiting for transfers between devices  52.9 us (40%)
  starting transfers between devices  46.1 us (35%)
  Pallas kernels  20.8 us (16%)
  local copies, waits for them, and re-layouts  6.7 us (5%)
  other arithmetic  4.04 us (3%)
    ppermute x32, waiting for transfers between devices, turn(): return lax.ppermute(value, axis, [(i, i ^ bits) for i in range(count)])  45.2 us
    ppermute x32, starting transfers between devices, turn(): return lax.ppermute(value, axis, [(i, i ^ bits) for i in range(count)])  36.9 us
    pallas_call x13, Pallas kernels, call(): pl.pallas_call(kernel, out_shape=out_shape, in_specs=specs, out_specs=[VM...  20.8 us
    unnamed x24, local copies, waits for them, and re-layouts  5.53 us
    ppermute x4, waiting for transfers between devices, flip(): return lax.ppermute(value, 'tp', [(0, 1), (1, 0)])  3.85 us
    ppermute x1, waiting for transfers between devices, body(): end = lax.ppermute(after(over, near, weights_near), 'line', outer)  3.76 us
    ppermute x4, starting transfers between devices, flip(): return lax.ppermute(value, 'tp', [(0, 1), (1, 0)])  3.67 us
  transfers between devices with their start and end apart: 40, of which 16 were waited for; matrix products, arithmetic and copies ran while one was open for 4% of the time, Pallas kernels for 15%

profile of v2, /device:TPU:0, one launch (start us, length us, event | category | flops | bytes accessed | tf_op | source)
XLA Modules:
  0.0 130.7 jit_solution(12388787813324862204)
XLA Ops:
  0.0 3.0 %collective-permute-start.4 = (bf16[128,2048]{1,0:T(8,128)(2,1)}, bf16[128,2048]{1,0:T(8,128)(2,1)}, u32[]{:S(2)}, u32[]{:S(2)}) collective-permute-start(bf16[128,2048]{1,0:T(8,128)(2,1)} %refs_0_.1), channel_id=1, source_target_pairs={{0,8},{8,0},{16,24},{24,16},{1,9},{9,1},{17,25},{25,17},{2,10},{10... | collective-permute-start | bytes 1572872 | tf_op jit(solution)/shard_map/ppermute | solution.py:318
  3.0 1.5 %collective-permute-start.3 = (bf16[128,2048]{1,0:T(8,128)(2,1)}, bf16[128,2048]{1,0:T(8,128)(2,1)}, u32[]{:S(2)}, u32[]{:S(2)}) collective-permute-start(bf16[128,2048]{1,0:T(8,128)(2,1)} %refs_0_.1), channel_id=1, source_target_pairs={{8,16},{16,8},{9,17},{17,9},{10,18},{18,10},{11,19},{19,11},{12,20... | collective-permute-start | bytes 1572872 | tf_op jit(solution)/shard_map/ppermute | solution.py:373
  4.5 1.5 %collective-permute-start.6 = (bf16[128,2048]{1,0:T(8,128)(2,1)}, bf16[128,2048]{1,0:T(8,128)(2,1)S(1)}, u32[]{:S(2)}, u32[]{:S(2)}) collective-permute-start(bf16[128,2048]{1,0:T(8,128)(2,1)} %refs_0_.1), channel_id=1, source_target_pairs={{0,1},{1,0},{2,3},{3,2},{4,5},{5,4},{6,7},{7,6},{8,9},{9,8},{10,11... | collective-permute-start | bytes 1572872 | tf_op jit(solution)/shard_map/ppermute | solution.py:348
  6.0 1.2 copy-done
  7.2 0.9 copy-done.1
  8.2 0.9 copy-done.2
  9.1 0.7 copy-done.3
  9.8 0.7 shard_map.100
  10.5 2.5 %collective-permute-start.1 = (bf16[272,768]{1,0:T(8,128)(2,1)S(1)}, bf16[272,768]{1,0:T(8,128)(2,1)S(1)}, u32[]{:S(2)}, u32[]{:S(2)}) collective-permute-start(bf16[272,768]{1,0:T(8,128)(2,1)S(1)} %get-tuple-element.52), channel_id=1, source_target_pairs={{0,24},{8,16},{16,8},{24,0},{1,25},{9,17},{17,9},{25,1},{2,26},{10... | collective-permute-start | bytes 1253384 | tf_op jit(solution)/shard_map/ppermute | solution.py:318
  13.0 1.3 collective-permute-start
  14.3 1.4 %collective-permute-done.4.refs_2_ = bf16[128,2048]{1,0:T(8,128)(2,1)} collective-permute-done((bf16[128,2048]{1,0:T(8,128)(2,1)}, bf16[128,2048]{1,0:T(8,128)(2,1)}, u32[]{:S(2)}, u32[]{:S(2)}) %collective-permute-start.4) | collective-permute-done | bytes 524320 | tf_op jit(solution)/shard_map/ppermute | solution.py:318
  15.7 2.4 %collective-permute-done.6.refs_1_ = bf16[128,2048]{1,0:T(8,128)(2,1)S(1)} collective-permute-done((bf16[128,2048]{1,0:T(8,128)(2,1)}, bf16[128,2048]{1,0:T(8,128)(2,1)S(1)}, u32[]{:S(2)}, u32[]{:S(2)}) %collective-permute-start.6) | collective-permute-done | bytes 524320 | tf_op jit(solution)/shard_map/ppermute | solution.py:348
  18.1 1.5 %collective-permute-start.15 = (bf16[128,2048]{1,0:T(8,128)(2,1)}, bf16[128,2048]{1,0:T(8,128)(2,1)}, u32[]{:S(2)}, u32[]{:S(2)}) collective-permute-start(bf16[128,2048]{1,0:T(8,128)(2,1)} %collective-permute-done.4.refs_2_), channel_id=1, source_target_pairs={{8,16},{16,8},{9,17},{17,9},{10,18},{18,10},{11,19},{19,11},{12,20... | collective-permute-start | bytes 1572872 | tf_op jit(solution)/shard_map/ppermute | solution.py:377
  19.6 8.0 %collective-permute-done.1.first.refs_0_ = bf16[272,768]{1,0:T(8,128)(2,1)S(1)} collective-permute-done((bf16[272,768]{1,0:T(8,128)(2,1)S(1)}, bf16[272,768]{1,0:T(8,128)(2,1)S(1)}, u32[]{:S(2)}, u32[]{:S(2)}) %collective-permute-start.1) | collective-permute-done | bytes 417824 | tf_op jit(solution)/shard_map/ppermute | solution.py:318
  27.5 1.5 %collective-permute-start.7 = (bf16[128,2048]{1,0:T(8,128)(2,1)}, bf16[128,2048]{1,0:T(8,128)(2,1)}, u32[]{:S(2)}, u32[]{:S(2)}) collective-permute-start(bf16[128,2048]{1,0:T(8,128)(2,1)} %collective-permute-done.4.refs_2_), channel_id=1, source_target_pairs={{0,1},{1,0},{2,3},{3,2},{4,5},{5,4},{6,7},{7,6},{8,9},{9,8},{10,11... | collective-permute-start | bytes 1572872 | tf_op jit(solution)/shard_map/ppermute | solution.py:348
  29.0 4.0 %collective-permute-done.refs_1_.refs_2_ = bf16[272,768]{1,0:T(8,128)(2,1)S(1)} collective-permute-done((bf16[272,768]{1,0:T(8,128)(2,1)S(1)}, bf16[272,768]{1,0:T(8,128)(2,1)S(1)}, u32[]{:S(2)}, u32[]{:S(2)}) %collective-permute-start) | collective-permute-done | bytes 417824 | tf_op jit(solution)/shard_map/ppermute | solution.py:318
  33.1 1.3 collective-permute-start.5
  34.4 0.7 pad_clamp_fusion
  35.0 0.6 gather_fusion
  35.7 9.8 %collective-permute-start.2 = (s32[128]{0:T(128)}, s32[128]{0:T(128)S(1)}, u32[]{:S(2)}, u32[]{:S(2)}) collective-permute-start(s32[128]{0:T(128)} %param.12), channel_id=1, source_target_pairs={{0,16},{8,24},{16,0},{24,8},{1,17},{9,25},{17,1},{25,9},{2,18},{10... | collective-permute-start | bytes 1544 | tf_op jit(solution)/shard_map/ppermute | solution.py:318
  45.4 0.7 copy-done.4
  46.2 1.6 %collective-permute-start.9 = (bf16[528,768]{1,0:T(8,128)(2,1)S(1)}, bf16[528,768]{1,0:T(8,128)(2,1)S(1)}, u32[]{:S(2)}, u32[]{:S(2)}) collective-permute-start(bf16[528,768]{1,0:T(8,128)(2,1)S(1)} %shard_map.101.refs_0_.refs_8_), channel_id=1, source_target_pairs={{0,4},{2,6},{4,0},{6,2},{1,5},{3,7},{5,1},{7,3},{8,12},{10,14},{12... | collective-permute-start | bytes 2433032 | tf_op jit(solution)/shard_map/ppermute | solution.py:318
  47.7 1.3 collective-permute-start.16
  49.0 3.8 %collective-permute-done.5 = bf16[128,2048]{1,0:T(8,128)(2,1)} collective-permute-done((bf16[128,2048]{1,0:T(8,128)(2,1)}, bf16[128,2048]{1,0:T(8,128)(2,1)}, u32[]{:S(2)}, u32[]{:S(2)}) %collective-permute-start.5) | collective-permute-done | bytes 524320 | tf_op jit(solution)/shard_map/ppermute | solution.py:378
  52.8 1.1 broadcast_select_fusion.1.refs_4_
  54.7 8.1 %collective-permute-done.9.refs_2_.refs_10_ = bf16[528,768]{1,0:T(8,128)(2,1)S(1)} collective-permute-done((bf16[528,768]{1,0:T(8,128)(2,1)S(1)}, bf16[528,768]{1,0:T(8,128)(2,1)S(1)}, u32[]{:S(2)}, u32[]{:S(2)}) %collective-permute-start.9) | collective-permute-done | bytes 811040 | tf_op jit(solution)/shard_map/ppermute | solution.py:318
  63.1 0.6 collective-permute-done.8.refs_5_
  63.7 1.5 %collective-permute-start.10 = (bf16[272,768]{1,0:T(8,128)(2,1)S(1)}, bf16[272,768]{1,0:T(8,128)(2,1)S(1)}, u32[]{:S(2)}, u32[]{:S(2)}) collective-permute-start(bf16[272,768]{1,0:T(8,128)(2,1)S(1)} %shard_map.102.refs_1_.refs_9_), channel_id=1, source_target_pairs={{0,4},{2,6},{4,0},{6,2},{1,5},{3,7},{5,1},{7,3},{8,12},{10,14},{12... | collective-permute-start | bytes 1253384 | tf_op jit(solution)/shard_map/ppermute | solution.py:318
  65.2 1.1 broadcast_select_fusion.refs_6_
  66.3 0.6 collective-permute-start.17
  66.9 8.3 %collective-permute-done.10.refs_3_.refs_11_ = bf16[272,768]{1,0:T(8,128)(2,1)S(1)} collective-permute-done((bf16[272,768]{1,0:T(8,128)(2,1)S(1)}, bf16[272,768]{1,0:T(8,128)(2,1)S(1)}, u32[]{:S(2)}, u32[]{:S(2)}) %collective-permute-start.10) | collective-permute-done | bytes 417824 | tf_op jit(solution)/shard_map/ppermute | solution.py:318
  75.2 3.6 %collective-permute-done.18.value = bf16[256,768]{1,0:T(8,128)(2,1)S(1)} collective-permute-done((bf16[256,768]{1,0:T(8,128)(2,1)S(1)}, bf16[256,768]{1,0:T(8,128)(2,1)S(1)}, u32[]{:S(2)}, u32[]{:S(2)}) %collective-permute-start.18) | collective-permute-done | bytes 393248 | tf_op jit(solution)/shard_map/ppermute | solution.py:318
  79.0 0.9 collective-permute-done.17.refs_7_
  79.9 0.7 collective-permute-start.19
  80.8 1.3 collective-permute-start.22
  82.1 1.0 copy-done.9
  83.1 2.9 %shard_map.104 = (f32[512,256]{1,0:T(8,128)S(1)}, bf16[512,1024]{1,0:T(8,128)(2,1)S(1)}, bf16[512,4096]{1,0:T(8,128)(2,1)S(1)}) custom-call(s32[4]{0:T(128)S(1)} %pad_add_fusion.places, s32[16]{0:T(128)S(1)} %fusion.table, bf16[128,2048]{1,0:T(8,128)(2,1)S(1)} %copy-done.7, bf16[128,2048]{1,0:T(8,128)(2,1)S(1)} %copy-done.9, ...), custom_call_target="tpu_custom_call" | custom-call | flops 3221225472 | bytes 14876752 | tf_op jit(solution)/shard_map/pallas_call | solution.py:39
  86.1 2.7 %shard_map.103 = (f32[512,128]{1,0:T(8,128)S(1)}, bf16[2048,128]{1,0:T(8,128)(2,1)S(1)}, bf16[512,128]{1,0:T(8,128)(2,1)S(1)}, s32[1,512]{1,0:T(1,128)S(1)}, s32[4,128]{1,0:T(4,128)S(1)}) custom-call(s32[4]{0:T(128)S(1)} %broadcast_add_fusion.2.mine, s32[16]{0:T(128)S(1)} %add.56.order, s32[16]{0:T(128)S(1)} %add.60.came, s32[1]{0:T(128)} %bitcast.mate.twist, ...), custom_call_target="tpu_custom_call" | custom-call | flops 1000000000 | bytes 5837516 | tf_op jit(solution)/shard_map/pallas_call | solution.py:39
  88.8 0.9 sine_multiply_fusion
  90.3 0.8 collective-permute-done.21.refs_3_
  91.2 0.5 shard_map.106.refs_4_
  91.9 0.7 collective-permute-start.28
  92.7 1.8 %shard_map.107.total = f32[512,512]{1,0:T(8,128)S(1)} custom-call(bf16[512,4096]{1,0:T(8,128)(2,1)S(1)} %get-tuple-element.73.tokens, bf16[528,768]{1,0:T(8,128)(2,1)S(1)} %shard_map.101.refs_0_.refs_8_, bf16[272,768]{1,0:T(8,128)(2,1)S(1)} %shard_map.102.refs_1_.refs_9_, bf16[528,768]{1,0:T(8,128)(2,1)S(1)} %collective-permute-done.9.refs_2_.refs_10_, ...), custom_call_target="tpu_custom_call" | custom-call | flops 2147483648 | bytes 10158080 | tf_op jit(solution)/shard_map/pallas_call | solution.py:39
  94.5 1.4 %shard_map.109 = (bf16[256,256]{1,0:T(8,128)(2,1)S(1)}, bf16[256,256]{1,0:T(8,128)(2,1)S(1)}, bf16[256,256]{1,0:T(8,128)(2,1)S(1)}, bf16[256,256]{1,0:T(8,128)(2,1)S(1)}) custom-call(f32[512,512]{1,0:T(8,128)S(1)} %shard_map.107.total, bf16[512,1024]{1,0:T(8,128)(2,1)S(1)} %get-tuple-element.67.later, bf16[256,512]{1,0:T(8,128)(2,1)S(1)} %get-tuple-element.74.refs_0_, ...), custom_call_target="tpu_custom_call" | custom-call | flops 536870912 | bytes 4196352 | tf_op jit(solution)/shard_map/pallas_call | solution.py:39
  96.0 1.3 collective-permute-start.30
  97.3 0.5 collective-permute-start.31
  97.8 1.4 %shard_map.108 = (bf16[256,256]{1,0:T(8,128)(2,1)S(1)}, bf16[256,256]{1,0:T(8,128)(2,1)S(1)}, bf16[256,256]{1,0:T(8,128)(2,1)S(1)}, bf16[256,256]{1,0:T(8,128)(2,1)S(1)}) custom-call(f32[512,512]{1,0:T(8,128)S(1)} %shard_map.107.total, bf16[512,1024]{1,0:T(8,128)(2,1)S(1)} %get-tuple-element.67.later, bf16[256,512]{1,0:T(8,128)(2,1)S(1)} %get-tuple-element.74.refs_0_, ...), custom_call_target="tpu_custom_call" | custom-call | flops 536870912 | bytes 4196352 | tf_op jit(solution)/shard_map/pallas_call | solution.py:39
  99.3 1.8 %collective-permute-done.28.refs_5_ = bf16[512,256]{1,0:T(8,128)(2,1)S(1)} collective-permute-done((bf16[512,256]{1,0:T(8,128)(2,1)S(1)}, bf16[512,256]{1,0:T(8,128)(2,1)S(1)}, u32[]{:S(2)}, u32[]{:S(2)}) %collective-permute-start.28) | collective-permute-done | bytes 262176 | tf_op jit(solution)/shard_map/ppermute | solution.py:318
  101.0 2.8 %collective-permute-done.30.refs_2_ = bf16[256,256]{1,0:T(8,128)(2,1)S(1)} collective-permute-done((bf16[256,256]{1,0:T(8,128)(2,1)S(1)}, bf16[256,256]{1,0:T(8,128)(2,1)S(1)}, u32[]{:S(2)}, u32[]{:S(2)}) %collective-permute-start.30) | collective-permute-done | bytes 131104 | tf_op jit(solution)/shard_map/ppermute | solution.py:318
  103.9 1.7 %collective-permute-done.31.refs_3_ = bf16[256,256]{1,0:T(8,128)(2,1)S(1)} collective-permute-done((bf16[256,256]{1,0:T(8,128)(2,1)S(1)}, bf16[256,256]{1,0:T(8,128)(2,1)S(1)}, u32[]{:S(2)}, u32[]{:S(2)}) %collective-permute-start.31) | collective-permute-done | bytes 131104 | tf_op jit(solution)/shard_map/ppermute | solution.py:318
  105.5 0.4 collective-permute-start.33
  106.4 0.7 collective-permute-start.26
  107.2 0.7 collective-permute-start.27
  107.9 4.0 %shard_map.111 = (bf16[128,256]{1,0:T(8,128)(2,1)S(1)}, bf16[128,256]{1,0:T(8,128)(2,1)S(1)}, bf16[128,256]{1,0:T(8,128)(2,1)S(1)}, bf16[128,256]{1,0:T(8,128)(2,1)S(1)}) custom-call(s32[4]{0:T(128)S(1)} %iota_xor_fusion.far, s32[4,128]{1,0:T(4,128)S(1)} %get-tuple-element.58.columns, bf16[512,128]{1,0:T(8,128)(2,1)S(1)} %get-tuple-element.59.query_bar, ...), custom_call_target="tpu_custom_call" | custom-call | flops 2147483648 | bytes 2492432 | tf_op jit(solution)/shard_map/pallas_call | solution.py:39
  111.9 1.9 %collective-permute-start.37 = (bf16[128,256]{1,0:T(8,128)(2,1)S(1)}, bf16[128,256]{1,0:T(8,128)(2,1)S(1)}, u32[]{:S(2)}, u32[]{:S(2)}) collective-permute-start(bf16[128,256]{1,0:T(8,128)(2,1)S(1)} %get-tuple-element.92), channel_id=1, source_target_pairs={{0,8},{8,0},{16,24},{24,16},{1,9},{9,1},{17,25},{25,17},{2,10},{10... | collective-permute-start | bytes 196616 | tf_op jit(solution)/shard_map/ppermute | solution.py:318
  113.8 0.9 collective-permute-start.38
  114.7 1.7 %collective-permute-start.39 = (bf16[128,256]{1,0:T(8,128)(2,1)S(1)}, bf16[128,256]{1,0:T(8,128)(2,1)S(1)}, u32[]{:S(2)}, u32[]{:S(2)}) collective-permute-start(bf16[128,256]{1,0:T(8,128)(2,1)S(1)} %get-tuple-element.94), channel_id=1, source_target_pairs={{0,24},{8,16},{16,8},{24,0},{1,25},{9,17},{17,9},{25,1},{2,26},{10... | collective-permute-start | bytes 196616 | tf_op jit(solution)/shard_map/ppermute | solution.py:318
  116.4 3.8 %shard_map.110 = (bf16[128,256]{1,0:T(8,128)(2,1)S(1)}, bf16[128,256]{1,0:T(8,128)(2,1)S(1)}, bf16[128,256]{1,0:T(8,128)(2,1)S(1)}, bf16[128,256]{1,0:T(8,128)(2,1)S(1)}) custom-call(s32[4]{0:T(128)S(1)} %iota_xor_fusion.far, s32[4,128]{1,0:T(4,128)S(1)} %get-tuple-element.58.columns, bf16[512,128]{1,0:T(8,128)(2,1)S(1)} %get-tuple-element.59.query_bar, ...), custom_call_target="tpu_custom_call" | custom-call | flops 2147483648 | bytes 2492432 | tf_op jit(solution)/shard_map/pallas_call | solution.py:39
  120.2 1.0 collective-permute-start.34
  121.2 1.8 %collective-permute-start.35 = (bf16[128,256]{1,0:T(8,128)(2,1)S(1)}, bf16[128,256]{1,0:T(8,128)(2,1)S(1)}, u32[]{:S(2)}, u32[]{:S(2)}) collective-permute-start(bf16[128,256]{1,0:T(8,128)(2,1)S(1)} %get-tuple-element.89), channel_id=1, source_target_pairs={{0,16},{8,24},{16,0},{24,8},{1,17},{9,25},{17,1},{25,9},{2,18},{10... | collective-permute-start | bytes 196616 | tf_op jit(solution)/shard_map/ppermute | solution.py:318
  123.0 1.7 %collective-permute-start.36 = (bf16[128,256]{1,0:T(8,128)(2,1)S(1)}, bf16[128,256]{1,0:T(8,128)(2,1)S(1)}, u32[]{:S(2)}, u32[]{:S(2)}) collective-permute-start(bf16[128,256]{1,0:T(8,128)(2,1)S(1)} %get-tuple-element.90), channel_id=1, source_target_pairs={{0,24},{8,16},{16,8},{24,0},{1,25},{9,17},{17,9},{25,1},{2,26},{10... | collective-permute-start | bytes 196616 | tf_op jit(solution)/shard_map/ppermute | solution.py:318
  124.7 0.6 collective-permute-done.34.refs_1_
  125.2 4.1 %collective-permute-done.35.refs_2_ = bf16[128,256]{1,0:T(8,128)(2,1)S(1)} collective-permute-done((bf16[128,256]{1,0:T(8,128)(2,1)S(1)}, bf16[128,256]{1,0:T(8,128)(2,1)S(1)}, u32[]{:S(2)}, u32[]{:S(2)}) %collective-permute-start.35) | collective-permute-done | bytes 65568 | tf_op jit(solution)/shard_map/ppermute | solution.py:318
  129.3 1.4 %shard_map.112 = bf16[128,2048]{1,0:T(8,128)(2,1)} custom-call(s32[4]{0:T(128)S(1)} %iota_xor_fusion.far, bf16[128,256]{1,0:T(8,128)(2,1)S(1)} %get-tuple-element.87.refs_0_, bf16[128,256]{1,0:T(8,128)(2,1)S(1)} %collective-permute-done.34.refs_1_, bf16[128,256]{1,0:T(8,128)(2,1)S(1)} %collective-permute-done.35.refs_2_, ...), custom_call_target="tpu_custom_call" | custom-call | bytes 1048592 | tf_op jit(solution)/shard_map/pallas_call | solution.py:39
  (72 shorter events, 3.0 us)
Async XLA Ops:
  0.0 54.0 %copy-start.10 = (s32[4]{0:T(128)S(1)}, s32[4]{0:T(128)}, u32[]{:S(2)}) copy-start(s32[4]{0:T(128)} %constant.56.clone) | copy-start | bytes 52
  0.0 15.7 %collective-permute-start.4 = (bf16[128,2048]{1,0:T(8,128)(2,1)}, bf16[128,2048]{1,0:T(8,128)(2,1)}, u32[]{:S(2)}, u32[]{:S(2)}) collective-permute-start(bf16[128,2048]{1,0:T(8,128)(2,1)} %refs_0_.1), channel_id=1, source_target_pairs={{0,8},{8,0},{16,24},{24,16},{1,9},{9,1},{17,25},{25,17},{2,10},{10... | collective-permute-start | bytes 1572872 | tf_op jit(solution)/shard_map/ppermute | solution.py:318
  3.0 12.7 %collective-permute-start.3 = (bf16[128,2048]{1,0:T(8,128)(2,1)}, bf16[128,2048]{1,0:T(8,128)(2,1)}, u32[]{:S(2)}, u32[]{:S(2)}) collective-permute-start(bf16[128,2048]{1,0:T(8,128)(2,1)} %refs_0_.1), channel_id=1, source_target_pairs={{8,16},{16,8},{9,17},{17,9},{10,18},{18,10},{11,19},{19,11},{12,20... | collective-permute-start | bytes 1572872 | tf_op jit(solution)/shard_map/ppermute | solution.py:373
  4.5 13.6 %collective-permute-start.6 = (bf16[128,2048]{1,0:T(8,128)(2,1)}, bf16[128,2048]{1,0:T(8,128)(2,1)S(1)}, u32[]{:S(2)}, u32[]{:S(2)}) collective-permute-start(bf16[128,2048]{1,0:T(8,128)(2,1)} %refs_0_.1), channel_id=1, source_target_pairs={{0,1},{1,0},{2,3},{3,2},{4,5},{5,4},{6,7},{7,6},{8,9},{9,8},{10,11... | collective-permute-start | bytes 1572872 | tf_op jit(solution)/shard_map/ppermute | solution.py:348
  6.0 1.2 copy-start
  7.2 0.9 copy-start.1
  8.2 0.9 copy-start.2
  9.1 0.7 copy-start.3
  9.8 72.3 %copy-start.7 = (bf16[128,2048]{1,0:T(8,128)(2,1)S(1)}, bf16[128,2048]{1,0:T(8,128)(2,1)}, u32[]{:S(2)}) copy-start(bf16[128,2048]{1,0:T(8,128)(2,1)} %refs_0_.1) | copy-start | bytes 1572868
  10.5 17.0 %collective-permute-start.1 = (bf16[272,768]{1,0:T(8,128)(2,1)S(1)}, bf16[272,768]{1,0:T(8,128)(2,1)S(1)}, u32[]{:S(2)}, u32[]{:S(2)}) collective-permute-start(bf16[272,768]{1,0:T(8,128)(2,1)S(1)} %get-tuple-element.52), channel_id=1, source_target_pairs={{0,24},{8,16},{16,8},{24,0},{1,25},{9,17},{17,9},{25,1},{2,26},{10... | collective-permute-start | bytes 1253384 | tf_op jit(solution)/shard_map/ppermute | solution.py:318
  13.0 20.0 %collective-permute-start = (bf16[272,768]{1,0:T(8,128)(2,1)S(1)}, bf16[272,768]{1,0:T(8,128)(2,1)S(1)}, u32[]{:S(2)}, u32[]{:S(2)}) collective-permute-start(bf16[272,768]{1,0:T(8,128)(2,1)S(1)} %get-tuple-element.51), channel_id=1, source_target_pairs={{0,8},{8,0},{16,24},{24,16},{1,9},{9,1},{17,25},{25,17},{2,10},{10... | collective-permute-start | bytes 1253384 | tf_op jit(solution)/shard_map/ppermute | solution.py:318
  18.1 17.6 %copy-start.8 = (bf16[128,2048]{1,0:T(8,128)(2,1)}, bf16[128,2048]{1,0:T(8,128)(2,1)S(1)}, u32[]{:S(2)}) copy-start(bf16[128,2048]{1,0:T(8,128)(2,1)S(1)} %collective-permute-done.6.refs_1_) | copy-start | bytes 1572868
  18.1 29.7 %collective-permute-start.15 = (bf16[128,2048]{1,0:T(8,128)(2,1)}, bf16[128,2048]{1,0:T(8,128)(2,1)}, u32[]{:S(2)}, u32[]{:S(2)}) collective-permute-start(bf16[128,2048]{1,0:T(8,128)(2,1)} %collective-permute-done.4.refs_2_), channel_id=1, source_target_pairs={{8,16},{16,8},{9,17},{17,9},{10,18},{18,10},{11,19},{19,11},{12,20... | collective-permute-start | bytes 1572872 | tf_op jit(solution)/shard_map/ppermute | solution.py:377
  27.5 20.2 %collective-permute-start.7 = (bf16[128,2048]{1,0:T(8,128)(2,1)}, bf16[128,2048]{1,0:T(8,128)(2,1)}, u32[]{:S(2)}, u32[]{:S(2)}) collective-permute-start(bf16[128,2048]{1,0:T(8,128)(2,1)} %collective-permute-done.4.refs_2_), channel_id=1, source_target_pairs={{0,1},{1,0},{2,3},{3,2},{4,5},{5,4},{6,7},{7,6},{8,9},{9,8},{10,11... | collective-permute-start | bytes 1572872 | tf_op jit(solution)/shard_map/ppermute | solution.py:348
  33.1 19.7 %collective-permute-start.5 = (bf16[128,2048]{1,0:T(8,128)(2,1)}, bf16[128,2048]{1,0:T(8,128)(2,1)}, u32[]{:S(2)}, u32[]{:S(2)}) collective-permute-start(bf16[128,2048]{1,0:T(8,128)(2,1)} %collective-permute-done.3), channel_id=1, source_target_pairs={{8,0},{16,24},{9,1},{17,25},{10,2},{18,26},{11,3},{19,27},{12,4},{... | collective-permute-start | bytes 1572872 | tf_op jit(solution)/shard_map/ppermute | solution.py:378
  35.7 18.2 %collective-permute-start.2 = (s32[128]{0:T(128)}, s32[128]{0:T(128)S(1)}, u32[]{:S(2)}, u32[]{:S(2)}) collective-permute-start(s32[128]{0:T(128)} %param.12), channel_id=1, source_target_pairs={{0,16},{8,24},{16,0},{24,8},{1,17},{9,25},{17,1},{25,9},{2,18},{10... | collective-permute-start | bytes 1544 | tf_op jit(solution)/shard_map/ppermute | solution.py:318
  45.4 0.7 copy-start.4
  46.2 16.7 %collective-permute-start.9 = (bf16[528,768]{1,0:T(8,128)(2,1)S(1)}, bf16[528,768]{1,0:T(8,128)(2,1)S(1)}, u32[]{:S(2)}, u32[]{:S(2)}) collective-permute-start(bf16[528,768]{1,0:T(8,128)(2,1)S(1)} %shard_map.101.refs_0_.refs_8_), channel_id=1, source_target_pairs={{0,4},{2,6},{4,0},{6,2},{1,5},{3,7},{5,1},{7,3},{8,12},{10,14},{12... | collective-permute-start | bytes 2433032 | tf_op jit(solution)/shard_map/ppermute | solution.py:318
  47.7 17.5 %collective-permute-start.16 = (bf16[128,2048]{1,0:T(8,128)(2,1)}, bf16[128,2048]{1,0:T(8,128)(2,1)}, u32[]{:S(2)}, u32[]{:S(2)}) collective-permute-start(bf16[128,2048]{1,0:T(8,128)(2,1)} %collective-permute-done.15), channel_id=1, source_target_pairs={{8,0},{16,24},{9,1},{17,25},{10,2},{18,26},{11,3},{19,27},{12,4},{... | collective-permute-start | bytes 1572872 | tf_op jit(solution)/shard_map/ppermute | solution.py:385
  53.9 9.8 %collective-permute-start.8 = (bf16[128,2048]{1,0:T(8,128)(2,1)S(1)}, bf16[128,2048]{1,0:T(8,128)(2,1)}, u32[]{:S(2)}, u32[]{:S(2)}) collective-permute-start(bf16[128,2048]{1,0:T(8,128)(2,1)S(1)} %broadcast_select_fusion.1.refs_4_), channel_id=1, source_target_pairs={{0,1},{1,0},{2,3},{3,2},{4,5},{5,4},{6,7},{7,6},{8,9},{9,8},{10,11... | collective-permute-start | bytes 1572872 | tf_op jit(solution)/shard_map/ppermute | solution.py:348
  54.6 25.9 %collective-permute-start.11 = (bf16[528,768]{1,0:T(8,128)(2,1)S(1)}, bf16[528,768]{1,0:T(8,128)(2,1)S(1)}, u32[]{:S(2)}, u32[]{:S(2)}) collective-permute-start(bf16[528,768]{1,0:T(8,128)(2,1)S(1)} %shard_map.101.refs_0_.refs_8_), channel_id=1, source_target_pairs={{0,2},{2,0},{4,6},{6,4},{1,3},{3,1},{5,7},{7,5},{8,10},{10,8},{12,... | collective-permute-start | bytes 2433032 | tf_op jit(solution)/shard_map/ppermute | solution.py:318
  62.8 15.9 %collective-permute-start.18 = (bf16[256,768]{1,0:T(8,128)(2,1)S(1)}, bf16[256,768]{1,0:T(8,128)(2,1)S(1)}, u32[]{:S(2)}, u32[]{:S(2)}) collective-permute-start(bf16[256,768]{1,0:T(8,128)(2,1)S(1)} %get-tuple-element.68), channel_id=1, source_target_pairs={{0,16},{8,24},{16,0},{24,8},{1,17},{9,25},{17,1},{25,9},{2,18},{10... | collective-permute-start | bytes 1179656 | tf_op jit(solution)/shard_map/ppermute | solution.py:318
  63.1 19.0 %collective-permute-start.13 = (bf16[528,768]{1,0:T(8,128)(2,1)S(1)}, bf16[528,768]{1,0:T(8,128)(2,1)S(1)}, u32[]{:S(2)}, u32[]{:S(2)}) collective-permute-start(bf16[528,768]{1,0:T(8,128)(2,1)S(1)} %collective-permute-done.9.refs_2_.refs_10_), channel_id=1, source_target_pairs={{0,2},{2,0},{4,6},{6,4},{1,3},{3,1},{5,7},{7,5},{8,10},{10,8},{12,... | collective-permute-start | bytes 2433032 | tf_op jit(solution)/shard_map/ppermute | solution.py:318
  63.7 11.5 %collective-permute-start.10 = (bf16[272,768]{1,0:T(8,128)(2,1)S(1)}, bf16[272,768]{1,0:T(8,128)(2,1)S(1)}, u32[]{:S(2)}, u32[]{:S(2)}) collective-permute-start(bf16[272,768]{1,0:T(8,128)(2,1)S(1)} %shard_map.102.refs_1_.refs_9_), channel_id=1, source_target_pairs={{0,4},{2,6},{4,0},{6,2},{1,5},{3,7},{5,1},{7,3},{8,12},{10,14},{12... | collective-permute-start | bytes 1253384 | tf_op jit(solution)/shard_map/ppermute | solution.py:318
  66.3 13.5 %collective-permute-start.17 = (bf16[128,2048]{1,0:T(8,128)(2,1)S(1)}, bf16[128,2048]{1,0:T(8,128)(2,1)S(1)}, u32[]{:S(2)}, u32[]{:S(2)}) collective-permute-start(bf16[128,2048]{1,0:T(8,128)(2,1)S(1)} %broadcast_select_fusion.refs_6_), channel_id=1, source_target_pairs={{0,1},{1,0},{2,3},{3,2},{4,5},{5,4},{6,7},{7,6},{8,9},{9,8},{10,11... | collective-permute-start | bytes 1572872 | tf_op jit(solution)/shard_map/ppermute | solution.py:348
  75.2 5.6 %collective-permute-start.12 = (bf16[272,768]{1,0:T(8,128)(2,1)S(1)}, bf16[272,768]{1,0:T(8,128)(2,1)S(1)}, u32[]{:S(2)}, u32[]{:S(2)}) collective-permute-start(bf16[272,768]{1,0:T(8,128)(2,1)S(1)} %shard_map.102.refs_1_.refs_9_), channel_id=1, source_target_pairs={{0,2},{2,0},{4,6},{6,4},{1,3},{3,1},{5,7},{7,5},{8,10},{10,8},{12,... | collective-permute-start | bytes 1253384 | tf_op jit(solution)/shard_map/ppermute | solution.py:318
  78.8 3.3 %collective-permute-start.14 = (bf16[272,768]{1,0:T(8,128)(2,1)S(1)}, bf16[272,768]{1,0:T(8,128)(2,1)S(1)}, u32[]{:S(2)}, u32[]{:S(2)}) collective-permute-start(bf16[272,768]{1,0:T(8,128)(2,1)S(1)} %collective-permute-done.10.refs_3_.refs_11_), channel_id=1, source_target_pairs={{0,2},{2,0},{4,6},{6,4},{1,3},{3,1},{5,7},{7,5},{8,10},{10,8},{12,... | collective-permute-start | bytes 1253384 | tf_op jit(solution)/shard_map/ppermute | solution.py:318
  79.9 9.9 %collective-permute-start.19 = (bf16[256,256]{1,0:T(8,128)(2,1)S(1)}, bf16[256,256]{1,0:T(8,128)(2,1)S(1)}, u32[]{:S(2)}, u32[]{:S(2)}) collective-permute-start(bf16[256,256]{1,0:T(8,128)(2,1)S(1)} %get-tuple-element.70.refs_0_), channel_id=1, source_target_pairs={{0,4},{2,6},{4,0},{6,2},{1,5},{3,7},{5,1},{7,3},{8,12},{10,14},{12... | collective-permute-start | bytes 393224 | tf_op jit(solution)/shard_map/ppermute | solution.py:318
  80.5 9.8 %collective-permute-start.20 = (bf16[256,256]{1,0:T(8,128)(2,1)S(1)}, bf16[256,256]{1,0:T(8,128)(2,1)S(1)}, u32[]{:S(2)}, u32[]{:S(2)}) collective-permute-start(bf16[256,256]{1,0:T(8,128)(2,1)S(1)} %get-tuple-element.70.refs_0_), channel_id=1, source_target_pairs={{0,2},{2,0},{4,6},{6,4},{1,3},{3,1},{5,7},{7,5},{8,10},{10,8},{12,... | collective-permute-start | bytes 393224 | tf_op jit(solution)/shard_map/ppermute | solution.py:318
  80.8 5.3 %copy-start.5 = (s32[13]{0:T(128)S(1)}, s32[13]{0:T(128)}, u32[]{:S(2)}) copy-start(s32[13]{0:T(128)} %doc_starts.1) | copy-start | bytes 160
  80.8 5.3 %copy-start.6 = (f32[1,128]{1,0:T(1,128)S(1)}, f32[1,128]{1,0:T(1,128)}, u32[]{:S(2)}) copy-start(f32[1,128]{1,0:T(1,128)} %constant.58.clone.freqs) | copy-start | bytes 1540
  80.8 10.9 %collective-permute-start.22 = (bf16[256,512]{1,0:T(8,128)(2,1)S(1)}, bf16[256,512]{1,0:T(8,128)(2,1)S(1)}, u32[]{:S(2)}, u32[]{:S(2)}) collective-permute-start(bf16[256,512]{1,0:T(8,128)(2,1)S(1)} %get-tuple-element.74.refs_0_), channel_id=1, source_target_pairs={{0,4},{2,6},{4,0},{6,2},{1,5},{3,7},{5,1},{7,3},{8,12},{10,14},{12... | collective-permute-start | bytes 786440 | tf_op jit(solution)/shard_map/ppermute | solution.py:318
  82.1 1.0 copy-start.9
  86.1 2.8 %copy-start.11 = (f32[128]{0:T(128)S(1)}, f32[128]{0:T(128)}, u32[]{:S(2)}) copy-start(f32[128]{0:T(128)} %constant.64) | copy-start | bytes 1540
  89.8 1.4 %collective-permute-start.21 = (bf16[256,256]{1,0:T(8,128)(2,1)S(1)}, bf16[256,256]{1,0:T(8,128)(2,1)S(1)}, u32[]{:S(2)}, u32[]{:S(2)}) collective-permute-start(bf16[256,256]{1,0:T(8,128)(2,1)S(1)} %collective-permute-done.19.refs_1_), channel_id=1, source_target_pairs={{0,2},{2,0},{4,6},{6,4},{1,3},{3,1},{5,7},{7,5},{8,10},{10,8},{12,... | collective-permute-start | bytes 393224 | tf_op jit(solution)/shard_map/ppermute | solution.py:318
  90.0 4.5 %collective-permute-start.23 = (bf16[256,512]{1,0:T(8,128)(2,1)S(1)}, bf16[256,512]{1,0:T(8,128)(2,1)S(1)}, u32[]{:S(2)}, u32[]{:S(2)}) collective-permute-start(bf16[256,512]{1,0:T(8,128)(2,1)S(1)} %get-tuple-element.74.refs_0_), channel_id=1, source_target_pairs={{0,2},{2,0},{4,6},{6,4},{1,3},{3,1},{5,7},{7,5},{8,10},{10,8},{12,... | collective-permute-start | bytes 786440 | tf_op jit(solution)/shard_map/ppermute | solution.py:318
  91.7 2.8 %collective-permute-start.24 = (bf16[256,512]{1,0:T(8,128)(2,1)S(1)}, bf16[256,512]{1,0:T(8,128)(2,1)S(1)}, u32[]{:S(2)}, u32[]{:S(2)}) collective-permute-start(bf16[256,512]{1,0:T(8,128)(2,1)S(1)} %collective-permute-done.22.refs_1_), channel_id=1, source_target_pairs={{0,2},{2,0},{4,6},{6,4},{1,3},{3,1},{5,7},{7,5},{8,10},{10,8},{12,... | collective-permute-start | bytes 786440 | tf_op jit(solution)/shard_map/ppermute | solution.py:318
  91.9 9.1 %collective-permute-start.28 = (bf16[512,256]{1,0:T(8,128)(2,1)S(1)}, bf16[512,256]{1,0:T(8,128)(2,1)S(1)}, u32[]{:S(2)}, u32[]{:S(2)}) collective-permute-start(bf16[512,256]{1,0:T(8,128)(2,1)S(1)} %shard_map.106.refs_4_), channel_id=1, source_target_pairs={{0,4},{2,6},{4,0},{6,2},{1,5},{3,7},{5,1},{7,3},{8,12},{10,14},{12... | collective-permute-start | bytes 786440 | tf_op jit(solution)/shard_map/ppermute | solution.py:318
  95.9 5.1 %collective-permute-start.29 = (bf16[256,256]{1,0:T(8,128)(2,1)S(1)}, bf16[256,256]{1,0:T(8,128)(2,1)S(1)}, u32[]{:S(2)}, u32[]{:S(2)}) collective-permute-start(bf16[256,256]{1,0:T(8,128)(2,1)S(1)} %get-tuple-element.82), channel_id=1, source_target_pairs={{0,2},{2,0},{4,6},{6,4},{1,3},{3,1},{5,7},{7,5},{8,10},{10,8},{12,... | collective-permute-start | bytes 393224 | tf_op jit(solution)/shard_map/ppermute | solution.py:318
  96.0 7.8 %collective-permute-start.30 = (bf16[256,256]{1,0:T(8,128)(2,1)S(1)}, bf16[256,256]{1,0:T(8,128)(2,1)S(1)}, u32[]{:S(2)}, u32[]{:S(2)}) collective-permute-start(bf16[256,256]{1,0:T(8,128)(2,1)S(1)} %get-tuple-element.83), channel_id=1, source_target_pairs={{0,4},{2,6},{4,0},{6,2},{1,5},{3,7},{5,1},{7,3},{8,12},{10,14},{12... | collective-permute-start | bytes 393224 | tf_op jit(solution)/shard_map/ppermute | solution.py:318
  97.3 8.2 %collective-permute-start.31 = (bf16[256,256]{1,0:T(8,128)(2,1)S(1)}, bf16[256,256]{1,0:T(8,128)(2,1)S(1)}, u32[]{:S(2)}, u32[]{:S(2)}) collective-permute-start(bf16[256,256]{1,0:T(8,128)(2,1)S(1)} %get-tuple-element.84), channel_id=1, source_target_pairs={{0,6},{2,4},{4,2},{6,0},{1,7},{3,5},{5,3},{7,1},{8,14},{10,12},{12... | collective-permute-start | bytes 393224 | tf_op jit(solution)/shard_map/ppermute | solution.py:318
  105.5 2.4 %collective-permute-start.33 = (bf16[512,256]{1,0:T(8,128)(2,1)S(1)}, bf16[512,256]{1,0:T(8,128)(2,1)S(1)}, u32[]{:S(2)}, u32[]{:S(2)}) collective-permute-start(bf16[512,256]{1,0:T(8,128)(2,1)S(1)} %collective-permute-done.28.refs_5_), channel_id=1, source_target_pairs={{0,2},{2,0},{4,6},{6,4},{1,3},{3,1},{5,7},{7,5},{8,10},{10,8},{12,... | collective-permute-start | bytes 786440 | tf_op jit(solution)/shard_map/ppermute | solution.py:318
  105.9 2.0 %collective-permute-start.32 = (bf16[512,256]{1,0:T(8,128)(2,1)S(1)}, bf16[512,256]{1,0:T(8,128)(2,1)S(1)}, u32[]{:S(2)}, u32[]{:S(2)}) collective-permute-start(bf16[512,256]{1,0:T(8,128)(2,1)S(1)} %shard_map.106.refs_4_), channel_id=1, source_target_pairs={{0,2},{2,0},{4,6},{6,4},{1,3},{3,1},{5,7},{7,5},{8,10},{10,8},{12,... | collective-permute-start | bytes 786440 | tf_op jit(solution)/shard_map/ppermute | solution.py:318
  106.0 8.7 %collective-permute-start.25 = (bf16[256,256]{1,0:T(8,128)(2,1)S(1)}, bf16[256,256]{1,0:T(8,128)(2,1)S(1)}, u32[]{:S(2)}, u32[]{:S(2)}) collective-permute-start(bf16[256,256]{1,0:T(8,128)(2,1)S(1)} %get-tuple-element.78), channel_id=1, source_target_pairs={{0,2},{2,0},{4,6},{6,4},{1,3},{3,1},{5,7},{7,5},{8,10},{10,8},{12,... | collective-permute-start | bytes 393224 | tf_op jit(solution)/shard_map/ppermute | solution.py:318
  106.4 9.9 %collective-permute-start.26 = (bf16[256,256]{1,0:T(8,128)(2,1)S(1)}, bf16[256,256]{1,0:T(8,128)(2,1)S(1)}, u32[]{:S(2)}, u32[]{:S(2)}) collective-permute-start(bf16[256,256]{1,0:T(8,128)(2,1)S(1)} %get-tuple-element.79), channel_id=1, source_target_pairs={{0,4},{2,6},{4,0},{6,2},{1,5},{3,7},{5,1},{7,3},{8,12},{10,14},{12... | collective-permute-start | bytes 393224 | tf_op jit(solution)/shard_map/ppermute | solution.py:318
  107.2 9.2 %collective-permute-start.27 = (bf16[256,256]{1,0:T(8,128)(2,1)S(1)}, bf16[256,256]{1,0:T(8,128)(2,1)S(1)}, u32[]{:S(2)}, u32[]{:S(2)}) collective-permute-start(bf16[256,256]{1,0:T(8,128)(2,1)S(1)} %get-tuple-element.80), channel_id=1, source_target_pairs={{0,6},{2,4},{4,2},{6,0},{1,7},{3,5},{5,3},{7,1},{8,14},{10,12},{12... | collective-permute-start | bytes 393224 | tf_op jit(solution)/shard_map/ppermute | solution.py:318
  111.9 11.1 %collective-permute-start.37 = (bf16[128,256]{1,0:T(8,128)(2,1)S(1)}, bf16[128,256]{1,0:T(8,128)(2,1)S(1)}, u32[]{:S(2)}, u32[]{:S(2)}) collective-permute-start(bf16[128,256]{1,0:T(8,128)(2,1)S(1)} %get-tuple-element.92), channel_id=1, source_target_pairs={{0,8},{8,0},{16,24},{24,16},{1,9},{9,1},{17,25},{25,17},{2,10},{10... | collective-permute-start | bytes 196616 | tf_op jit(solution)/shard_map/ppermute | solution.py:318
  113.8 10.8 %collective-permute-start.38 = (bf16[128,256]{1,0:T(8,128)(2,1)S(1)}, bf16[128,256]{1,0:T(8,128)(2,1)S(1)}, u32[]{:S(2)}, u32[]{:S(2)}) collective-permute-start(bf16[128,256]{1,0:T(8,128)(2,1)S(1)} %get-tuple-element.93), channel_id=1, source_target_pairs={{0,16},{8,24},{16,0},{24,8},{1,17},{9,25},{17,1},{25,9},{2,18},{10... | collective-permute-start | bytes 196616 | tf_op jit(solution)/shard_map/ppermute | solution.py:318
  114.7 9.9 %collective-permute-start.39 = (bf16[128,256]{1,0:T(8,128)(2,1)S(1)}, bf16[128,256]{1,0:T(8,128)(2,1)S(1)}, u32[]{:S(2)}, u32[]{:S(2)}) collective-permute-start(bf16[128,256]{1,0:T(8,128)(2,1)S(1)} %get-tuple-element.94), channel_id=1, source_target_pairs={{0,24},{8,16},{16,8},{24,0},{1,25},{9,17},{17,9},{25,1},{2,26},{10... | collective-permute-start | bytes 196616 | tf_op jit(solution)/shard_map/ppermute | solution.py:318
  120.2 5.0 %collective-permute-start.34 = (bf16[128,256]{1,0:T(8,128)(2,1)S(1)}, bf16[128,256]{1,0:T(8,128)(2,1)S(1)}, u32[]{:S(2)}, u32[]{:S(2)}) collective-permute-start(bf16[128,256]{1,0:T(8,128)(2,1)S(1)} %get-tuple-element.88), channel_id=1, source_target_pairs={{0,8},{8,0},{16,24},{24,16},{1,9},{9,1},{17,25},{25,17},{2,10},{10... | collective-permute-start | bytes 196616 | tf_op jit(solution)/shard_map/ppermute | solution.py:318
  121.2 8.1 %collective-permute-start.35 = (bf16[128,256]{1,0:T(8,128)(2,1)S(1)}, bf16[128,256]{1,0:T(8,128)(2,1)S(1)}, u32[]{:S(2)}, u32[]{:S(2)}) collective-permute-start(bf16[128,256]{1,0:T(8,128)(2,1)S(1)} %get-tuple-element.89), channel_id=1, source_target_pairs={{0,16},{8,24},{16,0},{24,8},{1,17},{9,25},{17,1},{25,9},{2,18},{10... | collective-permute-start | bytes 196616 | tf_op jit(solution)/shard_map/ppermute | solution.py:318
  123.0 6.4 %collective-permute-start.36 = (bf16[128,256]{1,0:T(8,128)(2,1)S(1)}, bf16[128,256]{1,0:T(8,128)(2,1)S(1)}, u32[]{:S(2)}, u32[]{:S(2)}) collective-permute-start(bf16[128,256]{1,0:T(8,128)(2,1)S(1)} %get-tuple-element.90), channel_id=1, source_target_pairs={{0,24},{8,16},{16,8},{24,0},{1,25},{9,17},{17,9},{25,1},{2,26},{10... | collective-permute-start | bytes 196616 | tf_op jit(solution)/shard_map/ppermute | solution.py:318

commit v3 on v1

--- a/solution.py
+++ b/solution.py
@@ -255,9 +255,10 @@
     for kv in kvs:
         own = slice(start, start + kv.shape[0])
         keys[own, :HEAD_SIZE] = kv[:, :HEAD_SIZE]
-        values[own, :] = kv[:, HEAD_SIZE:]
+        values[own, :HEAD_SIZE] = kv[:, HEAD_SIZE:]
         start += kv.shape[0]
     keys[:, HEAD_SIZE:] = key_hot[...]
+    values[:, HEAD_SIZE:] = jnp.ones_like(key_hot)
     span = arrived[0].shape[0] // groups
     at = lax.broadcasted_iota(jnp.int32, (span * query_parts, rows), 0)
     for group in range(groups):
@@ -288,8 +289,8 @@
         held = scores[step % 2]
         top = jnp.max(held, axis=1, keepdims=True)
         kept = jnp.exp2((held - top) * factor)
-        total = jnp.sum(kept, axis=1, keepdims=True)
-        mixed = dot(kept.astype(jnp.bfloat16), values[...])
+        both = dot(kept.astype(jnp.bfloat16), values[...])
+        mixed, total = both[:, :HEAD_SIZE], both[:, HEAD_SIZE : HEAD_SIZE + 1]
         context[own, head * HEAD_SIZE : (head + 1) * HEAD_SIZE] = (mixed / total).astype(
             context.dtype
         )
@@ -498,7 +499,7 @@
             [far, columns, query_bar, key_hot, *arrived, *kvs],
             scratch=[
                 pltpu.VMEM((keys, size + LANES), jnp.bfloat16),
-                pltpu.VMEM((keys, size), jnp.bfloat16),
+                pltpu.VMEM((keys, size + LANES), jnp.bfloat16),
                 pltpu.VMEM((pair // size, total_rows, size + LANES), jnp.bfloat16),
                 pltpu.VMEM((2, block_rows, keys), jnp.float32),
                 pltpu.VMEM((total_rows, pair), jnp.bfloat16),

time: 130 us -> 130 us (level)
  no operation moved by 1% of the time
where the time goes in v3:
time: 130 us
  waiting for transfers between devices  54.7 us (42%)
  starting transfers between devices  46 us (35%)
  Pallas kernels  20.3 us (16%)
  local copies, waits for them, and re-layouts  4.99 us (4%)
  other arithmetic  3.38 us (3%)
    ppermute x32, waiting for transfers between devices, turn(): return lax.ppermute(value, axis, [(i, i ^ bits) for i in range(count)])  44.2 us
    ppermute x32, starting transfers between devices, turn(): return lax.ppermute(value, axis, [(i, i ^ bits) for i in range(count)])  36.8 us
    pallas_call x12, Pallas kernels, call(): pl.pallas_call(kernel, out_shape=out_shape, in_specs=specs, out_specs=[VM...  20.3 us
    ppermute x4, waiting for transfers between devices, flip(): return lax.ppermute(value, 'tp', [(0, 1), (1, 0)])  5.35 us
    ppermute x1, waiting for transfers between devices, body(): end = lax.ppermute(after(over, near, weights_near), 'line', outer)  5.08 us
    unnamed x26, local copies, waits for them, and re-layouts  3.81 us
    ppermute x4, starting transfers between devices, flip(): return lax.ppermute(value, 'tp', [(0, 1), (1, 0)])  3.67 us
  transfers between devices with their start and end apart: 40, of which 17 were waited for; matrix products, arithmetic and copies ran while one was open for 4% of the time, Pallas kernels for 15%

profile of v3, /device:TPU:0, one launch (start us, length us, event | category | flops | bytes accessed | tf_op | source)
XLA Modules:
  0.0 129.6 jit_solution(4961270309969797993)
XLA Ops:
  0.0 3.0 %collective-permute-start.4 = (bf16[128,2048]{1,0:T(8,128)(2,1)}, bf16[128,2048]{1,0:T(8,128)(2,1)S(1)}, u32[]{:S(2)}, u32[]{:S(2)}) collective-permute-start(bf16[128,2048]{1,0:T(8,128)(2,1)} %refs_0_.1), channel_id=1, source_target_pairs={{0,8},{8,0},{16,24},{24,16},{1,9},{9,1},{17,25},{25,17},{2,10},{10... | collective-permute-start | bytes 1572872 | tf_op jit(solution)/shard_map/ppermute | solution.py:314
  3.0 1.5 %collective-permute-start.3 = (bf16[128,2048]{1,0:T(8,128)(2,1)}, bf16[128,2048]{1,0:T(8,128)(2,1)}, u32[]{:S(2)}, u32[]{:S(2)}) collective-permute-start(bf16[128,2048]{1,0:T(8,128)(2,1)} %refs_0_.1), channel_id=1, source_target_pairs={{8,16},{16,8},{9,17},{17,9},{10,18},{18,10},{11,19},{19,11},{12,20... | collective-permute-start | bytes 1572872 | tf_op jit(solution)/shard_map/ppermute | solution.py:369
  4.5 1.5 %collective-permute-start.6 = (bf16[128,2048]{1,0:T(8,128)(2,1)}, bf16[128,2048]{1,0:T(8,128)(2,1)S(1)}, u32[]{:S(2)}, u32[]{:S(2)}) collective-permute-start(bf16[128,2048]{1,0:T(8,128)(2,1)} %refs_0_.1), channel_id=1, source_target_pairs={{0,1},{1,0},{2,3},{3,2},{4,5},{5,4},{6,7},{7,6},{8,9},{9,8},{10,11... | collective-permute-start | bytes 1572872 | tf_op jit(solution)/shard_map/ppermute | solution.py:344
  6.0 1.2 copy-done
  7.2 0.9 copy-done.1
  8.2 0.9 copy-done.2
  9.2 0.7 copy-done.3
  9.8 0.7 shard_map.100
  10.5 2.5 %collective-permute-start.1 = (bf16[272,768]{1,0:T(8,128)(2,1)S(1)}, bf16[272,768]{1,0:T(8,128)(2,1)S(1)}, u32[]{:S(2)}, u32[]{:S(2)}) collective-permute-start(bf16[272,768]{1,0:T(8,128)(2,1)S(1)} %get-tuple-element.50), channel_id=1, source_target_pairs={{0,24},{8,16},{16,8},{24,0},{1,25},{9,17},{17,9},{25,1},{2,26},{10... | collective-permute-start | bytes 1253384 | tf_op jit(solution)/shard_map/ppermute | solution.py:314
  13.1 1.3 collective-permute-start
  14.3 1.3 %collective-permute-done.4.refs_2_ = bf16[128,2048]{1,0:T(8,128)(2,1)S(1)} collective-permute-done((bf16[128,2048]{1,0:T(8,128)(2,1)}, bf16[128,2048]{1,0:T(8,128)(2,1)S(1)}, u32[]{:S(2)}, u32[]{:S(2)}) %collective-permute-start.4) | collective-permute-done | bytes 524320 | tf_op jit(solution)/shard_map/ppermute | solution.py:314
  15.7 2.4 %collective-permute-done.6.refs_1_ = bf16[128,2048]{1,0:T(8,128)(2,1)S(1)} collective-permute-done((bf16[128,2048]{1,0:T(8,128)(2,1)}, bf16[128,2048]{1,0:T(8,128)(2,1)S(1)}, u32[]{:S(2)}, u32[]{:S(2)}) %collective-permute-start.6) | collective-permute-done | bytes 524320 | tf_op jit(solution)/shard_map/ppermute | solution.py:344
  18.1 1.5 %collective-permute-start.15 = (bf16[128,2048]{1,0:T(8,128)(2,1)S(1)}, bf16[128,2048]{1,0:T(8,128)(2,1)}, u32[]{:S(2)}, u32[]{:S(2)}) collective-permute-start(bf16[128,2048]{1,0:T(8,128)(2,1)S(1)} %collective-permute-done.4.refs_2_), channel_id=1, source_target_pairs={{8,16},{16,8},{9,17},{17,9},{10,18},{18,10},{11,19},{19,11},{12,20... | collective-permute-start | bytes 1572872 | tf_op jit(solution)/shard_map/ppermute | solution.py:373
  19.6 8.0 %collective-permute-done.1.first.refs_0_ = bf16[272,768]{1,0:T(8,128)(2,1)S(1)} collective-permute-done((bf16[272,768]{1,0:T(8,128)(2,1)S(1)}, bf16[272,768]{1,0:T(8,128)(2,1)S(1)}, u32[]{:S(2)}, u32[]{:S(2)}) %collective-permute-start.1) | collective-permute-done | bytes 417824 | tf_op jit(solution)/shard_map/ppermute | solution.py:314
  27.5 1.5 %collective-permute-start.7 = (bf16[128,2048]{1,0:T(8,128)(2,1)S(1)}, bf16[128,2048]{1,0:T(8,128)(2,1)}, u32[]{:S(2)}, u32[]{:S(2)}) collective-permute-start(bf16[128,2048]{1,0:T(8,128)(2,1)S(1)} %collective-permute-done.4.refs_2_), channel_id=1, source_target_pairs={{0,1},{1,0},{2,3},{3,2},{4,5},{5,4},{6,7},{7,6},{8,9},{9,8},{10,11... | collective-permute-start | bytes 1572872 | tf_op jit(solution)/shard_map/ppermute | solution.py:344
  29.0 4.0 %collective-permute-done.refs_1_.refs_2_ = bf16[272,768]{1,0:T(8,128)(2,1)S(1)} collective-permute-done((bf16[272,768]{1,0:T(8,128)(2,1)S(1)}, bf16[272,768]{1,0:T(8,128)(2,1)S(1)}, u32[]{:S(2)}, u32[]{:S(2)}) %collective-permute-start) | collective-permute-done | bytes 417824 | tf_op jit(solution)/shard_map/ppermute | solution.py:314
  33.1 1.3 collective-permute-start.5
  34.4 0.6 gather_fusion
  35.0 9.7 %collective-permute-start.2 = (s32[128]{0:T(128)S(1)}, s32[128]{0:T(128)S(1)}, u32[]{:S(2)}, u32[]{:S(2)}) collective-permute-start(s32[128]{0:T(128)S(1)} %copy-done.4), channel_id=1, source_target_pairs={{0,16},{8,24},{16,0},{24,8},{1,17},{9,25},{17,1},{25,9},{2,18},{10... | collective-permute-start | bytes 1544 | tf_op jit(solution)/shard_map/ppermute | solution.py:314
  44.8 1.6 %collective-permute-start.9 = (bf16[528,768]{1,0:T(8,128)(2,1)S(1)}, bf16[528,768]{1,0:T(8,128)(2,1)S(1)}, u32[]{:S(2)}, u32[]{:S(2)}) collective-permute-start(bf16[528,768]{1,0:T(8,128)(2,1)S(1)} %shard_map.101.refs_0_.refs_8_), channel_id=1, source_target_pairs={{0,4},{2,6},{4,0},{6,2},{1,5},{3,7},{5,1},{7,3},{8,12},{10,14},{12... | collective-permute-start | bytes 2433032 | tf_op jit(solution)/shard_map/ppermute | solution.py:314
  46.4 1.3 collective-permute-start.16
  47.7 5.1 %collective-permute-done.5 = bf16[128,2048]{1,0:T(8,128)(2,1)} collective-permute-done((bf16[128,2048]{1,0:T(8,128)(2,1)}, bf16[128,2048]{1,0:T(8,128)(2,1)}, u32[]{:S(2)}, u32[]{:S(2)}) %collective-permute-start.5) | collective-permute-done | bytes 524320 | tf_op jit(solution)/shard_map/ppermute | solution.py:374
  52.8 1.1 broadcast_select_fusion.1.refs_4_
  54.7 6.8 %collective-permute-done.9.refs_2_.refs_10_ = bf16[528,768]{1,0:T(8,128)(2,1)S(1)} collective-permute-done((bf16[528,768]{1,0:T(8,128)(2,1)S(1)}, bf16[528,768]{1,0:T(8,128)(2,1)S(1)}, u32[]{:S(2)}, u32[]{:S(2)}) %collective-permute-start.9) | collective-permute-done | bytes 811040 | tf_op jit(solution)/shard_map/ppermute | solution.py:314
  61.5 0.3 collective-permute-start.18
  61.8 1.9 %collective-permute-done.8.refs_5_ = bf16[128,2048]{1,0:T(8,128)(2,1)} collective-permute-done((bf16[128,2048]{1,0:T(8,128)(2,1)S(1)}, bf16[128,2048]{1,0:T(8,128)(2,1)}, u32[]{:S(2)}, u32[]{:S(2)}) %collective-permute-start.8) | collective-permute-done | bytes 524320 | tf_op jit(solution)/shard_map/ppermute | solution.py:344
  63.7 1.5 %collective-permute-start.10 = (bf16[272,768]{1,0:T(8,128)(2,1)S(1)}, bf16[272,768]{1,0:T(8,128)(2,1)S(1)}, u32[]{:S(2)}, u32[]{:S(2)}) collective-permute-start(bf16[272,768]{1,0:T(8,128)(2,1)S(1)} %shard_map.102.refs_1_.refs_9_), channel_id=1, source_target_pairs={{0,4},{2,6},{4,0},{6,2},{1,5},{3,7},{5,1},{7,3},{8,12},{10,14},{12... | collective-permute-start | bytes 1253384 | tf_op jit(solution)/shard_map/ppermute | solution.py:314
  65.2 1.1 broadcast_select_fusion.refs_6_
  66.3 0.6 collective-permute-start.17
  66.9 7.0 %collective-permute-done.10.refs_3_.refs_11_ = bf16[272,768]{1,0:T(8,128)(2,1)S(1)} collective-permute-done((bf16[272,768]{1,0:T(8,128)(2,1)S(1)}, bf16[272,768]{1,0:T(8,128)(2,1)S(1)}, u32[]{:S(2)}, u32[]{:S(2)}) %collective-permute-start.10) | collective-permute-done | bytes 417824 | tf_op jit(solution)/shard_map/ppermute | solution.py:314
  73.9 3.5 %collective-permute-done.18.value = bf16[256,768]{1,0:T(8,128)(2,1)S(1)} collective-permute-done((bf16[256,768]{1,0:T(8,128)(2,1)S(1)}, bf16[256,768]{1,0:T(8,128)(2,1)S(1)}, u32[]{:S(2)}, u32[]{:S(2)}) %collective-permute-start.18) | collective-permute-done | bytes 393248 | tf_op jit(solution)/shard_map/ppermute | solution.py:314
  77.5 1.0 collective-permute-done.17.refs_7_
  78.6 0.6 collective-permute-start.21
  79.3 1.4 %collective-permute-start.19 = (bf16[256,512]{1,0:T(8,128)(2,1)S(1)}, bf16[256,512]{1,0:T(8,128)(2,1)S(1)}, u32[]{:S(2)}, u32[]{:S(2)}) collective-permute-start(bf16[256,512]{1,0:T(8,128)(2,1)S(1)} %get-tuple-element.67.refs_0_), channel_id=1, source_target_pairs={{0,4},{2,6},{4,0},{6,2},{1,5},{3,7},{5,1},{7,3},{8,12},{10,14},{12... | collective-permute-start | bytes 786440 | tf_op jit(solution)/shard_map/ppermute | solution.py:314
  80.8 4.3 %shard_map.104 = (f32[512,768]{1,0:T(8,128)S(1)}, bf16[512,1024]{1,0:T(8,128)(2,1)S(1)}) custom-call(s32[4]{0:T(128)S(1)} %pad_add_fusion.places, s32[16]{0:T(128)S(1)} %fusion.table, bf16[128,2048]{1,0:T(8,128)(2,1)S(1)} %copy-done.7, bf16[128,2048]{1,0:T(8,128)(2,1)S(1)} %copy-done.9, bf16[128,2048]{1,0:T(8,128)(2,1)S(1)} %collective-permute-done.4.refs_2_, ...), custom_call_target="tpu_custom_call" | custom-call | flops 3221225472 | bytes 11731024 | tf_op jit(solution)/shard_map/pallas_call | solution.py:39
  85.1 2.7 %shard_map.103 = (f32[512,128]{1,0:T(8,128)S(1)}, bf16[2048,128]{1,0:T(8,128)(2,1)S(1)}, bf16[512,128]{1,0:T(8,128)(2,1)S(1)}, s32[1,512]{1,0:T(1,128)S(1)}, s32[4,128]{1,0:T(4,128)S(1)}) custom-call(s32[4]{0:T(128)S(1)} %broadcast_add_fusion.2.mine, s32[16]{0:T(128)S(1)} %add.56.order, s32[16]{0:T(128)S(1)} %add.60.came, s32[1]{0:T(128)} %bitcast.mate.twist, ...), custom_call_target="tpu_custom_call" | custom-call | flops 1000000000 | bytes 5837516 | tf_op jit(solution)/shard_map/pallas_call | solution.py:39
  87.8 0.9 sine_multiply_fusion
  89.0 0.3 collective-permute-start.20
  89.3 0.8 collective-permute-done.23.refs_3_
  90.2 0.5 shard_map.106.refs_4_
  90.9 0.7 collective-permute-start.28
  91.6 0.7 collective-permute-done.24.refs_3_
  92.3 1.4 %shard_map.108 = (bf16[256,256]{1,0:T(8,128)(2,1)S(1)}, bf16[256,256]{1,0:T(8,128)(2,1)S(1)}, bf16[256,256]{1,0:T(8,128)(2,1)S(1)}, bf16[256,256]{1,0:T(8,128)(2,1)S(1)}) custom-call(f32[512,768]{1,0:T(8,128)S(1)} %get-tuple-element.63.total, bf16[512,1024]{1,0:T(8,128)(2,1)S(1)} %get-tuple-element.64.later, bf16[256,512]{1,0:T(8,128)(2,1)S(1)} %get-tuple-element.67.refs_0_, ...), custom_call_target="tpu_custom_call" | custom-call | flops 536870912 | bytes 4720640 | tf_op jit(solution)/shard_map/pallas_call | solution.py:39
  94.0 0.7 collective-permute-start.30
  94.6 1.0 collective-permute-start.31
  95.6 1.4 %shard_map.107 = (bf16[256,256]{1,0:T(8,128)(2,1)S(1)}, bf16[256,256]{1,0:T(8,128)(2,1)S(1)}, bf16[256,256]{1,0:T(8,128)(2,1)S(1)}, bf16[256,256]{1,0:T(8,128)(2,1)S(1)}) custom-call(f32[512,768]{1,0:T(8,128)S(1)} %get-tuple-element.63.total, bf16[512,1024]{1,0:T(8,128)(2,1)S(1)} %get-tuple-element.64.later, bf16[256,512]{1,0:T(8,128)(2,1)S(1)} %get-tuple-element.67.refs_0_, ...), custom_call_target="tpu_custom_call" | custom-call | flops 536870912 | bytes 4720640 | tf_op jit(solution)/shard_map/pallas_call | solution.py:39
  97.1 3.0 %collective-permute-done.28.refs_5_ = bf16[512,256]{1,0:T(8,128)(2,1)S(1)} collective-permute-done((bf16[512,256]{1,0:T(8,128)(2,1)S(1)}, bf16[512,256]{1,0:T(8,128)(2,1)S(1)}, u32[]{:S(2)}, u32[]{:S(2)}) %collective-permute-start.28) | collective-permute-done | bytes 262176 | tf_op jit(solution)/shard_map/ppermute | solution.py:314
  100.1 2.8 %collective-permute-done.30.refs_2_ = bf16[256,256]{1,0:T(8,128)(2,1)S(1)} collective-permute-done((bf16[256,256]{1,0:T(8,128)(2,1)S(1)}, bf16[256,256]{1,0:T(8,128)(2,1)S(1)}, u32[]{:S(2)}, u32[]{:S(2)}) %collective-permute-start.30) | collective-permute-done | bytes 131104 | tf_op jit(solution)/shard_map/ppermute | solution.py:314
  102.9 1.6 %collective-permute-done.31.refs_3_ = bf16[256,256]{1,0:T(8,128)(2,1)S(1)} collective-permute-done((bf16[256,256]{1,0:T(8,128)(2,1)S(1)}, bf16[256,256]{1,0:T(8,128)(2,1)S(1)}, u32[]{:S(2)}, u32[]{:S(2)}) %collective-permute-start.31) | collective-permute-done | bytes 131104 | tf_op jit(solution)/shard_map/ppermute | solution.py:314
  104.5 0.4 collective-permute-start.33
  105.0 0.4 collective-permute-start.25
  105.4 0.7 collective-permute-start.26
  106.1 0.8 collective-permute-start.27
  106.9 4.0 %shard_map.110 = (bf16[128,256]{1,0:T(8,128)(2,1)S(1)}, bf16[128,256]{1,0:T(8,128)(2,1)S(1)}, bf16[128,256]{1,0:T(8,128)(2,1)S(1)}, bf16[128,256]{1,0:T(8,128)(2,1)S(1)}) custom-call(s32[4]{0:T(128)S(1)} %iota_xor_fusion.far, s32[4,128]{1,0:T(4,128)S(1)} %get-tuple-element.56.columns, bf16[512,128]{1,0:T(8,128)(2,1)S(1)} %get-tuple-element.57.query_bar, ...), custom_call_target="tpu_custom_call" | custom-call | flops 2147483648 | bytes 2492432 | tf_op jit(solution)/shard_map/pallas_call | solution.py:39
  110.9 1.8 %collective-permute-start.37 = (bf16[128,256]{1,0:T(8,128)(2,1)S(1)}, bf16[128,256]{1,0:T(8,128)(2,1)S(1)}, u32[]{:S(2)}, u32[]{:S(2)}) collective-permute-start(bf16[128,256]{1,0:T(8,128)(2,1)S(1)} %get-tuple-element.88), channel_id=1, source_target_pairs={{0,8},{8,0},{16,24},{24,16},{1,9},{9,1},{17,25},{25,17},{2,10},{10... | collective-permute-start | bytes 196616 | tf_op jit(solution)/shard_map/ppermute | solution.py:314
  112.7 0.9 collective-permute-start.38
  113.7 1.7 %collective-permute-start.39 = (bf16[128,256]{1,0:T(8,128)(2,1)S(1)}, bf16[128,256]{1,0:T(8,128)(2,1)S(1)}, u32[]{:S(2)}, u32[]{:S(2)}) collective-permute-start(bf16[128,256]{1,0:T(8,128)(2,1)S(1)} %get-tuple-element.90), channel_id=1, source_target_pairs={{0,24},{8,16},{16,8},{24,0},{1,25},{9,17},{17,9},{25,1},{2,26},{10... | collective-permute-start | bytes 196616 | tf_op jit(solution)/shard_map/ppermute | solution.py:314
  115.4 3.8 %shard_map.109 = (bf16[128,256]{1,0:T(8,128)(2,1)S(1)}, bf16[128,256]{1,0:T(8,128)(2,1)S(1)}, bf16[128,256]{1,0:T(8,128)(2,1)S(1)}, bf16[128,256]{1,0:T(8,128)(2,1)S(1)}) custom-call(s32[4]{0:T(128)S(1)} %iota_xor_fusion.far, s32[4,128]{1,0:T(4,128)S(1)} %get-tuple-element.56.columns, bf16[512,128]{1,0:T(8,128)(2,1)S(1)} %get-tuple-element.57.query_bar, ...), custom_call_target="tpu_custom_call" | custom-call | flops 2147483648 | bytes 2492432 | tf_op jit(solution)/shard_map/pallas_call | solution.py:39
  119.1 0.9 collective-permute-start.34
  120.1 1.8 %collective-permute-start.35 = (bf16[128,256]{1,0:T(8,128)(2,1)S(1)}, bf16[128,256]{1,0:T(8,128)(2,1)S(1)}, u32[]{:S(2)}, u32[]{:S(2)}) collective-permute-start(bf16[128,256]{1,0:T(8,128)(2,1)S(1)} %get-tuple-element.85), channel_id=1, source_target_pairs={{0,16},{8,24},{16,0},{24,8},{1,17},{9,25},{17,1},{25,9},{2,18},{10... | collective-permute-start | bytes 196616 | tf_op jit(solution)/shard_map/ppermute | solution.py:314
  121.9 1.7 %collective-permute-start.36 = (bf16[128,256]{1,0:T(8,128)(2,1)S(1)}, bf16[128,256]{1,0:T(8,128)(2,1)S(1)}, u32[]{:S(2)}, u32[]{:S(2)}) collective-permute-start(bf16[128,256]{1,0:T(8,128)(2,1)S(1)} %get-tuple-element.86), channel_id=1, source_target_pairs={{0,24},{8,16},{16,8},{24,0},{1,25},{9,17},{17,9},{25,1},{2,26},{10... | collective-permute-start | bytes 196616 | tf_op jit(solution)/shard_map/ppermute | solution.py:314
  123.6 0.6 collective-permute-done.34.refs_1_
  124.2 4.1 %collective-permute-done.35.refs_2_ = bf16[128,256]{1,0:T(8,128)(2,1)S(1)} collective-permute-done((bf16[128,256]{1,0:T(8,128)(2,1)S(1)}, bf16[128,256]{1,0:T(8,128)(2,1)S(1)}, u32[]{:S(2)}, u32[]{:S(2)}) %collective-permute-start.35) | collective-permute-done | bytes 65568 | tf_op jit(solution)/shard_map/ppermute | solution.py:314
  128.2 1.4 %shard_map.111 = bf16[128,2048]{1,0:T(8,128)(2,1)} custom-call(s32[4]{0:T(128)S(1)} %iota_xor_fusion.far, bf16[128,256]{1,0:T(8,128)(2,1)S(1)} %get-tuple-element.83.refs_0_, bf16[128,256]{1,0:T(8,128)(2,1)S(1)} %collective-permute-done.34.refs_1_, bf16[128,256]{1,0:T(8,128)(2,1)S(1)} %collective-permute-done.35.refs_2_, ...), custom_call_target="tpu_custom_call" | custom-call | bytes 1048592 | tf_op jit(solution)/shard_map/pallas_call | solution.py:39
  (73 shorter events, 2.1 us)
Async XLA Ops:
  0.0 34.4 %copy-start.10 = (s32[4]{0:T(128)S(1)}, s32[4]{0:T(128)}, u32[]{:S(2)}) copy-start(s32[4]{0:T(128)} %constant.65) | copy-start | bytes 52
  0.0 35.0 %copy-start.4 = (s32[128]{0:T(128)S(1)}, s32[128]{0:T(128)}, u32[]{:S(2)}) copy-start(s32[128]{0:T(128)} %param.12) | copy-start | bytes 1540
  0.0 15.7 %collective-permute-start.4 = (bf16[128,2048]{1,0:T(8,128)(2,1)}, bf16[128,2048]{1,0:T(8,128)(2,1)S(1)}, u32[]{:S(2)}, u32[]{:S(2)}) collective-permute-start(bf16[128,2048]{1,0:T(8,128)(2,1)} %refs_0_.1), channel_id=1, source_target_pairs={{0,8},{8,0},{16,24},{24,16},{1,9},{9,1},{17,25},{25,17},{2,10},{10... | collective-permute-start | bytes 1572872 | tf_op jit(solution)/shard_map/ppermute | solution.py:314
  3.0 12.6 %collective-permute-start.3 = (bf16[128,2048]{1,0:T(8,128)(2,1)}, bf16[128,2048]{1,0:T(8,128)(2,1)}, u32[]{:S(2)}, u32[]{:S(2)}) collective-permute-start(bf16[128,2048]{1,0:T(8,128)(2,1)} %refs_0_.1), channel_id=1, source_target_pairs={{8,16},{16,8},{9,17},{17,9},{10,18},{18,10},{11,19},{19,11},{12,20... | collective-permute-start | bytes 1572872 | tf_op jit(solution)/shard_map/ppermute | solution.py:369
  4.5 13.6 %collective-permute-start.6 = (bf16[128,2048]{1,0:T(8,128)(2,1)}, bf16[128,2048]{1,0:T(8,128)(2,1)S(1)}, u32[]{:S(2)}, u32[]{:S(2)}) collective-permute-start(bf16[128,2048]{1,0:T(8,128)(2,1)} %refs_0_.1), channel_id=1, source_target_pairs={{0,1},{1,0},{2,3},{3,2},{4,5},{5,4},{6,7},{7,6},{8,9},{9,8},{10,11... | collective-permute-start | bytes 1572872 | tf_op jit(solution)/shard_map/ppermute | solution.py:344
  6.0 1.2 copy-start
  7.2 0.9 copy-start.1
  8.2 0.9 copy-start.2
  9.1 0.7 copy-start.3
  10.5 17.0 %collective-permute-start.1 = (bf16[272,768]{1,0:T(8,128)(2,1)S(1)}, bf16[272,768]{1,0:T(8,128)(2,1)S(1)}, u32[]{:S(2)}, u32[]{:S(2)}) collective-permute-start(bf16[272,768]{1,0:T(8,128)(2,1)S(1)} %get-tuple-element.50), channel_id=1, source_target_pairs={{0,24},{8,16},{16,8},{24,0},{1,25},{9,17},{17,9},{25,1},{2,26},{10... | collective-permute-start | bytes 1253384 | tf_op jit(solution)/shard_map/ppermute | solution.py:314
  13.1 20.0 %collective-permute-start = (bf16[272,768]{1,0:T(8,128)(2,1)S(1)}, bf16[272,768]{1,0:T(8,128)(2,1)S(1)}, u32[]{:S(2)}, u32[]{:S(2)}) collective-permute-start(bf16[272,768]{1,0:T(8,128)(2,1)S(1)} %get-tuple-element.49), channel_id=1, source_target_pairs={{0,8},{8,0},{16,24},{24,16},{1,9},{9,1},{17,25},{25,17},{2,10},{10... | collective-permute-start | bytes 1253384 | tf_op jit(solution)/shard_map/ppermute | solution.py:314
  18.1 29.6 %copy-start.8 = (bf16[128,2048]{1,0:T(8,128)(2,1)}, bf16[128,2048]{1,0:T(8,128)(2,1)S(1)}, u32[]{:S(2)}) copy-start(bf16[128,2048]{1,0:T(8,128)(2,1)S(1)} %collective-permute-done.6.refs_1_) | copy-start | bytes 1572868
  18.1 28.3 %collective-permute-start.15 = (bf16[128,2048]{1,0:T(8,128)(2,1)S(1)}, bf16[128,2048]{1,0:T(8,128)(2,1)}, u32[]{:S(2)}, u32[]{:S(2)}) collective-permute-start(bf16[128,2048]{1,0:T(8,128)(2,1)S(1)} %collective-permute-done.4.refs_2_), channel_id=1, source_target_pairs={{8,16},{16,8},{9,17},{17,9},{10,18},{18,10},{11,19},{19,11},{12,20... | collective-permute-start | bytes 1572872 | tf_op jit(solution)/shard_map/ppermute | solution.py:373
  27.5 18.9 %collective-permute-start.7 = (bf16[128,2048]{1,0:T(8,128)(2,1)S(1)}, bf16[128,2048]{1,0:T(8,128)(2,1)}, u32[]{:S(2)}, u32[]{:S(2)}) collective-permute-start(bf16[128,2048]{1,0:T(8,128)(2,1)S(1)} %collective-permute-done.4.refs_2_), channel_id=1, source_target_pairs={{0,1},{1,0},{2,3},{3,2},{4,5},{5,4},{6,7},{7,6},{8,9},{9,8},{10,11... | collective-permute-start | bytes 1572872 | tf_op jit(solution)/shard_map/ppermute | solution.py:344
  33.1 19.7 %collective-permute-start.5 = (bf16[128,2048]{1,0:T(8,128)(2,1)}, bf16[128,2048]{1,0:T(8,128)(2,1)}, u32[]{:S(2)}, u32[]{:S(2)}) collective-permute-start(bf16[128,2048]{1,0:T(8,128)(2,1)} %collective-permute-done.3), channel_id=1, source_target_pairs={{8,0},{16,24},{9,1},{17,25},{10,2},{18,26},{11,3},{19,27},{12,4},{... | collective-permute-start | bytes 1572872 | tf_op jit(solution)/shard_map/ppermute | solution.py:374
  35.0 19.0 %copy-start.11 = (s32[4]{0:T(128)S(1)}, s32[4]{0:T(128)}, u32[]{:S(2)}) copy-start(s32[4]{0:T(128)} %constant.56.clone) | copy-start | bytes 52
  35.0 18.9 %collective-permute-start.2 = (s32[128]{0:T(128)S(1)}, s32[128]{0:T(128)S(1)}, u32[]{:S(2)}, u32[]{:S(2)}) collective-permute-start(s32[128]{0:T(128)S(1)} %copy-done.4), channel_id=1, source_target_pairs={{0,16},{8,24},{16,0},{24,8},{1,17},{9,25},{17,1},{25,9},{2,18},{10... | collective-permute-start | bytes 1544 | tf_op jit(solution)/shard_map/ppermute | solution.py:314
  44.8 16.7 %collective-permute-start.9 = (bf16[528,768]{1,0:T(8,128)(2,1)S(1)}, bf16[528,768]{1,0:T(8,128)(2,1)S(1)}, u32[]{:S(2)}, u32[]{:S(2)}) collective-permute-start(bf16[528,768]{1,0:T(8,128)(2,1)S(1)} %shard_map.101.refs_0_.refs_8_), channel_id=1, source_target_pairs={{0,4},{2,6},{4,0},{6,2},{1,5},{3,7},{5,1},{7,3},{8,12},{10,14},{12... | collective-permute-start | bytes 2433032 | tf_op jit(solution)/shard_map/ppermute | solution.py:314
  46.4 18.8 %collective-permute-start.16 = (bf16[128,2048]{1,0:T(8,128)(2,1)}, bf16[128,2048]{1,0:T(8,128)(2,1)}, u32[]{:S(2)}, u32[]{:S(2)}) collective-permute-start(bf16[128,2048]{1,0:T(8,128)(2,1)} %collective-permute-done.15), channel_id=1, source_target_pairs={{8,0},{16,24},{9,1},{17,25},{10,2},{18,26},{11,3},{19,27},{12,4},{... | collective-permute-start | bytes 1572872 | tf_op jit(solution)/shard_map/ppermute | solution.py:381
  53.9 9.8 %collective-permute-start.8 = (bf16[128,2048]{1,0:T(8,128)(2,1)S(1)}, bf16[128,2048]{1,0:T(8,128)(2,1)}, u32[]{:S(2)}, u32[]{:S(2)}) collective-permute-start(bf16[128,2048]{1,0:T(8,128)(2,1)S(1)} %broadcast_select_fusion.1.refs_4_), channel_id=1, source_target_pairs={{0,1},{1,0},{2,3},{3,2},{4,5},{5,4},{6,7},{7,6},{8,9},{9,8},{10,11... | collective-permute-start | bytes 1572872 | tf_op jit(solution)/shard_map/ppermute | solution.py:344
  54.6 26.1 %copy-start.7 = (bf16[128,2048]{1,0:T(8,128)(2,1)S(1)}, bf16[128,2048]{1,0:T(8,128)(2,1)}, u32[]{:S(2)}) copy-start(bf16[128,2048]{1,0:T(8,128)(2,1)} %refs_0_.1) | copy-start | bytes 1572868
  54.6 26.1 %copy-start.9 = (bf16[128,2048]{1,0:T(8,128)(2,1)S(1)}, bf16[128,2048]{1,0:T(8,128)(2,1)}, u32[]{:S(2)}) copy-start(bf16[128,2048]{1,0:T(8,128)(2,1)} %copy-done.8) | copy-start | bytes 1572868
  54.6 24.5 %collective-permute-start.11 = (bf16[528,768]{1,0:T(8,128)(2,1)S(1)}, bf16[528,768]{1,0:T(8,128)(2,1)S(1)}, u32[]{:S(2)}, u32[]{:S(2)}) collective-permute-start(bf16[528,768]{1,0:T(8,128)(2,1)S(1)} %shard_map.101.refs_0_.refs_8_), channel_id=1, source_target_pairs={{0,2},{2,0},{4,6},{6,4},{1,3},{3,1},{5,7},{7,5},{8,10},{10,8},{12,... | collective-permute-start | bytes 2433032 | tf_op jit(solution)/shard_map/ppermute | solution.py:314
  61.5 15.8 %collective-permute-start.18 = (bf16[256,768]{1,0:T(8,128)(2,1)S(1)}, bf16[256,768]{1,0:T(8,128)(2,1)S(1)}, u32[]{:S(2)}, u32[]{:S(2)}) collective-permute-start(bf16[256,768]{1,0:T(8,128)(2,1)S(1)} %get-tuple-element.65), channel_id=1, source_target_pairs={{0,16},{8,24},{16,0},{24,8},{1,17},{9,25},{17,1},{25,9},{2,18},{10... | collective-permute-start | bytes 1179656 | tf_op jit(solution)/shard_map/ppermute | solution.py:314
  61.8 19.0 %collective-permute-start.13 = (bf16[528,768]{1,0:T(8,128)(2,1)S(1)}, bf16[528,768]{1,0:T(8,128)(2,1)S(1)}, u32[]{:S(2)}, u32[]{:S(2)}) collective-permute-start(bf16[528,768]{1,0:T(8,128)(2,1)S(1)} %collective-permute-done.9.refs_2_.refs_10_), channel_id=1, source_target_pairs={{0,2},{2,0},{4,6},{6,4},{1,3},{3,1},{5,7},{7,5},{8,10},{10,8},{12,... | collective-permute-start | bytes 2433032 | tf_op jit(solution)/shard_map/ppermute | solution.py:314
  63.7 10.1 %collective-permute-start.10 = (bf16[272,768]{1,0:T(8,128)(2,1)S(1)}, bf16[272,768]{1,0:T(8,128)(2,1)S(1)}, u32[]{:S(2)}, u32[]{:S(2)}) collective-permute-start(bf16[272,768]{1,0:T(8,128)(2,1)S(1)} %shard_map.102.refs_1_.refs_9_), channel_id=1, source_target_pairs={{0,4},{2,6},{4,0},{6,2},{1,5},{3,7},{5,1},{7,3},{8,12},{10,14},{12... | collective-permute-start | bytes 1253384 | tf_op jit(solution)/shard_map/ppermute | solution.py:314
  66.3 12.2 %collective-permute-start.17 = (bf16[128,2048]{1,0:T(8,128)(2,1)S(1)}, bf16[128,2048]{1,0:T(8,128)(2,1)S(1)}, u32[]{:S(2)}, u32[]{:S(2)}) collective-permute-start(bf16[128,2048]{1,0:T(8,128)(2,1)S(1)} %broadcast_select_fusion.refs_6_), channel_id=1, source_target_pairs={{0,1},{1,0},{2,3},{3,2},{4,5},{5,4},{6,7},{7,6},{8,9},{9,8},{10,11... | collective-permute-start | bytes 1572872 | tf_op jit(solution)/shard_map/ppermute | solution.py:344
  73.9 5.5 %collective-permute-start.12 = (bf16[272,768]{1,0:T(8,128)(2,1)S(1)}, bf16[272,768]{1,0:T(8,128)(2,1)S(1)}, u32[]{:S(2)}, u32[]{:S(2)}) collective-permute-start(bf16[272,768]{1,0:T(8,128)(2,1)S(1)} %shard_map.102.refs_1_.refs_9_), channel_id=1, source_target_pairs={{0,2},{2,0},{4,6},{6,4},{1,3},{3,1},{5,7},{7,5},{8,10},{10,8},{12,... | collective-permute-start | bytes 1253384 | tf_op jit(solution)/shard_map/ppermute | solution.py:314
  77.3 3.4 %collective-permute-start.14 = (bf16[272,768]{1,0:T(8,128)(2,1)S(1)}, bf16[272,768]{1,0:T(8,128)(2,1)S(1)}, u32[]{:S(2)}, u32[]{:S(2)}) collective-permute-start(bf16[272,768]{1,0:T(8,128)(2,1)S(1)} %collective-permute-done.10.refs_3_.refs_11_), channel_id=1, source_target_pairs={{0,2},{2,0},{4,6},{6,4},{1,3},{3,1},{5,7},{7,5},{8,10},{10,8},{12,... | collective-permute-start | bytes 1253384 | tf_op jit(solution)/shard_map/ppermute | solution.py:314
  78.6 10.2 %collective-permute-start.21 = (bf16[256,256]{1,0:T(8,128)(2,1)S(1)}, bf16[256,256]{1,0:T(8,128)(2,1)S(1)}, u32[]{:S(2)}, u32[]{:S(2)}) collective-permute-start(bf16[256,256]{1,0:T(8,128)(2,1)S(1)} %get-tuple-element.68.refs_0_), channel_id=1, source_target_pairs={{0,4},{2,6},{4,0},{6,2},{1,5},{3,7},{5,1},{7,3},{8,12},{10,14},{12... | collective-permute-start | bytes 393224 | tf_op jit(solution)/shard_map/ppermute | solution.py:314
  79.2 10.2 %collective-permute-start.22 = (bf16[256,256]{1,0:T(8,128)(2,1)S(1)}, bf16[256,256]{1,0:T(8,128)(2,1)S(1)}, u32[]{:S(2)}, u32[]{:S(2)}) collective-permute-start(bf16[256,256]{1,0:T(8,128)(2,1)S(1)} %get-tuple-element.68.refs_0_), channel_id=1, source_target_pairs={{0,2},{2,0},{4,6},{6,4},{1,3},{3,1},{5,7},{7,5},{8,10},{10,8},{12,... | collective-permute-start | bytes 393224 | tf_op jit(solution)/shard_map/ppermute | solution.py:314
  79.3 5.7 %copy-start.5 = (s32[13]{0:T(128)S(1)}, s32[13]{0:T(128)}, u32[]{:S(2)}) copy-start(s32[13]{0:T(128)} %doc_starts.1) | copy-start | bytes 160
  79.3 5.7 %copy-start.6 = (f32[1,128]{1,0:T(1,128)S(1)}, f32[1,128]{1,0:T(1,128)}, u32[]{:S(2)}) copy-start(f32[1,128]{1,0:T(1,128)} %constant.58.clone.freqs) | copy-start | bytes 1540
  79.3 11.4 %collective-permute-start.19 = (bf16[256,512]{1,0:T(8,128)(2,1)S(1)}, bf16[256,512]{1,0:T(8,128)(2,1)S(1)}, u32[]{:S(2)}, u32[]{:S(2)}) collective-permute-start(bf16[256,512]{1,0:T(8,128)(2,1)S(1)} %get-tuple-element.67.refs_0_), channel_id=1, source_target_pairs={{0,4},{2,6},{4,0},{6,2},{1,5},{3,7},{5,1},{7,3},{8,12},{10,14},{12... | collective-permute-start | bytes 786440 | tf_op jit(solution)/shard_map/ppermute | solution.py:314
  85.1 2.7 %copy-start.12 = (f32[128]{0:T(128)S(1)}, f32[128]{0:T(128)}, u32[]{:S(2)}) copy-start(f32[128]{0:T(128)} %constant.64) | copy-start | bytes 1540
  88.8 1.4 %collective-permute-start.23 = (bf16[256,256]{1,0:T(8,128)(2,1)S(1)}, bf16[256,256]{1,0:T(8,128)(2,1)S(1)}, u32[]{:S(2)}, u32[]{:S(2)}) collective-permute-start(bf16[256,256]{1,0:T(8,128)(2,1)S(1)} %collective-permute-done.21.refs_1_), channel_id=1, source_target_pairs={{0,2},{2,0},{4,6},{6,4},{1,3},{3,1},{5,7},{7,5},{8,10},{10,8},{12,... | collective-permute-start | bytes 393224 | tf_op jit(solution)/shard_map/ppermute | solution.py:314
  89.0 2.6 %collective-permute-start.20 = (bf16[256,512]{1,0:T(8,128)(2,1)S(1)}, bf16[256,512]{1,0:T(8,128)(2,1)S(1)}, u32[]{:S(2)}, u32[]{:S(2)}) collective-permute-start(bf16[256,512]{1,0:T(8,128)(2,1)S(1)} %get-tuple-element.67.refs_0_), channel_id=1, source_target_pairs={{0,2},{2,0},{4,6},{6,4},{1,3},{3,1},{5,7},{7,5},{8,10},{10,8},{12,... | collective-permute-start | bytes 786440 | tf_op jit(solution)/shard_map/ppermute | solution.py:314
  90.7 1.6 %collective-permute-start.24 = (bf16[256,512]{1,0:T(8,128)(2,1)S(1)}, bf16[256,512]{1,0:T(8,128)(2,1)S(1)}, u32[]{:S(2)}, u32[]{:S(2)}) collective-permute-start(bf16[256,512]{1,0:T(8,128)(2,1)S(1)} %collective-permute-done.19.refs_1_), channel_id=1, source_target_pairs={{0,2},{2,0},{4,6},{6,4},{1,3},{3,1},{5,7},{7,5},{8,10},{10,8},{12,... | collective-permute-start | bytes 786440 | tf_op jit(solution)/shard_map/ppermute | solution.py:314
  90.9 9.1 %collective-permute-start.28 = (bf16[512,256]{1,0:T(8,128)(2,1)S(1)}, bf16[512,256]{1,0:T(8,128)(2,1)S(1)}, u32[]{:S(2)}, u32[]{:S(2)}) collective-permute-start(bf16[512,256]{1,0:T(8,128)(2,1)S(1)} %shard_map.106.refs_4_), channel_id=1, source_target_pairs={{0,4},{2,6},{4,0},{6,2},{1,5},{3,7},{5,1},{7,3},{8,12},{10,14},{12... | collective-permute-start | bytes 786440 | tf_op jit(solution)/shard_map/ppermute | solution.py:314
  93.7 6.4 %collective-permute-start.29 = (bf16[256,256]{1,0:T(8,128)(2,1)S(1)}, bf16[256,256]{1,0:T(8,128)(2,1)S(1)}, u32[]{:S(2)}, u32[]{:S(2)}) collective-permute-start(bf16[256,256]{1,0:T(8,128)(2,1)S(1)} %get-tuple-element.78), channel_id=1, source_target_pairs={{0,2},{2,0},{4,6},{6,4},{1,3},{3,1},{5,7},{7,5},{8,10},{10,8},{12,... | collective-permute-start | bytes 393224 | tf_op jit(solution)/shard_map/ppermute | solution.py:314
  94.0 8.9 %collective-permute-start.30 = (bf16[256,256]{1,0:T(8,128)(2,1)S(1)}, bf16[256,256]{1,0:T(8,128)(2,1)S(1)}, u32[]{:S(2)}, u32[]{:S(2)}) collective-permute-start(bf16[256,256]{1,0:T(8,128)(2,1)S(1)} %get-tuple-element.79), channel_id=1, source_target_pairs={{0,4},{2,6},{4,0},{6,2},{1,5},{3,7},{5,1},{7,3},{8,12},{10,14},{12... | collective-permute-start | bytes 393224 | tf_op jit(solution)/shard_map/ppermute | solution.py:314
  94.6 9.9 %collective-permute-start.31 = (bf16[256,256]{1,0:T(8,128)(2,1)S(1)}, bf16[256,256]{1,0:T(8,128)(2,1)S(1)}, u32[]{:S(2)}, u32[]{:S(2)}) collective-permute-start(bf16[256,256]{1,0:T(8,128)(2,1)S(1)} %get-tuple-element.80), channel_id=1, source_target_pairs={{0,6},{2,4},{4,2},{6,0},{1,7},{3,5},{5,3},{7,1},{8,14},{10,12},{12... | collective-permute-start | bytes 393224 | tf_op jit(solution)/shard_map/ppermute | solution.py:314
  104.5 2.4 %collective-permute-start.33 = (bf16[512,256]{1,0:T(8,128)(2,1)S(1)}, bf16[512,256]{1,0:T(8,128)(2,1)S(1)}, u32[]{:S(2)}, u32[]{:S(2)}) collective-permute-start(bf16[512,256]{1,0:T(8,128)(2,1)S(1)} %collective-permute-done.28.refs_5_), channel_id=1, source_target_pairs={{0,2},{2,0},{4,6},{6,4},{1,3},{3,1},{5,7},{7,5},{8,10},{10,8},{12,... | collective-permute-start | bytes 786440 | tf_op jit(solution)/shard_map/ppermute | solution.py:314
  104.9 2.0 %collective-permute-start.32 = (bf16[512,256]{1,0:T(8,128)(2,1)S(1)}, bf16[512,256]{1,0:T(8,128)(2,1)S(1)}, u32[]{:S(2)}, u32[]{:S(2)}) collective-permute-start(bf16[512,256]{1,0:T(8,128)(2,1)S(1)} %shard_map.106.refs_4_), channel_id=1, source_target_pairs={{0,2},{2,0},{4,6},{6,4},{1,3},{3,1},{5,7},{7,5},{8,10},{10,8},{12,... | collective-permute-start | bytes 786440 | tf_op jit(solution)/shard_map/ppermute | solution.py:314
  105.0 8.6 %collective-permute-start.25 = (bf16[256,256]{1,0:T(8,128)(2,1)S(1)}, bf16[256,256]{1,0:T(8,128)(2,1)S(1)}, u32[]{:S(2)}, u32[]{:S(2)}) collective-permute-start(bf16[256,256]{1,0:T(8,128)(2,1)S(1)} %get-tuple-element.74), channel_id=1, source_target_pairs={{0,2},{2,0},{4,6},{6,4},{1,3},{3,1},{5,7},{7,5},{8,10},{10,8},{12,... | collective-permute-start | bytes 393224 | tf_op jit(solution)/shard_map/ppermute | solution.py:314
  105.4 9.9 %collective-permute-start.26 = (bf16[256,256]{1,0:T(8,128)(2,1)S(1)}, bf16[256,256]{1,0:T(8,128)(2,1)S(1)}, u32[]{:S(2)}, u32[]{:S(2)}) collective-permute-start(bf16[256,256]{1,0:T(8,128)(2,1)S(1)} %get-tuple-element.75), channel_id=1, source_target_pairs={{0,4},{2,6},{4,0},{6,2},{1,5},{3,7},{5,1},{7,3},{8,12},{10,14},{12... | collective-permute-start | bytes 393224 | tf_op jit(solution)/shard_map/ppermute | solution.py:314
  106.1 9.2 %collective-permute-start.27 = (bf16[256,256]{1,0:T(8,128)(2,1)S(1)}, bf16[256,256]{1,0:T(8,128)(2,1)S(1)}, u32[]{:S(2)}, u32[]{:S(2)}) collective-permute-start(bf16[256,256]{1,0:T(8,128)(2,1)S(1)} %get-tuple-element.76), channel_id=1, source_target_pairs={{0,6},{2,4},{4,2},{6,0},{1,7},{3,5},{5,3},{7,1},{8,14},{10,12},{12... | collective-permute-start | bytes 393224 | tf_op jit(solution)/shard_map/ppermute | solution.py:314
  110.9 11.0 %collective-permute-start.37 = (bf16[128,256]{1,0:T(8,128)(2,1)S(1)}, bf16[128,256]{1,0:T(8,128)(2,1)S(1)}, u32[]{:S(2)}, u32[]{:S(2)}) collective-permute-start(bf16[128,256]{1,0:T(8,128)(2,1)S(1)} %get-tuple-element.88), channel_id=1, source_target_pairs={{0,8},{8,0},{16,24},{24,16},{1,9},{9,1},{17,25},{25,17},{2,10},{10... | collective-permute-start | bytes 196616 | tf_op jit(solution)/shard_map/ppermute | solution.py:314
  112.7 10.9 %collective-permute-start.38 = (bf16[128,256]{1,0:T(8,128)(2,1)S(1)}, bf16[128,256]{1,0:T(8,128)(2,1)S(1)}, u32[]{:S(2)}, u32[]{:S(2)}) collective-permute-start(bf16[128,256]{1,0:T(8,128)(2,1)S(1)} %get-tuple-element.89), channel_id=1, source_target_pairs={{0,16},{8,24},{16,0},{24,8},{1,17},{9,25},{17,1},{25,9},{2,18},{10... | collective-permute-start | bytes 196616 | tf_op jit(solution)/shard_map/ppermute | solution.py:314
  113.7 9.9 %collective-permute-start.39 = (bf16[128,256]{1,0:T(8,128)(2,1)S(1)}, bf16[128,256]{1,0:T(8,128)(2,1)S(1)}, u32[]{:S(2)}, u32[]{:S(2)}) collective-permute-start(bf16[128,256]{1,0:T(8,128)(2,1)S(1)} %get-tuple-element.90), channel_id=1, source_target_pairs={{0,24},{8,16},{16,8},{24,0},{1,25},{9,17},{17,9},{25,1},{2,26},{10... | collective-permute-start | bytes 196616 | tf_op jit(solution)/shard_map/ppermute | solution.py:314
  119.1 5.0 %collective-permute-start.34 = (bf16[128,256]{1,0:T(8,128)(2,1)S(1)}, bf16[128,256]{1,0:T(8,128)(2,1)S(1)}, u32[]{:S(2)}, u32[]{:S(2)}) collective-permute-start(bf16[128,256]{1,0:T(8,128)(2,1)S(1)} %get-tuple-element.84), channel_id=1, source_target_pairs={{0,8},{8,0},{16,24},{24,16},{1,9},{9,1},{17,25},{25,17},{2,10},{10... | collective-permute-start | bytes 196616 | tf_op jit(solution)/shard_map/ppermute | solution.py:314
  120.1 8.2 %collective-permute-start.35 = (bf16[128,256]{1,0:T(8,128)(2,1)S(1)}, bf16[128,256]{1,0:T(8,128)(2,1)S(1)}, u32[]{:S(2)}, u32[]{:S(2)}) collective-permute-start(bf16[128,256]{1,0:T(8,128)(2,1)S(1)} %get-tuple-element.85), channel_id=1, source_target_pairs={{0,16},{8,24},{16,0},{24,8},{1,17},{9,25},{17,1},{25,9},{2,18},{10... | collective-permute-start | bytes 196616 | tf_op jit(solution)/shard_map/ppermute | solution.py:314
  121.9 6.3 %collective-permute-start.36 = (bf16[128,256]{1,0:T(8,128)(2,1)S(1)}, bf16[128,256]{1,0:T(8,128)(2,1)S(1)}, u32[]{:S(2)}, u32[]{:S(2)}) collective-permute-start(bf16[128,256]{1,0:T(8,128)(2,1)S(1)} %get-tuple-element.86), channel_id=1, source_target_pairs={{0,24},{8,16},{16,8},{24,0},{1,25},{9,17},{17,9},{25,1},{2,26},{10... | collective-permute-start | bytes 196616 | tf_op jit(solution)/shard_map/ppermute | solution.py:314
